TPU v7x, 32 devices: a whole 2x2x4 slice. The times are simulated.
32 devices in a mesh: fsdp: 2 (over x), ctx: 4 (over y, core), tp: 4 (over z).
Axes of the slice: x: 2, y: 2, z: 4, core: 2. Of those that a mesh axis runs over, the one named last changes fastest.
Arguments:
- layer_input: bfloat16 [8, 1024, 768], P('fsdp', 'ctx'), may hold values from -6 to 6
- gain_attn: bfloat16 [768], P('fsdp'), may hold values from 0.5 to 1.5
- query_weight: bfloat16 [768, 768], P('fsdp', 'tp'), may hold values from -0.21875 to 0.21875
- key_weight: bfloat16 [768, 768], P('fsdp', 'tp'), may hold values from -0.21875 to 0.21875
- value_weight: bfloat16 [768, 768], P('fsdp', 'tp'), may hold values from -0.21875 to 0.21875
- output_weight: bfloat16 [768, 768], P('tp', 'fsdp'), may hold values from -1.75 to 1.75
- gain_ffn: bfloat16 [768], P('fsdp'), may hold values from 0.5 to 1.5
- router: bfloat16 [768, 8], P('fsdp'), may hold values from -0.15625 to 0.15625
- exp_gate: bfloat16 [8, 768, 2048], P(None, 'fsdp', 'tp'), may hold values from -0.21875 to 0.21875
- exp_up: bfloat16 [8, 768, 2048], P(None, 'fsdp', 'tp'), may hold values from -0.21875 to 0.21875
- exp_down: bfloat16 [8, 2048, 768], P(None, 'tp', 'fsdp'), may hold values from -0.5 to 0.5
- shared_gate_weight: bfloat16 [768, 2048], P('fsdp', 'tp'), may hold values from -0.21875 to 0.21875
- shared_up_weight: bfloat16 [768, 2048], P('fsdp', 'tp'), may hold values from -0.21875 to 0.21875
- shared_down_weight: bfloat16 [2048, 768], P('tp', 'fsdp'), may hold values from -0.125 to 0.125
- routes: int32 [8, 1024, 2], P('fsdp', 'ctx'), may hold values from 0 to 7, all different within a row; in each aligned block of 256 rows (0 to 255, 256 to 511, ..., all dimensions but the last counted through in order) at most 80 rows name the same one
- prefix: int32 [8], P('fsdp'), may hold values from 102 to 512
- cotangent: bfloat16 [8, 1024, 768], P('fsdp', 'ctx'), may hold values from -6 to 6
Outputs:
- activations: bfloat16 [8, 1024, 768], P('fsdp', 'ctx')
- grad_input: float32 [8, 1024, 768], P('fsdp', 'ctx')
- grad_gain_attn: float32 [768], P(('fsdp', 'ctx'))
- grad_w_query: float32 [768, 768], P(('fsdp', 'ctx'), 'tp')
- grad_w_key: float32 [768, 768], P(('fsdp', 'ctx'), 'tp')
- grad_w_value: float32 [768, 768], P(('fsdp', 'ctx'), 'tp')
- grad_w_out: float32 [768, 768], P('tp', ('fsdp', 'ctx'))
- grad_gain_ffn: float32 [768], P(('fsdp', 'ctx'))
- grad_router: float32 [768, 8], P(('fsdp', 'ctx'))
- grad_exp_gate: float32 [8, 768, 2048], P(None, ('fsdp', 'ctx'), 'tp')
- grad_exp_up: float32 [8, 768, 2048], P(None, ('fsdp', 'ctx'), 'tp')
- grad_exp_down: float32 [8, 2048, 768], P(None, 'tp', ('fsdp', 'ctx'))
- grad_shared_gate: float32 [768, 2048], P(('fsdp', 'ctx'), 'tp')
- grad_shared_up: float32 [768, 2048], P(('fsdp', 'ctx'), 'tp')
- grad_shared_down: float32 [2048, 768], P('tp', ('fsdp', 'ctx'))
Inputs may be any that keep to these rules, and one draw needn't show every extreme that they name: `routes`: A token's two experts differ. In each aligned block of 256 rows (the tokens of one sequence on one index of ctx) no expert is named by more than 80 rows, a bound that some block reaches.
All inputs are finite; a program needn't handle non-finite values.
Results may differ from a plain program's by a relative error of at most 0.02.
Values may be sent and summed in bfloat16 or wider, within the bound.
No kernel may reach another device: no remote copies, remote signals or barrier semaphores. Data moves between devices by JAX's collectives and lax.ppermute only.
A program may use at most 320 MiB of HBM per device.

v0:
```python
import math

import jax
import jax.numpy as jnp
from jax import lax
from jax.sharding import PartitionSpec as P

HD = 64
EXPERT_SLOTS = 80


EPS = 1e-06


def rope_tables(positions, half):
    inverse = jnp.exp(jnp.arange(half, dtype=jnp.float32) * (-math.log(10000.0) / half))
    angles = positions.astype(jnp.float32)[:, None] * inverse[None, :]
    return (jnp.cos(angles), jnp.sin(angles))


def rotate(value_rows, cosine, sine):
    half = value_rows.shape[-1] // 2
    first = value_rows[..., :half]
    second = value_rows[..., half:]
    cosine = cosine[:, None, :]
    sine = sine[:, None, :]
    return jnp.concatenate(
        [first * cosine - second * sine, second * cosine + first * sine], axis=-1
    )


def unrotate(value_rows, cosine, sine):
    half = value_rows.shape[-1] // 2
    first = value_rows[..., :half]
    second = value_rows[..., half:]
    cosine = cosine[:, None, :]
    sine = sine[:, None, :]
    return jnp.concatenate(
        [first * cosine + second * sine, second * cosine - first * sine], axis=-1
    )


def silu_slope(value_rows):
    sigma = jax.nn.sigmoid(value_rows)
    return sigma * (1.0 + value_rows * (1.0 - sigma))


def norm_back(grad_out, value_rows, scale, gain):
    weighted = grad_out * gain
    return scale * weighted - value_rows * scale * scale * scale * jnp.mean(
        weighted * value_rows, -1, keepdims=True
    )


def body(
    layer_input,
    gain_attn,
    query_weight,
    key_weight,
    value_weight,
    output_weight,
    gain_ffn,
    router,
    exp_gate,
    exp_up,
    exp_down,
    shared_gate_weight,
    shared_up_weight,
    shared_down_weight,
    routes,
    prefix,
    cotangent,
):
    sequences, local_len, model_width = layer_input.shape
    tokens = sequences * local_len
    experts = exp_gate.shape[0]
    capacity = EXPERT_SLOTS
    heads_here = query_weight.shape[1] // HD
    head_cols = heads_here * HD
    total_len = local_len * lax.axis_size("ctx")
    scaling = HD ** (-0.5)
    (
        query_whole,
        key_whole,
        value_whole,
        out_whole,
        gain_one,
        gain_two,
        router_whole,
        gate_whole,
        up_whole,
        down_whole,
        shgate_whole,
        shup_whole,
        shdown_whole,
    ) = (
        lax.all_gather(query_weight, "fsdp", axis=0, tiled=True),
        lax.all_gather(key_weight, "fsdp", axis=0, tiled=True),
        lax.all_gather(value_weight, "fsdp", axis=0, tiled=True),
        lax.all_gather(output_weight, "fsdp", axis=1, tiled=True),
        lax.all_gather(gain_attn, "fsdp", axis=0, tiled=True),
        lax.all_gather(gain_ffn, "fsdp", axis=0, tiled=True),
        lax.all_gather(router, "fsdp", axis=0, tiled=True),
        lax.all_gather(exp_gate, "fsdp", axis=1, tiled=True),
        lax.all_gather(exp_up, "fsdp", axis=1, tiled=True),
        lax.all_gather(exp_down, "fsdp", axis=2, tiled=True),
        lax.all_gather(shared_gate_weight, "fsdp", axis=0, tiled=True),
        lax.all_gather(shared_up_weight, "fsdp", axis=0, tiled=True),
        lax.all_gather(shared_down_weight, "fsdp", axis=1, tiled=True),
    )
    gain_one_f = gain_one.astype(jnp.float32)
    gain_two_f = gain_two.astype(jnp.float32)
    layer_inputs = layer_input.astype(jnp.float32).reshape(tokens, model_width)
    scale_one = lax.rsqrt(jnp.mean(layer_inputs * layer_inputs, -1, keepdims=True) + EPS)
    first_normed = (layer_inputs * scale_one * gain_one_f).astype(jnp.bfloat16)
    query_lin = jnp.dot(first_normed, query_whole, preferred_element_type=jnp.float32)
    key_lin = jnp.dot(first_normed, key_whole, preferred_element_type=jnp.float32)
    value_lin = jnp.dot(first_normed, value_whole, preferred_element_type=jnp.float32)
    positions = lax.axis_index("ctx") * local_len + jnp.arange(local_len, dtype=jnp.int32)
    cosine, sine = rope_tables(positions, HD // 2)
    split_into_heads = (sequences, local_len, heads_here, HD)
    query_rot = rotate(query_lin.reshape(split_into_heads), cosine, sine).astype(jnp.bfloat16)
    key_rot = rotate(key_lin.reshape(split_into_heads), cosine, sine).astype(jnp.bfloat16)
    value_low = value_lin.astype(jnp.bfloat16).reshape(sequences, local_len, head_cols)
    key_all, value_all = (
        lax.all_gather(key_rot.reshape(sequences, local_len, head_cols), "ctx", axis=1, tiled=True),
        lax.all_gather(value_low, "ctx", axis=1, tiled=True),
    )
    key_all = key_all.reshape(sequences, total_len, heads_here, HD)
    value_all = value_all.reshape(sequences, total_len, heads_here, HD)
    key_pos = jnp.arange(total_len, dtype=jnp.int32)
    seen = (key_pos[None, None, :] <= positions[None, :, None]) | (
        key_pos[None, None, :] < prefix[:, None, None]
    )

    def masked_scores():
        raw = (
            jnp.einsum("sqhd,skhd->shqk", query_rot, key_all, preferred_element_type=jnp.float32)
            * scaling
        )
        return jnp.where(seen[:, None], raw, -1e30)

    scores = masked_scores()
    peak = jnp.max(scores, -1, keepdims=True)
    expo = jnp.exp(scores - peak)
    row_total = jnp.sum(expo, -1, keepdims=True)
    log_total = peak + jnp.log(row_total)
    probs_low = (expo / row_total).astype(jnp.bfloat16)
    attention_result = jnp.einsum(
        "shqk,skhd->sqhd", probs_low, value_all, preferred_element_type=jnp.float32
    )
    attended_low = attention_result.astype(jnp.bfloat16).reshape(tokens, head_cols)
    attn_part = jnp.dot(attended_low, out_whole, preferred_element_type=jnp.float32)
    middle_state = layer_inputs + lax.psum(attn_part.astype(jnp.bfloat16), "tp").astype(jnp.float32)
    scale_two = lax.rsqrt(jnp.mean(middle_state * middle_state, -1, keepdims=True) + EPS)
    second_normed = (middle_state * scale_two * gain_two_f).astype(jnp.bfloat16)
    router_logits = jnp.dot(second_normed, router_whole, preferred_element_type=jnp.float32)
    expo_router = jnp.exp(router_logits)
    gates = expo_router / jnp.sum(expo_router, -1, keepdims=True)
    route_pair = routes.reshape(tokens, 2)
    choose = route_pair[:, :, None] == jnp.arange(experts, dtype=jnp.int32)[None, None, :]
    chosen = jnp.sum(jnp.where(choose, gates[:, None, :], 0.0), -1)
    flat_routes = routes.reshape(sequences, local_len * 2)
    hot = (flat_routes[:, :, None] == jnp.arange(experts, dtype=jnp.int32)[None, None, :]).astype(
        jnp.int32
    )
    place = jnp.sum((jnp.cumsum(hot, axis=1) - hot) * hot, -1).reshape(sequences, local_len, 2)
    slot_order = jnp.transpose(routes * capacity + place, (0, 2, 1))
    picker = (
        jnp.arange(experts * capacity, dtype=jnp.int32)[None, None, :, None]
        == slot_order[:, :, None, :]
    ).astype(jnp.bfloat16)
    picker = picker.reshape(sequences, 2, experts, capacity, local_len)
    dispatch_matrix = picker[:, 0] + picker[:, 1]
    expert_input = (
        jnp.einsum(
            "secq,sqd->escd",
            dispatch_matrix,
            second_normed.reshape(sequences, local_len, model_width),
            preferred_element_type=jnp.float32,
        )
        .astype(jnp.bfloat16)
        .reshape(experts, sequences * capacity, model_width)
    )
    gate_act = jnp.einsum(
        "end,edf->enf", expert_input, gate_whole, preferred_element_type=jnp.float32
    )
    up_act = jnp.einsum("end,edf->enf", expert_input, up_whole, preferred_element_type=jnp.float32)
    expert_hid = (jax.nn.silu(gate_act) * up_act).astype(jnp.bfloat16)
    expert_output = jnp.einsum(
        "enf,efd->end", expert_hid, down_whole, preferred_element_type=jnp.float32
    )
    seq_index = jnp.arange(sequences, dtype=jnp.int32)[:, None, None]
    picked = expert_output.reshape(experts, sequences, capacity, model_width)[
        routes, seq_index, place
    ]
    chosen_rows = chosen.reshape(sequences, local_len, 2)
    expert_mixture = jnp.sum(picked * chosen_rows[..., None], 2).reshape(tokens, model_width)
    shared_gate_act = jnp.dot(second_normed, shgate_whole, preferred_element_type=jnp.float32)
    shared_up_act = jnp.dot(second_normed, shup_whole, preferred_element_type=jnp.float32)
    shared_hidden = (jax.nn.silu(shared_gate_act) * shared_up_act).astype(jnp.bfloat16)
    shared_output = jnp.dot(shared_hidden, shdown_whole, preferred_element_type=jnp.float32)
    result = middle_state + lax.psum(
        (expert_mixture + shared_output).astype(jnp.bfloat16), "tp"
    ).astype(jnp.float32)
    activations = result.astype(jnp.bfloat16).reshape(layer_input.shape)
    upstream = cotangent.astype(jnp.float32).reshape(tokens, model_width)
    upstream_low = upstream.astype(jnp.bfloat16)
    grad_shdown = jnp.einsum(
        "tf,td->fd", shared_hidden, upstream_low, preferred_element_type=jnp.float32
    )
    shared_back = jnp.einsum(
        "td,fd->tf", upstream_low, shdown_whole, preferred_element_type=jnp.float32
    )
    shared_a_back = (shared_back * shared_up_act * silu_slope(shared_gate_act)).astype(jnp.bfloat16)
    shared_b_back = (shared_back * jax.nn.silu(shared_gate_act)).astype(jnp.bfloat16)
    grad_shgate = jnp.einsum(
        "td,tf->df", second_normed, shared_a_back, preferred_element_type=jnp.float32
    )
    grad_shup = jnp.einsum(
        "td,tf->df", second_normed, shared_b_back, preferred_element_type=jnp.float32
    )
    shared_norm_back = jnp.einsum(
        "tf,df->td", shared_a_back, shgate_whole, preferred_element_type=jnp.float32
    ) + jnp.einsum("tf,df->td", shared_b_back, shup_whole, preferred_element_type=jnp.float32)
    gated_up = (
        (chosen[:, :, None] * upstream[:, None, :])
        .astype(jnp.bfloat16)
        .reshape(sequences, local_len, 2, model_width)
    )
    expert_out_back = (
        jnp.einsum("sceaq,sqcd->esad", picker, gated_up, preferred_element_type=jnp.float32)
        .astype(jnp.bfloat16)
        .reshape(experts, sequences * capacity, model_width)
    )
    grad_down = jnp.einsum(
        "enf,end->efd", expert_hid, expert_out_back, preferred_element_type=jnp.float32
    )
    hid_back = jnp.einsum(
        "end,efd->enf", expert_out_back, down_whole, preferred_element_type=jnp.float32
    )
    gate_back = (hid_back * up_act * silu_slope(gate_act)).astype(jnp.bfloat16)
    up_back = (hid_back * jax.nn.silu(gate_act)).astype(jnp.bfloat16)
    grad_gate = jnp.einsum(
        "end,enf->edf", expert_input, gate_back, preferred_element_type=jnp.float32
    )
    grad_up = jnp.einsum("end,enf->edf", expert_input, up_back, preferred_element_type=jnp.float32)
    expert_in_back = jnp.einsum(
        "enf,edf->end", gate_back, gate_whole, preferred_element_type=jnp.float32
    ) + jnp.einsum("enf,edf->end", up_back, up_whole, preferred_element_type=jnp.float32)
    back_rows = expert_in_back.reshape(experts, sequences, capacity, model_width)[
        routes, seq_index, place
    ]
    moe_norm_back = jnp.sum(back_rows, 2).reshape(tokens, model_width)
    gate_dots = jnp.sum(
        picked * upstream.reshape(sequences, local_len, 1, model_width), -1
    ).reshape(tokens, 2)
    norm_part, gate_grad = (
        lax.psum((moe_norm_back + shared_norm_back).astype(jnp.bfloat16), "tp").astype(jnp.float32),
        lax.psum(gate_dots.astype(jnp.bfloat16), "tp").astype(jnp.float32),
    )
    prob_back = jnp.sum(jnp.where(choose, gate_grad[:, :, None], 0.0), 1)
    logit_back = (gates * (prob_back - jnp.sum(prob_back * gates, -1, keepdims=True))).astype(
        jnp.bfloat16
    )
    grad_router_here = jnp.einsum(
        "td,te->de", second_normed, logit_back, preferred_element_type=jnp.float32
    )
    norm_two_back = norm_part + jnp.einsum(
        "te,de->td", logit_back, router_whole, preferred_element_type=jnp.float32
    )
    grad_gain_two = jnp.sum(norm_two_back * middle_state * scale_two, 0)
    middle_back = upstream + norm_back(norm_two_back, middle_state, scale_two, gain_two_f)
    middle_low = middle_back.astype(jnp.bfloat16)
    grad_out_here = jnp.einsum(
        "th,td->hd", attended_low, middle_low, preferred_element_type=jnp.float32
    )
    attended_back = (
        jnp.einsum("td,hd->th", middle_low, out_whole, preferred_element_type=jnp.float32)
        .astype(jnp.bfloat16)
        .reshape(split_into_heads)
    )
    probs = jnp.exp(masked_scores() - log_total)
    probs_back = jnp.einsum(
        "sqhd,skhd->shqk", attended_back, value_all, preferred_element_type=jnp.float32
    )
    score_back = (probs * (probs_back - jnp.sum(probs_back * probs, -1, keepdims=True))).astype(
        jnp.bfloat16
    )
    query_back = (
        jnp.einsum("shqk,skhd->sqhd", score_back, key_all, preferred_element_type=jnp.float32)
        * scaling
    )
    key_all_back = (
        jnp.einsum("shqk,sqhd->skhd", score_back, query_rot, preferred_element_type=jnp.float32)
        * scaling
    )
    value_all_back = jnp.einsum(
        "shqk,sqhd->skhd",
        probs.astype(jnp.bfloat16),
        attended_back,
        preferred_element_type=jnp.float32,
    )
    key_back, value_back = (
        lax.psum_scatter(
            key_all_back.reshape(sequences, total_len, head_cols).astype(jnp.bfloat16),
            "ctx",
            scatter_dimension=1,
            tiled=True,
        ).astype(jnp.float32),
        lax.psum_scatter(
            value_all_back.reshape(sequences, total_len, head_cols).astype(jnp.bfloat16),
            "ctx",
            scatter_dimension=1,
            tiled=True,
        ).astype(jnp.float32),
    )
    query_pre = unrotate(query_back, cosine, sine).astype(jnp.bfloat16).reshape(tokens, head_cols)
    key_pre = (
        unrotate(key_back.reshape(split_into_heads), cosine, sine)
        .astype(jnp.bfloat16)
        .reshape(tokens, head_cols)
    )
    value_pre = value_back.astype(jnp.bfloat16).reshape(tokens, head_cols)
    grad_query_here = jnp.einsum(
        "td,th->dh", first_normed, query_pre, preferred_element_type=jnp.float32
    )
    grad_key_here = jnp.einsum(
        "td,th->dh", first_normed, key_pre, preferred_element_type=jnp.float32
    )
    grad_value_here = jnp.einsum(
        "td,th->dh", first_normed, value_pre, preferred_element_type=jnp.float32
    )
    norm_one_part = (
        jnp.einsum("th,dh->td", query_pre, query_whole, preferred_element_type=jnp.float32)
        + jnp.einsum("th,dh->td", key_pre, key_whole, preferred_element_type=jnp.float32)
        + jnp.einsum("th,dh->td", value_pre, value_whole, preferred_element_type=jnp.float32)
    )
    norm_one_back = lax.psum(norm_one_part.astype(jnp.bfloat16), "tp").astype(jnp.float32)
    grad_gain_one = jnp.sum(norm_one_back * layer_inputs * scale_one, 0)
    input_back = middle_back + norm_back(norm_one_back, layer_inputs, scale_one, gain_one_f)
    sent_all = (
        lax.psum_scatter(grad_gain_one, ("fsdp", "ctx"), scatter_dimension=0, tiled=True),
        lax.psum_scatter(grad_query_here, ("fsdp", "ctx"), scatter_dimension=0, tiled=True),
        lax.psum_scatter(grad_key_here, ("fsdp", "ctx"), scatter_dimension=0, tiled=True),
        lax.psum_scatter(grad_value_here, ("fsdp", "ctx"), scatter_dimension=0, tiled=True),
        lax.psum_scatter(grad_out_here, ("fsdp", "ctx"), scatter_dimension=1, tiled=True),
        lax.psum_scatter(grad_gain_two, ("fsdp", "ctx"), scatter_dimension=0, tiled=True),
        lax.psum_scatter(grad_router_here, ("fsdp", "ctx"), scatter_dimension=0, tiled=True),
        lax.psum_scatter(grad_gate, ("fsdp", "ctx"), scatter_dimension=1, tiled=True),
        lax.psum_scatter(grad_up, ("fsdp", "ctx"), scatter_dimension=1, tiled=True),
        lax.psum_scatter(grad_down, ("fsdp", "ctx"), scatter_dimension=2, tiled=True),
        lax.psum_scatter(grad_shgate, ("fsdp", "ctx"), scatter_dimension=0, tiled=True),
        lax.psum_scatter(grad_shup, ("fsdp", "ctx"), scatter_dimension=0, tiled=True),
        lax.psum_scatter(grad_shdown, ("fsdp", "ctx"), scatter_dimension=1, tiled=True),
    )
    return (
        activations,
        input_back.reshape(layer_input.shape),
        sent_all[0],
        sent_all[1],
        sent_all[2],
        sent_all[3],
        sent_all[4],
        sent_all[5],
        sent_all[6],
        sent_all[7],
        sent_all[8],
        sent_all[9],
        sent_all[10],
        sent_all[11],
        sent_all[12],
    )


def solution(mesh):
    placed = (
        P("fsdp", "ctx", None),
        P("fsdp"),
        P("fsdp", "tp"),
        P("fsdp", "tp"),
        P("fsdp", "tp"),
        P("tp", "fsdp"),
        P("fsdp"),
        P("fsdp", None),
        P(None, "fsdp", "tp"),
        P(None, "fsdp", "tp"),
        P(None, "tp", "fsdp"),
        P("fsdp", "tp"),
        P("fsdp", "tp"),
        P("tp", "fsdp"),
        P("fsdp", "ctx", None),
        P("fsdp"),
        P("fsdp", "ctx", None),
    )
    return jax.shard_map(
        body,
        mesh=mesh,
        in_specs=placed,
        out_specs=(
            P("fsdp", "ctx", None),
            P("fsdp", "ctx", None),
            P(("fsdp", "ctx")),
            P(("fsdp", "ctx"), "tp"),
            P(("fsdp", "ctx"), "tp"),
            P(("fsdp", "ctx"), "tp"),
            P("tp", ("fsdp", "ctx")),
            P(("fsdp", "ctx")),
            P(("fsdp", "ctx"), None),
            P(None, ("fsdp", "ctx"), "tp"),
            P(None, ("fsdp", "ctx"), "tp"),
            P(None, "tp", ("fsdp", "ctx")),
            P(("fsdp", "ctx"), "tp"),
            P(("fsdp", "ctx"), "tp"),
            P("tp", ("fsdp", "ctx")),
        ),
        check_vma=False,
    )
```

profile of v0, /device:TPU:0, one launch (start us, length us, event | category | flops | bytes accessed | tf_op | source)
XLA Modules:
  0.0 1452.6 jit_solution(10331659133252985261)
XLA Ops:
  98.7 20.4 %all_gather.57 = bf16[768,512]{1,0:T(8,128)(2,1)} all-gather(bf16[384,512]{1,0:T(8,128)(2,1)S(1)} %copy-done.35), channel_id=1, replica_groups=mesh['fsdp'=2,'ctx'=4,'tp'=4] {'fsdp'}, dimensions={0}, use_global_device_ids=true | all-gather | bytes 1179648 | tf_op jit(solution)/shard_map/all_gather | solution.py:107
  119.0 21.8 %all_gather.58 = bf16[768,512]{1,0:T(8,128)(2,1)} all-gather(bf16[384,512]{1,0:T(8,128)(2,1)} %param.29), channel_id=1, replica_groups=mesh['fsdp'=2,'ctx'=4,'tp'=4] {'fsdp'}, dimensions={0}, use_global_device_ids=true | all-gather | bytes 1179648 | tf_op jit(solution)/shard_map/all_gather | solution.py:108
  149.7 20.7 %all_gather.59 = bf16[512,768]{1,0:T(8,128)(2,1)} all-gather(bf16[512,384]{1,0:T(8,128)(2,1)} %param.30), channel_id=1, replica_groups=mesh['fsdp'=2,'ctx'=4,'tp'=4] {'fsdp'}, dimensions={1}, use_global_device_ids=true | all-gather | bytes 1179648 | tf_op jit(solution)/shard_map/all_gather | solution.py:109
  205.8 69.9 %all-gather.12.cloned.1.call-done = bf16[8,768,512]{2,1,0:T(8,128)(2,1)} async-done(((bf16[8,384,512]{2,1,0:T(8,128)(2,1)}), bf16[8,768,512]{2,1,0:T(8,128)(2,1)}) %all-gather.12.cloned.1.call-update) | async-done | bytes 6291472 | tf_op jit(solution)/shard_map/all_gather | solution.py:104
  284.5 72.9 %all-gather.16.cloned.1.call-done = bf16[8,512,768]{2,1,0:T(8,128)(2,1)} async-done(((bf16[8,512,384]{2,1,0:T(8,128)(2,1)}), bf16[8,512,768]{2,1,0:T(8,128)(2,1)}) %all-gather.16.cloned.1.call-update) | async-done | bytes 6291472 | tf_op jit(solution)/shard_map/all_gather | solution.py:106
  386.5 39.7 %gather_fusion.1 = f32[2048,768]{1,0:T(8,128)} fusion(f32[8,4,80,768]{3,2,1,0:T(8,128)} %bitcast.236, s32[2048]{0:T(1024)S(1)} %reshape.419), kind=kCustom, calls=%fused_computation.1 | custom fusion | bytes 12607488 | tf_op jit(solution)/shard_map/gather | solution.py:251
  434.6 11.9 reduce_sum.151
  460.9 40.1 %gather_fusion = f32[2048,768]{1,0:T(8,128)} fusion(f32[8,4,80,768]{3,2,1,0:T(8,128)} %bitcast.235, s32[2048]{0:T(1024)S(1)} %reshape.419), kind=kCustom, calls=%fused_computation | custom fusion | bytes 12607488 | tf_op jit(solution)/shard_map/gather | solution.py:194
  561.5 36.0 %copy.200 = bf16[4,1024,192]{0,2,1:T(8,128)(2,1)} copy(bf16[4,1024,192]{1,2,0:T(8,128)(2,1)S(1)} %bitcast.251) | data formatting | bytes 3145728
  597.5 91.1 %reshape.449 = bf16[1024,768]{1,0:T(8,128)(2,1)} reshape(bf16[1024,192,4]{2,1,0:T(8,128)(2,1)} %bitcast.237) | data formatting | bytes 3145728
  714.2 29.3 %reshape.450 = bf16[256,192,4]{2,1,0:T(8,128)(2,1)} reshape(bf16[256,768]{1,0:T(8,128)(2,1)} %reduce-scatter.40.cloned.1.call-done) | data formatting | bytes 786432
  743.4 12.5 copy.201
  776.6 12.0 copy.194
  828.7 85.1 %all-reduce.12.cloned.1.call-done = (bf16[1024,768]{1,0:T(8,128)(2,1)}, bf16[1024,768]{1,0:T(8,128)(2,1)}) async-done(((bf16[1024,768]{1,0:T(8,128)(2,1)}, bf16[1024,768]{1,0:T(8,128)(2,1)}), (bf16[1024,768]{1,0:T(8,128)(2,1)}, bf16[1024,768]{1,0:T(8,128)(2,1)})) %all-reduce.12.cloned.1.call-update) | async-done | bytes 3145744 | tf_op jit(solution)/shard_map/psum | solution.py:203
  916.6 13.8 all-reduce.2
  936.7 18.4 %reduce-scatter.38.cloned.1.call-done = f32[512,96]{0,1:T(8,128)} async-done(((f32[512,768]{0,1:T(8,128)}), f32[512,96]{0,1:T(8,128)}) %reduce-scatter.38.cloned.1.call-update) | async-done | bytes 196624 | tf_op jit(solution)/shard_map/reduce_scatter | solution.py:355
  955.0 42.3 %reduce-scatter.36.cloned.1.call-done = f32[96,512]{1,0:T(8,128)} async-done(((f32[768,512]{1,0:T(8,128)}), f32[96,512]{1,0:T(8,128)}) %reduce-scatter.36.cloned.1.call-update) | async-done | bytes 196624 | tf_op jit(solution)/shard_map/reduce_scatter | solution.py:354
  997.4 42.2 %reduce-scatter.34.cloned.1.call-done = f32[96,512]{1,0:T(8,128)} async-done(((f32[768,512]{1,0:T(8,128)}), f32[96,512]{1,0:T(8,128)}) %reduce-scatter.34.cloned.1.call-update) | async-done | bytes 196624 | tf_op jit(solution)/shard_map/reduce_scatter | solution.py:353
  1039.5 38.7 %reduce-scatter.22.cloned.1.call-done = f32[96,192]{1,0:T(8,128)} async-done(((f32[768,192]{1,0:T(8,128)}), f32[96,192]{1,0:T(8,128)}) %reduce-scatter.22.cloned.1.call-update) | async-done | bytes 73744 | tf_op jit(solution)/shard_map/reduce_scatter | solution.py:344
  1078.3 38.6 %reduce-scatter.24.cloned.1.call-done = f32[96,192]{1,0:T(8,128)} async-done(((f32[768,192]{1,0:T(8,128)}), f32[96,192]{1,0:T(8,128)}) %reduce-scatter.24.cloned.1.call-update) | async-done | bytes 73744 | tf_op jit(solution)/shard_map/reduce_scatter | solution.py:345
  1116.9 38.6 %reduce-scatter.26.cloned.1.call-done = f32[96,192]{1,0:T(8,128)} async-done(((f32[768,192]{1,0:T(8,128)}), f32[96,192]{1,0:T(8,128)}) %reduce-scatter.26.cloned.1.call-update) | async-done | bytes 73744 | tf_op jit(solution)/shard_map/reduce_scatter | solution.py:346
  1155.5 96.4 %reduce-scatter.32.cloned.1.call-done = f32[8,512,96]{1,2,0:T(8,128)} async-done(((f32[8,512,768]{1,2,0:T(8,128)}), f32[8,512,96]{1,2,0:T(8,128)}) %reduce-scatter.32.cloned.1.call-update) | async-done | bytes 1572880 | tf_op jit(solution)/shard_map/reduce_scatter | solution.py:352
  1251.8 96.4 %reduce-scatter.30.cloned.1.call-done = f32[8,96,512]{2,1,0:T(8,128)} async-done(((f32[8,768,512]{2,1,0:T(8,128)}), f32[8,96,512]{2,1,0:T(8,128)}) %reduce-scatter.30.cloned.1.call-update) | async-done | bytes 1572880 | tf_op jit(solution)/shard_map/reduce_scatter | solution.py:351
  1348.2 96.4 %reduce-scatter.28.cloned.1.call-done = f32[8,96,512]{2,1,0:T(8,128)} async-done(((f32[8,768,512]{2,1,0:T(8,128)}), f32[8,96,512]{2,1,0:T(8,128)}) %reduce-scatter.28.cloned.1.call-update) | async-done | bytes 1572880 | tf_op jit(solution)/shard_map/reduce_scatter | solution.py:350
  (284 shorter events, 349.5 us)
Async XLA Ops:
  8.0 45.0 %all-gather.10.cloned.1.call-start = ((), (), s32[]{:S(2)}) async-start(), calls=%async_computation.14 | async-start | bytes 1966080 | tf_op jit(solution)/shard_map/all_gather | solution.py:126
  31.3 43.7 %all-gather.8.cloned.1.call-start = ((), (), s32[]{:S(2)}) async-start(), calls=%async_computation.13 | async-start | bytes 1966080 | tf_op jit(solution)/shard_map/all_gather | solution.py:127
  39.4 134.1 %all-reduce.8.cloned.1.call-start = ((), (), s32[]{:S(2)}) async-start(), calls=%async_computation.15 | async-start | bytes 3145728 | tf_op jit(solution)/shard_map/psum | solution.py:154
  86.4 110.5 %all-gather.14.cloned.1.call-start = ((), (), s32[]{:S(2)}) async-start(), calls=%async_computation.17 | async-start | bytes 9437184 | tf_op jit(solution)/shard_map/all_gather | solution.py:105
  87.0 188.7 %all-gather.12.cloned.1.call-start = ((), (), s32[]{:S(2)}) async-start(), calls=%async_computation.16 | async-start | bytes 9437184 | tf_op jit(solution)/shard_map/all_gather | solution.py:104
  87.6 269.8 %all-gather.16.cloned.1.call-start = ((), (), s32[]{:S(2)}) async-start(), calls=%async_computation.18 | async-start | bytes 9437184 | tf_op jit(solution)/shard_map/all_gather | solution.py:106
  88.2 439.6 %all-reduce.10.cloned.1.call-start = ((), (), s32[]{:S(2)}) async-start(), calls=%async_computation.19 | async-start | bytes 3145728 | tf_op jit(solution)/shard_map/psum | solution.py:259
  452.0 251.2 %reduce-scatter.20.cloned.1.call-start = ((), (), s32[]{:S(2)}) async-start(), calls=%async_computation.20 | async-start | bytes 1966080 | tf_op jit(solution)/shard_map/reduce_scatter | solution.py:305
  554.2 160.0 %reduce-scatter.40.cloned.1.call-start = ((), (), s32[]{:S(2)}) async-start(), calls=%async_computation.30 | async-start | bytes 1966080
  597.5 91.1 %copy-start.11 = (bf16[1024,768]{1,0:T(8,128)(2,1)S(1)}, bf16[1024,768]{1,0:T(8,128)(2,1)}, u32[]{:S(2)}) copy-start(bf16[1024,768]{1,0:T(8,128)(2,1)} %copy-done.10) | copy-start | bytes 4718596
  597.5 91.1 %copy-start.47 = (bf16[1024,8]{0,1:T(8,128)(2,1)S(1)}, bf16[1024,8]{0,1:T(8,128)(2,1)}, u32[]{:S(2)}) copy-start(bf16[1024,8]{0,1:T(8,128)(2,1)} %copy-done.46) | copy-start | bytes 49156
  688.6 136.9 %reduce-scatter.44.cloned.1.call-start = ((), (), s32[]{:S(2)}) async-start(), calls=%async_computation.32 | async-start | bytes 442368
  694.9 132.1 %reduce-scatter.42.cloned.1.call-start = ((), (), s32[]{:S(2)}) async-start(), calls=%async_computation.31 | async-start | bytes 884736
  703.0 210.8 %all-reduce.12.cloned.1.call-start = ((), (), s32[]{:S(2)}) async-start(), calls=%async_computation.33 | async-start | bytes 6291456 | tf_op jit(solution)/shard_map/psum | solution.py:203
  760.8 194.2 %reduce-scatter.38.cloned.1.call-start = ((), (), s32[]{:S(2)}) async-start(), calls=%async_computation.29 | async-start | bytes 1769472 | tf_op jit(solution)/shard_map/reduce_scatter | solution.py:355
  764.8 232.5 %reduce-scatter.36.cloned.1.call-start = ((), (), s32[]{:S(2)}) async-start(), calls=%async_computation.28 | async-start | bytes 1769472 | tf_op jit(solution)/shard_map/reduce_scatter | solution.py:354
  768.3 271.2 %reduce-scatter.34.cloned.1.call-start = ((), (), s32[]{:S(2)}) async-start(), calls=%async_computation.27 | async-start | bytes 1769472 | tf_op jit(solution)/shard_map/reduce_scatter | solution.py:353
  772.4 305.9 %reduce-scatter.22.cloned.1.call-start = ((), (), s32[]{:S(2)}) async-start(), calls=%async_computation.21 | async-start | bytes 884736 | tf_op jit(solution)/shard_map/reduce_scatter | solution.py:344
  775.0 341.9 %reduce-scatter.24.cloned.1.call-start = ((), (), s32[]{:S(2)}) async-start(), calls=%async_computation.22 | async-start | bytes 884736 | tf_op jit(solution)/shard_map/reduce_scatter | solution.py:345
  776.6 378.9 %reduce-scatter.26.cloned.1.call-start = ((), (), s32[]{:S(2)}) async-start(), calls=%async_computation.23 | async-start | bytes 884736 | tf_op jit(solution)/shard_map/reduce_scatter | solution.py:346
  790.2 461.6 %reduce-scatter.32.cloned.1.call-start = ((), (), s32[]{:S(2)}) async-start(), calls=%async_computation.26 | async-start | bytes 14155776 | tf_op jit(solution)/shard_map/reduce_scatter | solution.py:352
  801.6 546.6 %reduce-scatter.30.cloned.1.call-start = ((), (), s32[]{:S(2)}) async-start(), calls=%async_computation.25 | async-start | bytes 14155776 | tf_op jit(solution)/shard_map/reduce_scatter | solution.py:351
  812.6 632.0 %reduce-scatter.28.cloned.1.call-start = ((), (), s32[]{:S(2)}) async-start(), calls=%async_computation.24 | async-start | bytes 14155776 | tf_op jit(solution)/shard_map/reduce_scatter | solution.py:350
  823.7 107.9 %copy-start.9 = (bf16[1024,768]{1,0:T(8,128)(2,1)S(1)}, bf16[1024,768]{1,0:T(8,128)(2,1)}, u32[]{:S(2)}) copy-start(bf16[1024,768]{1,0:T(8,128)(2,1)} %all-reduce.8.cloned.1.call-done) | copy-start | bytes 4718596
  (49 other events, 548.2 us)
Sparse Core Ops, SparseCore 0:
  31.4 21.5 all-gather.9
  55.1 19.8 all-gather.7
  86.5 69.1 all-reduce.7
  452.2 69.1 all-reduce.9
  554.4 25.5 reduce-scatter.19
  688.7 25.4 reduce-scatter.39
  717.2 33.8 reduce-scatter.43
  754.3 34.9 reduce-scatter.41
  792.3 121.4 all-reduce.11
  917.5 37.4 reduce-scatter.37
  958.9 38.4 reduce-scatter.35
  1001.1 38.4 reduce-scatter.33
  1043.3 34.9 reduce-scatter.21
  1081.9 34.9 reduce-scatter.23
  1120.4 34.9 reduce-scatter.25
  1159.4 92.3 reduce-scatter.31
  1255.7 92.3 reduce-scatter.29
  1352.1 92.3 reduce-scatter.27
Sparse Core Ops, SparseCore 1:
  88.4 105.6 all-gather.13
  195.5 80.2 all-gather.11
  277.2 80.2 all-gather.15
where the time goes:
time: 1460 us; the launch traced here: 1450 us
  waiting for transfers between devices  759 us (52%)
  local copies, waits for them, and re-layouts  310 us (21%)
  matrix products  181 us (12%)
  blocking collectives  126 us (9%)
  other arithmetic  56.9 us (4%)
  between operations  18 us (1%)
    unnamed x121, local copies, waits for them, and re-layouts  188 us
    reduce_scatter x1, waiting for transfers between devices, body(): lax.psum_scatter(grad_gate, ('fsdp', 'ctx'), scatter_dimension=1, tiled=T...  96.4 us
    reduce_scatter x1, waiting for transfers between devices, body(): lax.psum_scatter(grad_down, ('fsdp', 'ctx'), scatter_dimension=2, tiled=T...  96.4 us
    reduce_scatter x1, waiting for transfers between devices, body(): lax.psum_scatter(grad_up, ('fsdp', 'ctx'), scatter_dimension=1, tiled=True)  96.4 us
    psum x1, waiting for transfers between devices, body(): lax.psum((expert_mixture + shared_output).astype(jnp.bfloat16), 'tp')  85.1 us
    all_gather x1, waiting for transfers between devices, body(): lax.all_gather(exp_down, 'fsdp', axis=2, tiled=True)  72.9 us
    all_gather x1, waiting for transfers between devices, body(): lax.all_gather(exp_gate, 'fsdp', axis=1, tiled=True)  69.9 us
    gather x2, local copies, waits for them, and re-layouts, body(): expert_output.reshape(experts, sequences, capacity, model_width)  48.3 us
  transfers between devices with their start and end apart: 21, of which 15 were waited for; matrix products, arithmetic and copies ran while one was open for 28% of the time, Pallas kernels for 0%

commit v1 on v0

v1 whole, which is shorter than its diff:
```python
import functools
import math

import jax
import jax.numpy as jnp
from jax import lax
from jax.experimental import pallas as pl
from jax.experimental.pallas import tpu as pltpu
from jax.sharding import PartitionSpec as P

HD = 64
SLOTS = 80
EPS = 1e-06
F32 = jnp.float32
BF16 = jnp.bfloat16
VMEM_BYTES = 56 * 1024 * 1024


def mm(a, b):
    return lax.dot_general(a, b, (((1,), (0,)), ((), ())), preferred_element_type=F32)


def mm_nt(a, b):
    return lax.dot_general(a, b, (((1,), (1,)), ((), ())), preferred_element_type=F32)


def mm_tn(a, b):
    return lax.dot_general(a, b, (((0,), (0,)), ((), ())), preferred_element_type=F32)


def params(steps=1):
    return pltpu.CompilerParams(
        dimension_semantics=("arbitrary",) * steps, vmem_limit_bytes=VMEM_BYTES
    )


def rotation(width):
    row = lax.broadcasted_iota(jnp.int32, (width, width), 0)
    col = lax.broadcasted_iota(jnp.int32, (width, width), 1)
    first = (col % HD) < HD // 2
    minus = first & (row == col + HD // 2)
    plus = jnp.logical_not(first) & (row == col - HD // 2)
    return jnp.where(minus, -1.0, jnp.where(plus, 1.0, 0.0)).astype(BF16)


def row_scale(value):
    return lax.rsqrt(jnp.mean(value * value, -1, keepdims=True) + EPS)


def qkv_kernel(scal, x_ref, own_ref, oth_ref, cos_ref, sin_ref, n1_ref, q_ref, kv_ref, w_ref, small_ref, swap):
    half = own_ref.shape[0]

    @pl.when(pl.program_id(0) == 0)
    def _():
        mine = pl.multiple_of(scal[0] * half, half)
        other = pl.multiple_of((1 - scal[0]) * half, half)
        w_ref[pl.ds(mine, half), :] = own_ref[...]
        w_ref[pl.ds(other, half), :] = oth_ref[...]
        swap[...] = mm(w_ref[...], rotation(w_ref.shape[1])).astype(BF16)
        turned = jnp.transpose(w_ref[:, 128:256].astype(F32))
        small_ref[...] = turned[64:80, :]

    x = x_ref[0].astype(F32)
    n1 = (x * row_scale(x) * small_ref[8:9, :]).astype(BF16)
    n1_ref[0] = n1
    turned = mm(n1, w_ref[...]) * cos_ref[...] + mm(n1, swap[...]) * sin_ref[...]
    q_ref[0] = turned[:, :192].astype(BF16)
    kv_ref[0] = turned[:, 256:640].astype(BF16)


def visible(scal, prefix, keys, rows):
    key_pos = lax.broadcasted_iota(jnp.int32, (keys, rows), 0) ^ (scal[1] * rows)
    row_pos = lax.broadcasted_iota(jnp.int32, (keys, rows), 1) + scal[1] * rows
    return (key_pos <= row_pos) | (key_pos < prefix[pl.program_id(0)])


def only_head(rows, head):
    lane = lax.broadcasted_iota(jnp.int32, rows.shape, 1)
    return jnp.where((lane >= head * HD) & (lane < (head + 1) * HD), rows, jnp.zeros_like(rows))


def attn_fwd_kernel(scal, prefix, q_ref, kv0, kv1, kv2, kv3, o_ref, lse_ref):
    q = q_ref[0]
    rows, width = q.shape
    heads = width // HD
    kv = jnp.concatenate([kv0[0], kv1[0], kv2[0], kv3[0]], axis=0)
    k = kv[:, :width]
    value_t = jnp.transpose(kv[:, width:].astype(F32)).astype(BF16)
    seen = visible(scal, prefix, kv.shape[0], rows)
    outs = []
    for head in range(heads):
        scores = mm_nt(k, only_head(q, head) * (HD ** -0.5))
        scores = jnp.where(seen, scores, -1e30)
        peak = jnp.max(scores, 0, keepdims=True)
        expo = jnp.exp(scores - peak)
        total = jnp.sum(expo, 0, keepdims=True)
        probs = (expo * (1.0 / total)).astype(BF16)
        outs.append(mm(value_t[head * HD:(head + 1) * HD], probs))
        lse_ref[0, head:head + 1, :] = peak + jnp.log(total)
    o = jnp.transpose(jnp.concatenate(outs, axis=0))
    o_ref[0] = jnp.concatenate([o[: rows // 2], o[rows // 2:]], axis=1).astype(BF16)


def post_kernel(scal, o_ref, wo_ref, x_ref, small_ref, routes_ref, n2_ref, h2_ref, gates_ref, slots_ref, wo):
    step = pl.program_id(0)
    zs, width = wo_ref.shape[1], wo_ref.shape[2]
    half = wo_ref.shape[3]

    @pl.when(step == 0)
    def _():
        for z in range(zs):
            for side in range(2):
                wo[z * width:(z + 1) * width, side * half:(side + 1) * half] = wo_ref[side, z]

    low = jnp.zeros((o_ref.shape[2], 2 * half), F32)
    high = low
    for z in range(zs):
        block = o_ref[z, 0]
        weights = wo[z * width:(z + 1) * width, :]
        low += mm(block[:, :width], weights)
        high += mm(block[:, width:], weights)
    h2 = x_ref[0].astype(F32) + jnp.concatenate([low, high], axis=0)
    n2 = (h2 * row_scale(h2) * small_ref[9:10, :]).astype(BF16)
    n2_ref[0] = n2

    @pl.when(step == scal[2])
    def _():
        h2_ref[...] = h2

    expo = jnp.exp(mm_nt(small_ref[0:8, :].astype(BF16), n2))
    gates_ref[0] = expo / jnp.sum(expo, 0, keepdims=True)
    rows = n2.shape[0]
    expert = lax.broadcasted_iota(jnp.int32, (8, rows), 0)
    named = (routes_ref[0, 0:1, :] == expert) | (routes_ref[0, 1:2, :] == expert)
    before = lax.broadcasted_iota(jnp.int32, (rows, rows), 0) < lax.broadcasted_iota(jnp.int32, (rows, rows), 1)
    place = mm(named.astype(BF16), before.astype(BF16))
    slots_ref[0] = jnp.where(named, place.astype(jnp.int32), -1)


def silu_parts(value):
    sigma = 1.0 / (1.0 + jnp.exp(-value))
    return sigma, value * sigma


def split_blocks(core, value, blocks):
    rows = value.shape[0] // (2 * blocks)
    value = value.astype(BF16).reshape(blocks, 2, rows, value.shape[1])
    first = core == 0
    return jnp.where(first, value[:, 0], value[:, 1]), jnp.where(first, value[:, 1], value[:, 0])


def put_grads(core, keep_ref, send_ref, index, value):
    keep, send = split_blocks(core, value, keep_ref.shape[0])
    at = slice(index * keep.shape[1], (index + 1) * keep.shape[1])
    keep_ref[:, 0, at, :] = keep
    send_ref[:, 0, at, :] = send


def shared_kernel(
    scal, n2_ref, dy_ref, go_ref, uo_ref, do_ref, g0, g1, g2, g3, u0, u1, u2, u3, d0, d1, d2, d3,
    ys_ref, dn_ref, keep_ref, send_ref, wg, wu, wd, hs_s, da_s, db_s,
):
    step = pl.program_id(0)
    seqs, rows, width = n2_ref.shape
    half = go_ref.shape[0]
    hidden = go_ref.shape[1]

    @pl.when(step == 0)
    def _():
        mine = pl.multiple_of(scal[0] * half, half)
        other = (1 - scal[0]) * half
        wg[pl.ds(mine, half), :] = go_ref[...]
        wu[pl.ds(mine, half), :] = uo_ref[...]
        wd[:, pl.ds(mine, half)] = do_ref[...]
        for piece, (g, u, d) in enumerate(((g0, u0, d0), (g1, u1, d1), (g2, u2, d2), (g3, u3, d3))):
            quarter = scal[3] ^ piece
            at = pl.multiple_of(other + quarter * (half // 4), half // 4)
            wg[pl.ds(at, half // 4), :] = g[...]
            wu[pl.ds(at, half // 4), :] = u[...]
            at = pl.multiple_of(quarter * (hidden // 4), hidden // 4)
            wd[pl.ds(at, hidden // 4), pl.ds(pl.multiple_of(other, half), half)] = d[...]

    @pl.when(step < seqs)
    def _():
        n2 = n2_ref[step]
        dy = dy_ref[step]
        gate = mm(n2, wg[...])
        up = mm(n2, wu[...])
        sigma, silu = silu_parts(gate)
        hid = (silu * up).astype(BF16)
        ys_ref[0] = mm(hid, wd[...]).astype(BF16)
        back = mm_nt(dy, wd[...])
        da = (back * up * (sigma * (1.0 + gate * (1.0 - sigma)))).astype(BF16)
        db = (back * silu).astype(BF16)
        dn_ref[0] = (mm_nt(da, wg[...]) + mm_nt(db, wu[...])).astype(BF16)
        at = pl.ds(pl.multiple_of(step * rows, rows), rows)
        hs_s[at, :] = hid
        da_s[at, :] = da
        db_s[at, :] = db

    @pl.when(step == seqs)
    def _():
        n2 = n2_ref[...].reshape(seqs * rows, width)
        put_grads(scal[4], keep_ref, send_ref, 0, mm_tn(n2, da_s[...]))
        put_grads(scal[4], keep_ref, send_ref, 1, mm_tn(n2, db_s[...]))
        put_grads(scal[4], keep_ref, send_ref, 2, mm_tn(dy_ref[...].reshape(seqs * rows, width), hs_s[...]))


def moe_kernel(
    scal, n2_ref, dy_ref, slots_ref, gates_ref, ys_ref, dn_in_ref, go_ref, uo_ref, do_ref,
    g0, g1, g2, g3, u0, u1, u2, u3, d0, d1, d2, d3, keep_in, send_in,
    y_ref, dn_ref, keep_ref, send_ref, wg, wu, wd, pick_s, ye_s, dx_s, xe_s, dy_s, de_s, gs_s, dprob_s,
):
    step = pl.program_id(0)
    seqs, rows, width = n2_ref.shape
    half = go_ref.shape[1]
    experts = slots_ref.shape[1]

    @pl.when(step < experts)
    def _():
        piece = step // 2
        expert = 2 * (piece ^ scal[3]) + step % 2
        mine = pl.multiple_of(scal[0] * half, half)
        other = pl.multiple_of((1 - scal[0]) * half, half)
        wg[pl.ds(mine, half), :] = go_ref[0]
        wu[pl.ds(mine, half), :] = uo_ref[0]
        wd[:, pl.ds(mine, half)] = do_ref[0]
        for index, (g, u, d) in enumerate(((g0, u0, d0), (g1, u1, d1), (g2, u2, d2), (g3, u3, d3))):
            @pl.when(piece == index)
            def _(g=g, u=u, d=d):
                wg[pl.ds(other, half), :] = g[...]
                wu[pl.ds(other, half), :] = u[...]
                wd[:, pl.ds(other, half)] = d[...]

        slot_at = pl.ds(pl.multiple_of(step * SLOTS, 16), SLOTS)
        slot = lax.broadcasted_iota(jnp.int32, (SLOTS, rows), 0)
        for s in range(seqs):
            at = slice(s * SLOTS, (s + 1) * SLOTS)
            hit = slots_ref[s, pl.ds(expert, 1), :] == slot
            gate_slot = jnp.sum(jnp.where(hit, gates_ref[s, pl.ds(expert, 1), :], 0.0), 1, keepdims=True)
            pick = hit.astype(BF16)
            pick_s[s, slot_at, :] = pick
            xe_s[at, :] = mm(pick, n2_ref[s]).astype(BF16)
            upstream = mm(pick, dy_ref[s])
            dy_s[at, :] = upstream.astype(BF16)
            de_s[at, :] = (gate_slot * upstream).astype(BF16)
            gs_s[at, :] = jnp.broadcast_to(gate_slot, (SLOTS, 128))

        xe = xe_s[...]
        gate = mm(xe, wg[...])
        up = mm(xe, wu[...])
        sigma, silu = silu_parts(gate)
        hid = (silu * up).astype(BF16)
        ye = mm(hid, wd[...])
        dots = jnp.sum(ye * dy_s[...].astype(F32), 1, keepdims=True)
        ye = (ye * gs_s[:, 0:1]).astype(BF16)
        for s in range(seqs):
            at = slice(s * SLOTS, (s + 1) * SLOTS)
            ye_s[s, slot_at, :] = ye[at]
            hit = slots_ref[s, pl.ds(expert, 1), :] == slot
            dprob_s[s, pl.ds(expert, 1), :] = jnp.sum(jnp.where(hit, dots[at], 0.0), 0, keepdims=True)
        back = mm_nt(de_s[...], wd[...])
        da = (back * up * (sigma * (1.0 + gate * (1.0 - sigma)))).astype(BF16)
        db = (back * silu).astype(BF16)
        dx = (mm_nt(da, wg[...]) + mm_nt(db, wu[...])).astype(BF16)
        for s in range(seqs):
            dx_s[s, slot_at, :] = dx[s * SLOTS:(s + 1) * SLOTS]
        put_grads(scal[4], keep_ref, send_ref, 0, mm_tn(xe_s[...], da))
        put_grads(scal[4], keep_ref, send_ref, 1, mm_tn(xe_s[...], db))
        put_grads(scal[4], keep_ref, send_ref, 2, mm_tn(de_s[...], hid))

    @pl.when(step >= experts)
    def _():
        s = step - experts
        pick = pick_s[s]
        y_ref[0] = (ys_ref[0].astype(F32) + mm_tn(pick, ye_s[s])).astype(BF16)
        dn_ref[0, 0:rows, :] = (dn_in_ref[0].astype(F32) + mm_tn(pick, dx_s[s])).astype(BF16)
        tail = jnp.concatenate([dprob_s[s], jnp.zeros((dn_ref.shape[1] - rows - experts, rows), F32)], axis=0)
        tail = jnp.concatenate([tail, jnp.zeros((tail.shape[0], width - rows), F32)], axis=1)
        dn_ref[0, rows:, :] = tail.astype(BF16)


def norm_back(grad_out, value, scale, gain):
    weighted = grad_out * gain
    return scale * weighted - value * (scale * scale * scale) * jnp.mean(weighted * value, -1, keepdims=True)


def mid_kernel(scal, dn_ref, gates_ref, h2_ref, n2_ref, dy_ref, small_ref, wo_ref, dh2_ref, do_ref, low_ref, sums_ref, wo):
    rows = h2_ref.shape[0]
    zs, width, half = wo_ref.shape[1:]
    for z in range(zs):
        for side in range(2):
            wo[z * width:(z + 1) * width, side * half:(side + 1) * half] = wo_ref[side, z]
    gates = gates_ref[0]
    dprob = dn_ref[0, rows:rows + 8, 0:rows].astype(F32)
    dlogits = (gates * (dprob - jnp.sum(dprob * gates, 0, keepdims=True))).astype(BF16)
    dn2 = dn_ref[0, 0:rows, :].astype(F32) + mm_tn(dlogits, small_ref[0:8, :].astype(BF16))
    h2 = h2_ref[...]
    scale = row_scale(h2)
    sums_ref[0:8, :] = mm(dlogits, n2_ref[0])
    sums_ref[8:16, :] = jnp.zeros((8, h2.shape[1]), F32)
    sums_ref[9:10, :] = jnp.sum(dn2 * h2 * scale, 0, keepdims=True)
    dh2 = dy_ref[0].astype(F32) + norm_back(dn2, h2, scale, small_ref[9:10, :])
    dh2_ref[...] = dh2
    low = dh2.astype(BF16)
    low_ref[...] = low
    for z in range(zs):
        do = mm_nt(low, wo[z * width:(z + 1) * width, :])
        do_ref[z] = jnp.concatenate([do[: rows // 2], do[rows // 2:]], axis=1).astype(BF16)


def attn_bwd_kernel(
    scal, prefix, q_ref, kv0, kv1, kv2, kv3, lse_ref, do_ref, cos_ref, sin_ref, dq_ref, e0, e1, e2, e3
):
    q = q_ref[0]
    rows, width = q.shape
    heads = width // HD
    kv = jnp.concatenate([kv0[0], kv1[0], kv2[0], kv3[0]], axis=0)
    k = kv[:, :width]
    v = kv[:, width:]
    key_t = jnp.transpose(k.astype(F32)).astype(BF16)
    do = jnp.concatenate([do_ref[0][:, :width], do_ref[0][:, width:]], axis=0)
    seen = visible(scal, prefix, kv.shape[0], rows)
    cosine, sine = cos_ref[...], sin_ref[...]
    turned, ds_all, probs_all, q_all, do_all = [], [], [], [], []
    for head in range(heads):
        q_head = only_head(q, head) * (HD ** -0.5)
        do_head = only_head(do, head)
        scores = mm_nt(k, q_head)
        probs = jnp.where(seen, jnp.exp(scores - lse_ref[0, head:head + 1, :]), 0.0)
        dp = mm_nt(v, do_head)
        ds = (probs * (dp - jnp.sum(dp * probs, 0, keepdims=True))).astype(BF16)
        dq = mm(key_t[head * HD:(head + 1) * HD], ds) * (HD ** -0.5)
        first, second = dq[: HD // 2], dq[HD // 2:]
        turned += [first * cosine + second * sine, second * cosine - first * sine]
        ds_all.append(ds)
        probs_all.append(probs.astype(BF16))
        q_all.append(q_head)
        do_all.append(do_head)
    dq_ref[0] = jnp.transpose(jnp.concatenate(turned, axis=0)).astype(BF16)
    dk = mm(jnp.concatenate(ds_all, axis=1), jnp.concatenate(q_all, axis=0))
    dv = mm(jnp.concatenate(probs_all, axis=1), jnp.concatenate(do_all, axis=0))
    dkv = jnp.concatenate([dk, dv], axis=1).astype(BF16)
    for piece, out in enumerate((e0, e1, e2, e3)):
        out[0] = dkv[piece * rows:(piece + 1) * rows]


def last_kernel(scal, dq_ref, a_ref, b_ref, c_ref, n1_ref, w_ref, cos_ref, sin_ref, dh_ref, o_ref, dn1_ref, keep_ref, send_ref, all_s, o_s):
    step = pl.program_id(0)
    steps, rows, width = n1_ref.shape
    head_cols = dq_ref.shape[2]
    packed = w_ref.shape[1]
    at = pl.ds(pl.multiple_of(step * rows, rows), rows)
    dkv = a_ref[0].astype(F32) + b_ref[0].astype(F32) + c_ref[0].astype(F32)
    swung = dkv * sin_ref[:, 256:]
    high = swung.astype(BF16)
    low = (swung - high.astype(F32)).astype(BF16)
    turn = rotation(dkv.shape[1])
    dkv = dkv * cos_ref[:, 256:] + mm_nt(high, turn) + mm_nt(low, turn)
    all_s[at, :head_cols] = dq_ref[0]
    all_s[at, head_cols:256] = jnp.zeros((rows, 256 - head_cols), BF16)
    all_s[at, 256:] = dkv.astype(BF16)
    dn1_ref[0] = mm_nt(all_s[at, :], w_ref[...]).astype(BF16)
    block = o_ref[0]
    o_s[at, :] = jnp.concatenate([block[:, :head_cols], block[:, head_cols:]], axis=0)

    @pl.when(step == steps - 1)
    def _():
        blocks = keep_ref.shape[0]
        n1 = n1_ref[...].reshape(steps * rows, width)
        keep_ref[:, :, 0:packed], send_ref[:, :, 0:packed] = split_blocks(scal[4], mm_tn(n1, all_s[...]), blocks)
        out_t = mm_tn(dh_ref[...].reshape(steps * rows, width), o_s[...])
        rest = keep_ref.shape[2] - packed - head_cols
        out_t = jnp.concatenate([out_t, jnp.zeros((width, rest), F32)], axis=1)
        keep_ref[:, :, packed:], send_ref[:, :, packed:] = split_blocks(scal[4], out_t, blocks)


def end_kernel(scal, dn1_ref, dh2_ref, x_ref, small_ref, sums_in, gi_ref, sums_ref):
    x = x_ref[0].astype(F32)
    dn1 = dn1_ref[0].astype(F32)
    scale = row_scale(x)
    sums_ref[...] = sums_in[...]
    sums_ref[8:9, :] = jnp.sum(dn1 * x * scale, 0, keepdims=True)
    gi_ref[...] = (dh2_ref[...] + norm_back(dn1, x, scale, small_ref[8:9, :])).astype(BF16)


def whole(shape):
    return pl.BlockSpec(shape, lambda *_: (0,) * len(shape))


def by_step(shape):
    return pl.BlockSpec((1,) + shape, lambda i, *_: (i,) + (0,) * len(shape))


def call(kernel, grid, in_specs, out_specs, out_shape, scratch=(), prefetch=1, aliases=None, flops=0, nbytes=0):
    return pl.pallas_call(
        kernel,
        grid_spec=pltpu.PrefetchScalarGridSpec(
            num_scalar_prefetch=prefetch,
            grid=grid,
            in_specs=in_specs,
            out_specs=out_specs,
            scratch_shapes=scratch,
        ),
        out_shape=out_shape,
        input_output_aliases=aliases or {},
        compiler_params=params(len(grid)),
        cost_estimate=pl.CostEstimate(flops=int(flops), bytes_accessed=int(nbytes), transcendentals=0),
    )


def shape_of(shape, dtype=BF16):
    return jax.ShapeDtypeStruct(shape, dtype)


def body(
    fsdp_size,
    layer_input,
    gain_attn,
    query_weight,
    key_weight,
    value_weight,
    output_weight,
    gain_ffn,
    router,
    exp_gate,
    exp_up,
    exp_down,
    shared_gate_weight,
    shared_up_weight,
    shared_down_weight,
    routes,
    prefix,
    cotangent,
):
    seqs, rows, width = layer_input.shape
    experts = exp_gate.shape[0]
    hidden = exp_gate.shape[2]
    head_cols = query_weight.shape[1]
    half = width // 2
    paired = fsdp_size == 2
    ctx = lax.axis_index("ctx")
    tp = lax.axis_index("tp")
    ctx_size = lax.axis_size("ctx")
    tp_size = lax.axis_size("tp")
    side = lax.axis_index("fsdp") if paired else jnp.int32(0)
    weight_ctx = ctx if paired else jnp.int32(0)
    blocks = fsdp_size * ctx_size
    direct = paired and ctx_size == 4
    core = ctx % 2 if direct else jnp.int32(0)
    scal = jnp.stack([side, ctx, tp, weight_ctx, core]).astype(jnp.int32)

    def over_x(value):
        return lax.ppermute(value, "fsdp", [(0, 1), (1, 0)])

    def over_ctx(value, bit):
        return lax.ppermute(value, "ctx", [(i, i ^ bit) for i in range(ctx_size)])

    columns = jnp.concatenate(
        [
            query_weight,
            router,
            gain_attn[:, None],
            gain_ffn[:, None],
            jnp.zeros((query_weight.shape[0], 54), BF16),
            key_weight,
            value_weight,
        ],
        axis=1,
    )
    if paired:
        columns_own, columns_other = columns, over_x(columns)
    else:
        columns = lax.all_gather(columns, "fsdp", axis=0, tiled=True)
        columns_own, columns_other = columns[:half], columns[half:]

    if paired:
        def quarter(stack, shared):
            mine = lax.dynamic_slice_in_dim(stack, 2 * ctx, 2, 0).reshape(-1, stack.shape[2])
            part = shared.shape[0] // 4
            return jnp.concatenate([mine, lax.dynamic_slice_in_dim(shared, part * ctx, part, 0)], axis=0)

        def pieces(stack, shared):
            first = over_x(quarter(stack, shared))
            return first

        gate_0 = pieces(exp_gate, shared_gate_weight)
        up_0 = pieces(exp_up, shared_up_weight)
        down_0 = pieces(exp_down, shared_down_weight)
        own = (exp_gate, exp_up, exp_down, shared_gate_weight, shared_up_weight, shared_down_weight)
    else:
        gate_all = lax.all_gather(exp_gate, "fsdp", axis=1, tiled=True)
        up_all = lax.all_gather(exp_up, "fsdp", axis=1, tiled=True)
        down_all = lax.all_gather(exp_down, "fsdp", axis=2, tiled=True)
        sg_all = lax.all_gather(shared_gate_weight, "fsdp", axis=0, tiled=True)
        su_all = lax.all_gather(shared_up_weight, "fsdp", axis=0, tiled=True)
        sd_all = lax.all_gather(shared_down_weight, "fsdp", axis=1, tiled=True)
        own = (gate_all[:, :half], up_all[:, :half], down_all[:, :, :half], sg_all[:half], su_all[:half], sd_all[:, :half])

        def split(stack, shared):
            part = shared.shape[0] // 4
            return [
                jnp.concatenate(
                    [stack[2 * p:2 * p + 2].reshape(-1, stack.shape[2]), shared[p * part:(p + 1) * part]], axis=0
                )
                for p in range(4)
            ]

        gates_p = split(gate_all[:, half:], sg_all[half:])
        ups_p = split(up_all[:, half:], su_all[half:])
        downs_p = split(down_all[:, :, half:], sd_all[:, half:])

    out_pieces = lax.all_gather(output_weight, ("fsdp", "tp"), axis=0)
    out_pieces = out_pieces.reshape(fsdp_size, tp_size, head_cols, output_weight.shape[1])
    if not paired:
        out_pieces = jnp.transpose(out_pieces, (1, 2, 0, 3)).reshape(tp_size, head_cols, 2, half)
        out_pieces = jnp.transpose(out_pieces, (2, 0, 1, 3))

    positions = (ctx * rows + jnp.arange(rows, dtype=jnp.int32)).astype(F32)
    inverse = jnp.exp(jnp.arange(HD // 2, dtype=F32) * (-math.log(10000.0) / (HD // 2)))
    angles = positions[:, None] * inverse[None, :]
    cosine, sine = jnp.cos(angles), jnp.sin(angles)
    heads = head_cols // HD

    def table(value, rest):
        turned = jnp.tile(value, (1, 2 * heads))
        plain = jnp.full((rows, head_cols), rest, F32)
        return jnp.concatenate([turned, plain[:, :64], turned, plain], axis=1)

    cos_table, sin_table = table(cosine, 1.0), table(sine, 0.0)
    packed = cos_table.shape[1]

    n1, q, kv, w_qkv, small = call(
        qkv_kernel,
        (seqs,),
        [
            by_step((rows, width)),
            whole((half, packed)),
            whole((half, packed)),
            whole((rows, packed)),
            whole((rows, packed)),
        ],
        [
            by_step((rows, width)),
            by_step((rows, head_cols)),
            by_step((rows, 2 * head_cols)),
            whole((width, packed)),
            whole((16, width)),
        ],
        [
            shape_of((seqs, rows, width)),
            shape_of((seqs, rows, head_cols)),
            shape_of((seqs, rows, 2 * head_cols)),
            shape_of((width, packed)),
            shape_of((16, width), F32),
        ],
        [pltpu.VMEM((width, packed), BF16)],
        flops=4 * seqs * rows * width * packed,
        nbytes=8e6,
    )(scal, layer_input, columns_own, columns_other, cos_table, sin_table)

    kv_0 = kv
    kv_2 = over_ctx(kv_0, 2)
    kv_1 = over_ctx(kv_0, 1)
    kv_3 = over_ctx(kv_2, 1)
    kvs = (kv_0, kv_1, kv_2, kv_3)

    if paired:
        gate_2, up_2, down_2 = over_ctx(gate_0, 2), over_ctx(up_0, 2), over_ctx(down_0, 2)
        gates_p = (gate_0, over_ctx(gate_0, 1), gate_2, over_ctx(gate_2, 1))
        ups_p = (up_0, over_ctx(up_0, 1), up_2, over_ctx(up_2, 1))
        downs_p = (down_0, over_ctx(down_0, 1), down_2, over_ctx(down_2, 1))

    o, lse = call(
        attn_fwd_kernel,
        (seqs,),
        [by_step((rows, head_cols))] + [by_step((rows, 2 * head_cols))] * 4,
        [by_step((rows // 2, 2 * head_cols)), by_step((8, rows))],
        [shape_of((seqs, rows // 2, 2 * head_cols)), shape_of((seqs, 8, rows), F32)],
        prefetch=2,
        flops=4 * seqs * heads * rows * rows * ctx_size * 256,
        nbytes=4e6,
    )(scal, prefix, q, *kvs)

    o_all = lax.all_gather(o, "tp", axis=0)
    routes_t = jnp.pad(jnp.transpose(routes, (0, 2, 1)), ((0, 0), (0, 6), (0, 0)))
    n2, h2, gates, slots = call(
        post_kernel,
        (seqs,),
        [
            pl.BlockSpec((tp_size, 1, rows // 2, 2 * head_cols), lambda i, *_: (0, i, 0, 0)),
            whole((2, tp_size, head_cols, half)),
            by_step((rows, width)),
            whole((16, width)),
            by_step((8, rows)),
        ],
        [by_step((rows, width)), whole((rows, width)), by_step((8, rows)), by_step((8, rows))],
        [
            shape_of((seqs, rows, width)),
            shape_of((rows, width), F32),
            shape_of((seqs, 8, rows), F32),
            shape_of((seqs, 8, rows), jnp.int32),
        ],
        [pltpu.VMEM((width, width), BF16)],
        flops=2 * seqs * rows * width * width,
        nbytes=8e6,
    )(scal, o_all, out_pieces, layer_input, small, routes_t)

    part_rows = 3 * (width // 8)
    full = whole((seqs, rows, width))
    shared_down_rows = hidden // 4
    grads_shape = shape_of((4, experts + 1, part_rows, hidden))
    upper = pl.BlockSpec((half // 4, hidden), lambda *_: (8, 0))
    lower = pl.BlockSpec((shared_down_rows, half), lambda *_: (8, 0))
    row_out = pl.BlockSpec((1, rows, width), lambda i, *_: (jnp.minimum(i, seqs - 1), 0, 0))
    shared_grads = pl.BlockSpec((4, 1, part_rows, hidden), lambda *_: (0, experts, 0, 0))
    ys, dn_shared, keep, send = call(
        shared_kernel,
        (seqs + 1,),
        [full, full, whole((half, hidden)), whole((half, hidden)), whole((hidden, half))]
        + [upper] * 8
        + [lower] * 4,
        [row_out, row_out, shared_grads, shared_grads],
        [shape_of((seqs, rows, width)), shape_of((seqs, rows, width)), grads_shape, grads_shape],
        [pltpu.VMEM((width, hidden), BF16)] * 2
        + [pltpu.VMEM((hidden, width), BF16)]
        + [pltpu.VMEM((seqs * rows, hidden), BF16)] * 3,
        flops=18 * seqs * rows * width * hidden,
        nbytes=14e6,
    )(scal, n2, cotangent, *own[3:], *gates_p, *ups_p, *downs_p)

    def expert_of(i, scal):
        i = jnp.minimum(i, experts - 1)
        return 2 * ((i // 2) ^ scal[3]) + i % 2

    def own_spec(shape):
        return pl.BlockSpec((1,) + shape, lambda i, scal: (expert_of(i, scal), 0, 0))

    def piece_specs(shape):
        return [
            pl.BlockSpec(shape, lambda i, scal, p=p: (jnp.clip(i - 2 * p, 0, 1), 0)) for p in range(4)
        ]

    late = pl.BlockSpec((1, rows, width), lambda i, *_: (jnp.maximum(i - experts, 0), 0, 0))
    dn_rows = rows + 16
    expert_grads = pl.BlockSpec((4, 1, part_rows, hidden), lambda i, scal: (0, expert_of(i, scal), 0, 0))
    y, dn, keep, send = call(
        moe_kernel,
        (experts + seqs,),
        [full, full, whole((seqs, 8, rows)), whole((seqs, 8, rows)), late, late]
        + [own_spec((half, hidden)), own_spec((half, hidden)), own_spec((hidden, half))]
        + piece_specs((half, hidden)) * 2
        + piece_specs((hidden, half))
        + [pl.BlockSpec(memory_space=pl.ANY)] * 2,
        [
            late,
            pl.BlockSpec((1, dn_rows, width), lambda i, *_: (jnp.maximum(i - experts, 0), 0, 0)),
            expert_grads,
            expert_grads,
        ],
        [shape_of((seqs, rows, width)), shape_of((seqs, dn_rows, width)), grads_shape, grads_shape],
        [pltpu.VMEM((width, hidden), BF16)] * 2
        + [pltpu.VMEM((hidden, width), BF16)]
        + [pltpu.VMEM((seqs, experts * SLOTS, rows), BF16)]
        + [pltpu.VMEM((seqs, experts * SLOTS, width), BF16)] * 2
        + [pltpu.VMEM((seqs * SLOTS, width), BF16)] * 3
        + [pltpu.VMEM((seqs * SLOTS, 128), F32), pltpu.VMEM((seqs, 8, rows), F32)],
        aliases={22: 2, 23: 3},
        flops=18 * seqs * experts * SLOTS * width * hidden,
        nbytes=50e6,
    )(scal, n2, cotangent, slots, gates, ys, dn_shared, *own[:3], *gates_p, *ups_p, *downs_p, keep, send)

    dn_own = lax.psum_scatter(dn, "tp", scatter_dimension=0, tiled=True)
    mine = pl.BlockSpec((1, rows, width), lambda i, scal: (scal[2], 0, 0))
    dh2, do, dh2_low, sums = call(
        mid_kernel,
        (1,),
        [
            whole((1, dn_rows, width)),
            pl.BlockSpec((1, 8, rows), lambda i, scal: (scal[2], 0, 0)),
            whole((rows, width)),
            mine,
            mine,
            whole((16, width)),
            whole((2, tp_size, head_cols, half)),
        ],
        [
            whole((rows, width)),
            whole((tp_size, rows // 2, 2 * head_cols)),
            whole((rows, width)),
            whole((16, width)),
        ],
        [
            shape_of((rows, width), F32),
            shape_of((tp_size, rows // 2, 2 * head_cols)),
            shape_of((rows, width)),
            shape_of((16, width), F32),
        ],
        [pltpu.VMEM((width, width), BF16)],
        flops=2 * rows * width * width,
        nbytes=5e6,
    )(scal, dn_own, gates, h2, n2, cotangent, small, out_pieces)
    do = lax.all_to_all(do, "tp", 0, 0, tiled=True)
    dh2_all = lax.all_gather(dh2_low, "tp", axis=0)

    y_own = lax.psum_scatter(y, "tp", scatter_dimension=0, tiled=True)
    activations = lax.all_gather((h2 + y_own[0].astype(F32)).astype(BF16), "tp", axis=0)

    part = width // blocks
    along_x, along_y = side, ctx // 2

    def pick(value, x, y, first, last):
        value = value.reshape((2, 2) + value.shape[1:])[:, :, first:last]
        if y is not None:
            value = lax.dynamic_index_in_dim(value, y, 1, False)
        if x is not None:
            value = lax.dynamic_index_in_dim(value, x, 0, False)
        return value.astype(F32)

    def scatter(keep, got, first, last, y_first):
        def both(x, y):
            return pick(keep, x, y, first, last) + pick(got, x, y, first, last)

        if y_first:
            far = over_ctx(both(None, 1 - along_y).astype(BF16), 2)
            away = both(1 - along_x, along_y) + lax.dynamic_index_in_dim(far, 1 - along_x, 0, False).astype(F32)
            here = both(along_x, along_y) + lax.dynamic_index_in_dim(far, along_x, 0, False).astype(F32)
            return here + over_x(away.astype(BF16)).astype(F32)
        far = over_x(both(1 - along_x, None).astype(BF16))
        away = both(along_x, 1 - along_y) + lax.dynamic_index_in_dim(far, 1 - along_y, 0, False).astype(F32)
        here = both(along_x, along_y) + lax.dynamic_index_in_dim(far, along_y, 0, False).astype(F32)
        return here + over_ctx(away.astype(BF16), 2).astype(F32)

    def scatter_plain(keep, send):
        both = jnp.stack([keep, send], axis=1)
        count, cols = both.shape[2], both.shape[4]
        both = jnp.transpose(both, (0, 1, 3, 2, 4)).reshape(blocks, part, count, cols)
        both = jnp.transpose(both, (0, 2, 1, 3)).reshape(blocks, count * part, cols)
        both = lax.psum_scatter(both, ("fsdp", "ctx"), scatter_dimension=0, tiled=True)
        return both.reshape(count, part, cols).astype(F32)

    if direct:
        got = over_ctx(send, 1)
        cut = experts // 2
        low_part = scatter(keep, got, 0, cut, True).reshape(cut, 3, part, hidden)
        high_part = scatter(keep, got, cut, experts + 1, False).reshape(experts + 1 - cut, 3, part, hidden)
        grads_exp = [jnp.concatenate([low_part[:, i], high_part[:-1, i]], axis=0) for i in range(3)]
        grads_shared = high_part[-1]
    else:
        shape = (4, (experts + 1) * 3, width // 8, hidden)
        grads = scatter_plain(keep.reshape(shape), send.reshape(shape)).reshape(experts + 1, 3, part, hidden)
        grads_exp = [grads[:experts, i] for i in range(3)]
        grads_shared = grads[experts]

    cos_t, sin_t = jnp.transpose(cosine), jnp.transpose(sine)
    kv_block = by_step((rows, 2 * head_cols))
    dq, e0, e1, e2, e3 = call(
        attn_bwd_kernel,
        (seqs,),
        [by_step((rows, head_cols))]
        + [kv_block] * 4
        + [by_step((8, rows)), by_step((rows // 2, 2 * head_cols)), whole((HD // 2, rows)), whole((HD // 2, rows))],
        [by_step((rows, head_cols))] + [kv_block] * 4,
        [shape_of((seqs, rows, head_cols))] + [shape_of((seqs, rows, 2 * head_cols))] * 4,
        prefetch=2,
        flops=10 * seqs * heads * rows * rows * ctx_size * 256,
        nbytes=10e6,
    )(scal, prefix, q, *kvs, lse, do, cos_t, sin_t)
    from_core_1 = over_ctx(e1, 1)
    from_core_3 = over_ctx(e3, 1)
    far = (e2.astype(F32) + from_core_3.astype(F32)).astype(BF16)
    from_y = over_ctx(far, 2)

    dn1, keep, send = call(
        last_kernel,
        (seqs,),
        [
            by_step((rows, head_cols)),
            kv_block,
            kv_block,
            kv_block,
            whole((seqs, rows, width)),
            whole((width, packed)),
            whole((rows, packed)),
            whole((rows, packed)),
            whole((seqs, rows, width)),
            by_step((rows // 2, 2 * head_cols)),
        ],
        [by_step((rows, width)), whole((4, width // 8, 896)), whole((4, width // 8, 896))],
        [shape_of((seqs, rows, width)), shape_of((4, width // 8, 896)), shape_of((4, width // 8, 896))],
        [pltpu.VMEM((seqs * rows, packed), BF16), pltpu.VMEM((seqs * rows, head_cols), BF16)],
        flops=4 * seqs * rows * width * packed + 2 * seqs * rows * width * head_cols,
        nbytes=12e6,
    )(scal, dq, e0, from_core_1, from_y, n1, w_qkv, cos_table, sin_table, dh2_all, o)
    dn1_own = lax.psum_scatter(dn1, "tp", scatter_dimension=0, tiled=True)
    keep, send = keep[:, None], send[:, None]
    if direct:
        grads_attn = scatter(keep, over_ctx(send, 1), 0, 1, True)[0]
    else:
        grads_attn = scatter_plain(keep, send)[0]

    gi, sums = call(
        end_kernel,
        (1,),
        [whole((1, rows, width)), whole((rows, width)), mine, whole((16, width)), whole((16, width))],
        [whole((rows, width)), whole((16, width))],
        [shape_of((rows, width)), shape_of((16, width), F32)],
        nbytes=3e6,
    )(scal, dn1_own, dh2, layer_input, small, sums)
    grad_input = lax.all_gather(gi, "tp", axis=0).astype(F32)
    if direct and tp_size == 4:
        sums = sums + over_ctx(sums, 1)
        sums = sums + over_ctx(sums, 2)
        sums = sums + over_x(sums)
        for bit in (1, 2):
            sums = sums + lax.ppermute(sums, "tp", [(i, i ^ bit) for i in range(tp_size)])
    else:
        sums = lax.psum(sums, ("fsdp", "ctx", "tp"))
    block = lax.axis_index("fsdp") * ctx_size + ctx
    sums = lax.dynamic_slice_in_dim(sums, block * part, part, 1)

    return (
        activations.reshape(layer_input.shape),
        grad_input.reshape(layer_input.shape),
        sums[8],
        grads_attn[:, :head_cols],
        grads_attn[:, 256:256 + head_cols],
        grads_attn[:, 256 + head_cols:256 + 2 * head_cols],
        jnp.transpose(grads_attn[:, packed:packed + head_cols]),
        sums[9],
        jnp.transpose(sums[0:8]),
        grads_exp[0],
        grads_exp[1],
        jnp.transpose(grads_exp[2], (0, 2, 1)),
        grads_shared[0],
        grads_shared[1],
        jnp.transpose(grads_shared[2]),
    )


def solution(mesh):
    placed = (
        P("fsdp", "ctx", None),
        P("fsdp"),
        P("fsdp", "tp"),
        P("fsdp", "tp"),
        P("fsdp", "tp"),
        P("tp", "fsdp"),
        P("fsdp"),
        P("fsdp", None),
        P(None, "fsdp", "tp"),
        P(None, "fsdp", "tp"),
        P(None, "tp", "fsdp"),
        P("fsdp", "tp"),
        P("fsdp", "tp"),
        P("tp", "fsdp"),
        P("fsdp", "ctx", None),
        P("fsdp"),
        P("fsdp", "ctx", None),
    )
    return jax.shard_map(
        functools.partial(body, mesh.shape["fsdp"]),
        mesh=mesh,
        in_specs=placed,
        out_specs=(
            P("fsdp", "ctx", None),
            P("fsdp", "ctx", None),
            P(("fsdp", "ctx")),
            P(("fsdp", "ctx"), "tp"),
            P(("fsdp", "ctx"), "tp"),
            P(("fsdp", "ctx"), "tp"),
            P("tp", ("fsdp", "ctx")),
            P(("fsdp", "ctx")),
            P(("fsdp", "ctx"), None),
            P(None, ("fsdp", "ctx"), "tp"),
            P(None, ("fsdp", "ctx"), "tp"),
            P(None, "tp", ("fsdp", "ctx")),
            P(("fsdp", "ctx"), "tp"),
            P(("fsdp", "ctx"), "tp"),
            P("tp", ("fsdp", "ctx")),
        ),
        check_vma=False,
    )
```

time: 1460 us -> 480 us (0.33)
  waiting for transfers between devices: 759 us -> 219 us
  local copies, waits for them, and re-layouts: 310 us -> 51.6 us
  matrix products: 181 us -> 0 us
  blocking collectives: 126 us -> 0 us
  Pallas kernels: 0 us -> 125 us
  starting transfers between devices: 1.51 us -> 32.6 us
  other arithmetic: 56.9 us -> 36.1 us
    reduce_scatter x10 -> x3, waiting for transfers between devices: 508 us -> 50.1 us  [the longest x1 38.1 us: body(): dn_own = lax.psum_scatter(dn, 'tp', scatter_dimension=0, tiled=True)]
    dot_general x39 -> x0, matrix products: 178 us -> none  [the longest x1 11 us: body(): jnp.einsum('enf,end->efd', expert_hid, expert_out_back, preferred_element...]
    unnamed x121 -> x48, local copies, waits for them, and re-layouts: 188 us -> 17.2 us
    all_gather x5, waiting for transfers between devices: 160 us -> 25.9 us  [the longest x1 24.9 us: body(): lax.all_gather((h2 + y_own[0].astype(F32)).astype(BF16), 'tp', axis=0)]
    pallas_call x0 -> x9, Pallas kernels: none -> 125 us  [the longest x1 46 us: body(): call(moe_kernel, (experts + seqs,), [full, full, whole((seqs, 8, rows)),...]
    ppermute x0 -> x32, waiting for transfers between devices: none -> 124 us  [the longest x22 68.3 us: over_ctx(): return lax.ppermute(value, 'ctx', [(i, i ^ bit) for i in range(ctx_size)])]
    all_gather x10 -> x0, blocking collectives: 101 us -> none  [the longest x1 21.8 us: body(): lax.all_gather(shared_up_weight, 'fsdp', axis=0, tiled=True)]
    gather x4 -> x0, local copies, waits for them, and re-layouts: 96.4 us -> none  [the longest x2 48.3 us: body(): expert_output.reshape(experts, sequences, capacity, model_width)]
  transfers between devices with their start and end apart: 21 -> 41, of which waited for: 15 -> 20; matrix products, arithmetic and copies ran while one was open for 28% -> 14% of each run, Pallas kernels for 0% -> 13%
where the time goes in v1:
time: 480 us; the launch traced here: 478 us
  waiting for transfers between devices  219 us (46%)
  Pallas kernels  125 us (26%)
  local copies, waits for them, and re-layouts  51.6 us (11%)
  other arithmetic  36.1 us (8%)
  starting transfers between devices  32.6 us (7%)
  between operations  14.7 us (3%)
    ppermute x22, waiting for transfers between devices, over_ctx(): return lax.ppermute(value, 'ctx', [(i, i ^ bit) for i in range(ctx_size)])  68.3 us
    ppermute x8, waiting for transfers between devices, over_x(): return lax.ppermute(value, 'fsdp', [(0, 1), (1, 0)])  52.7 us
    pallas_call x1, Pallas kernels, body(): call(moe_kernel, (experts + seqs,), [full, full, whole((seqs, 8, rows)),...  46 us
    reduce_scatter x1, waiting for transfers between devices, body(): dn_own = lax.psum_scatter(dn, 'tp', scatter_dimension=0, tiled=True)  38.1 us
    all_gather x1, waiting for transfers between devices, body(): lax.all_gather((h2 + y_own[0].astype(F32)).astype(BF16), 'tp', axis=0)  24.9 us
    all_to_all x1, waiting for transfers between devices, body(): do = lax.all_to_all(do, 'tp', 0, 0, tiled=True)  17.6 us
    unnamed x48, local copies, waits for them, and re-layouts  17.2 us
    pallas_call x1, Pallas kernels, body(): call(attn_bwd_kernel, (seqs,), [by_step((rows, head_cols))] + [kv_block]...  16.6 us
  transfers between devices with their start and end apart: 41, of which 20 were waited for; matrix products, arithmetic and copies ran while one was open for 14% of the time, Pallas kernels for 13%

profile of v1, /device:TPU:0, one launch (start us, length us, event | category | flops | bytes accessed | tf_op | source)
XLA Modules:
  0.0 478.4 jit_solution(18011229637749938257)
XLA Ops:
  19.2 9.3 %collective-permute-done.oth_ref = bf16[384,640]{1,0:T(8,128)(2,1)S(1)} collective-permute-done((bf16[384,640]{1,0:T(8,128)(2,1)S(1)}, bf16[384,640]{1,0:T(8,128)(2,1)S(1)}, u32[]{:S(2)}, u32[]{:S(2)}) %collective-permute-start) | collective-permute-done | bytes 491552 | tf_op jit(solution)/shard_map/ppermute | solution.py:454
  29.2 8.3 %shard_map.280 = (bf16[4,256,768]{2,1,0:T(8,128)(2,1)}, bf16[4,256,192]{2,1,0:T(8,128)(2,1)}, bf16[4,256,384]{2,1,0:T(8,128)(2,1)}, bf16[768,640]{1,0:T(8,128)(2,1)}, f32[16,768]{1,0:T(8,128)}) custom-call(s32[5]{0:T(128)} %stack.20.scal, bf16[4,256,768]{2,1,0:T(8,128)(2,1)} %x_ref.5, bf16[384,640]{1,0:T(8,128)(2,1)} %copy-done.8, ...), custom_call_target="tpu_custom_call" | custom-call | flops 2013265920 | bytes 8000000 | tf_op jit(solution)/shard_map/pallas_call | solution.py:533
  41.6 14.1 %collective-permute-done.2.kv2 = bf16[4,256,384]{2,1,0:T(8,128)(2,1)} collective-permute-done((bf16[4,256,384]{2,1,0:T(8,128)(2,1)}, bf16[4,256,384]{2,1,0:T(8,128)(2,1)}, u32[]{:S(2)}, u32[]{:S(2)}) %collective-permute-start.2) | collective-permute-done | bytes 786464 | tf_op jit(solution)/shard_map/ppermute | solution.py:457
  63.0 12.5 %shard_map.281 = (bf16[4,128,384]{2,1,0:T(8,128)(2,1)}, f32[4,8,256]{2,1,0:T(8,128)}) custom-call(s32[5]{0:T(128)} %stack.20.scal, s32[4]{0:T(128)} %prefix.3, bf16[4,256,192]{2,1,0:T(8,128)(2,1)} %get-tuple-element.48.q_ref, bf16[4,256,384]{2,1,0:T(8,128)(2,1)} %get-tuple-element.49.kv0, bf16[4,256,384]{2,1,0:T(8,128)(2,1)} %collective-permute-done.1.kv1, ...), custom_call_target="tpu_custom_call" | custom-call | flops 3221225472 | bytes 4000000 | tf_op jit(solution)/shard_map/pallas_call | solution.py:574
  79.8 17.6 %collective-permute-done.8.u0 = bf16[864,512]{1,0:T(8,128)(2,1)} collective-permute-done((bf16[864,512]{1,0:T(8,128)(2,1)S(1)}, bf16[864,512]{1,0:T(8,128)(2,1)}, u32[]{:S(2)}, u32[]{:S(2)}) %collective-permute-start.8) | collective-permute-done | bytes 884768 | tf_op jit(solution)/shard_map/ppermute | solution.py:454
  98.8 17.2 %collective-permute-done.12.d0 = bf16[1152,384]{1,0:T(8,128)(2,1)} collective-permute-done((bf16[1152,384]{1,0:T(8,128)(2,1)S(1)}, bf16[1152,384]{1,0:T(8,128)(2,1)}, u32[]{:S(2)}, u32[]{:S(2)}) %collective-permute-start.12) | collective-permute-done | bytes 884768 | tf_op jit(solution)/shard_map/ppermute | solution.py:454
  119.9 18.3 %collective-permute-done.14.d2 = bf16[1152,384]{1,0:T(8,128)(2,1)S(1)} collective-permute-done((bf16[1152,384]{1,0:T(8,128)(2,1)}, bf16[1152,384]{1,0:T(8,128)(2,1)S(1)}, u32[]{:S(2)}, u32[]{:S(2)}) %collective-permute-start.14) | collective-permute-done | bytes 884768 | tf_op jit(solution)/shard_map/ppermute | solution.py:457
  139.0 7.3 %shard_map.282 = (bf16[4,256,768]{2,1,0:T(8,128)(2,1)}, f32[256,768]{1,0:T(8,128)}, f32[4,8,256]{2,1,0:T(8,128)}, s32[4,8,256]{2,1,0:T(8,128)}) custom-call(s32[5]{0:T(128)} %stack.20.scal, bf16[4,4,128,384]{3,2,1,0:T(8,128)(2,1)} %bitcast.137, bf16[2,4,192,384]{3,2,1,0:T(8,128)(2,1)} %bitcast.130, bf16[4,256,768]{2,1,0:T(8,128)(2,1)} %x_ref.5, ...), custom_call_target="tpu_custom_call" | custom-call | flops 1207959552 | bytes 8000000 | tf_op jit(solution)/shard_map/pallas_call | solution.py:587
  146.4 15.1 %shard_map.283 = (bf16[4,256,768]{2,1,0:T(8,128)(2,1)}, bf16[4,256,768]{2,1,0:T(8,128)(2,1)}, bf16[4,9,288,512]{3,2,1,0:T(8,128)(2,1)}, bf16[4,9,288,512]{3,2,1,0:T(8,128)(2,1)}) custom-call(s32[5]{0:T(128)} %stack.20.scal, bf16[4,256,768]{2,1,0:T(8,128)(2,1)} %get-tuple-element.53.n2_ref, bf16[4,256,768]{2,1,0:T(8,128)(2,1)} %dy_ref.5, ...), custom_call_target="tpu_custom_call" | custom-call | flops 7247757312 | bytes 14000000 | tf_op jit(solution)/shard_map/pallas_call | solution.py:617
  161.5 46.0 %shard_map.284 = (bf16[4,256,768]{2,1,0:T(8,128)(2,1)}, bf16[4,272,768]{2,1,0:T(8,128)(2,1)}, bf16[4,9,288,512]{3,2,1,0:T(8,128)(2,1)}, bf16[4,9,288,512]{3,2,1,0:T(8,128)(2,1)}) custom-call(s32[5]{0:T(128)} %stack.20.scal, bf16[4,256,768]{2,1,0:T(8,128)(2,1)} %get-tuple-element.53.n2_ref, ...), custom_call_target="tpu_custom_call", output_to_operand_aliasing={{2}: (22, {}), {3}: (23, {})} | custom-call | flops 18119393280 | bytes 50000000 | tf_op jit(solution)/shard_map/pallas_call | solution.py:647
  208.2 38.1 %reduce-scatter.6.cloned.1.call-done.dn_ref = bf16[1,272,768]{2,1,0:T(8,128)(2,1)} async-done(((bf16[4,272,768]{2,1,0:T(8,128)(2,1)}), bf16[1,272,768]{2,1,0:T(8,128)(2,1)}) %reduce-scatter.6.cloned.1.call-update) | async-done | bytes 417808 | tf_op jit(solution)/shard_map/reduce_scatter | solution.py:673
  246.3 4.6 shard_map.285
  256.1 17.6 %all-to-all-done.do_ref = bf16[4,128,384]{2,1,0:T(8,128)(2,1)S(1)} async-done(((bf16[4,128,384]{2,1,0:T(8,128)(2,1)}), bf16[4,128,384]{2,1,0:T(8,128)(2,1)S(1)}, u32[]{:S(2)}, u32[]{:S(2)}) %all-to-all-start) | async-done | bytes 393248 | tf_op jit(solution)/shard_map/all_to_all | solution.py:703
  274.5 16.6 %shard_map.286 = (bf16[4,256,192]{2,1,0:T(8,128)(2,1)}, bf16[4,256,384]{2,1,0:T(8,128)(2,1)}, bf16[4,256,384]{2,1,0:T(8,128)(2,1)}, bf16[4,256,384]{2,1,0:T(8,128)(2,1)}, bf16[4,256,384]{2,1,0:T(8,128)(2,1)}) custom-call(s32[5]{0:T(128)} %stack.20.scal, s32[4]{0:T(128)} %prefix.3, bf16[4,256,192]{2,1,0:T(8,128)(2,1)} %get-tuple-element.48.q_ref, ...), custom_call_target="tpu_custom_call" | custom-call | flops 8053063680 | bytes 10000000 | tf_op jit(solution)/shard_map/pallas_call | solution.py:757
  296.4 18.2 %collective-permute-done.18.c_ref = bf16[4,256,384]{2,1,0:T(8,128)(2,1)S(1)} collective-permute-done((bf16[4,256,384]{2,1,0:T(8,128)(2,1)S(1)}, bf16[4,256,384]{2,1,0:T(8,128)(2,1)S(1)}, u32[]{:S(2)}, u32[]{:S(2)}) %collective-permute-start.18) | collective-permute-done | bytes 786464 | tf_op jit(solution)/shard_map/ppermute | solution.py:457
  315.5 10.9 %shard_map.287 = (bf16[4,256,768]{2,1,0:T(8,128)(2,1)}, bf16[4,96,896]{2,1,0:T(8,128)(2,1)}, bf16[4,96,896]{2,1,0:T(8,128)(2,1)}) custom-call(s32[5]{0:T(128)} %stack.20.scal, bf16[4,256,192]{2,1,0:T(8,128)(2,1)} %get-tuple-element.64.dq_ref, bf16[4,256,384]{2,1,0:T(8,128)(2,1)} %get-tuple-element.65.a_ref, bf16[4,256,384]{2,1,0:T(8,128)(2,1)} %copy-done.6, ...), custom_call_target="tpu_custom_call" | custom-call | flops 2315255808 | bytes 12000000 | tf_op jit(solution)/shard_map/pallas_call | solution.py:774
  333.7 5.4 %slice.115 = bf16[2,2,5,288,512]{4,3,2,1,0:T(8,128)(2,1)S(1)} slice(bf16[2,2,9,288,512]{4,3,2,1,0:T(8,128)(2,1)} %bitcast.30), slice={[0:2], [0:2], [4:9], [0:288], [0:512]} | slice | bytes 11796480 | tf_op jit(solution)/shard_map/slice | solution.py:713
  346.7 4.4 slice.112
  355.6 9.9 %reduce-scatter.8.cloned.1.call-done.dn1_ref = bf16[1,256,768]{2,1,0:T(8,128)(2,1)} async-done(((bf16[4,256,768]{2,1,0:T(8,128)(2,1)}), bf16[1,256,768]{2,1,0:T(8,128)(2,1)}) %reduce-scatter.8.cloned.1.call-update) | async-done | bytes 393232 | tf_op jit(solution)/shard_map/reduce_scatter | solution.py:795
  378.9 24.9 %all-gather.15.cloned.1.call-done = bf16[1024,768]{1,0:T(8,128)(2,1)} async-done(((bf16[256,768]{1,0:T(8,128)(2,1)}), bf16[1024,768]{1,0:T(8,128)(2,1)}) %all-gather.15.cloned.1.call-update) | async-done | bytes 1572880 | tf_op jit(solution)/shard_map/all_gather | solution.py:707
  411.0 6.9 %collective-permute-done.20 = f32[16,768]{1,0:T(8,128)S(1)} collective-permute-done((f32[16,768]{1,0:T(8,128)S(1)}, f32[16,768]{1,0:T(8,128)S(1)}, u32[]{:S(2)}, u32[]{:S(2)}) %collective-permute-start.20) | collective-permute-done | bytes 49184 | tf_op jit(solution)/shard_map/ppermute | solution.py:457
  426.4 3.6 fusion.1
  446.7 5.0 %collective-permute-done.29 = bf16[4,288,512]{2,1,0:T(8,128)(2,1)} collective-permute-done((bf16[4,288,512]{2,1,0:T(8,128)(2,1)}, bf16[4,288,512]{2,1,0:T(8,128)(2,1)}, u32[]{:S(2)}, u32[]{:S(2)}) %collective-permute-start.29) | collective-permute-done | bytes 1179680 | tf_op jit(solution)/shard_map/ppermute | solution.py:454
  455.0 6.8 %collective-permute-done.31 = bf16[5,288,512]{2,1,0:T(8,128)(2,1)} collective-permute-done((bf16[5,288,512]{2,1,0:T(8,128)(2,1)}, bf16[5,288,512]{2,1,0:T(8,128)(2,1)}, u32[]{:S(2)}, u32[]{:S(2)}) %collective-permute-start.31) | collective-permute-done | bytes 1474592 | tf_op jit(solution)/shard_map/ppermute | solution.py:457
  (188 shorter events, 125.1 us)
Async XLA Ops:
  7.2 131.8 %all-gather.13.cloned.1.call-start = ((), (), s32[]{:S(2)}) async-start(), calls=%async_computation.8 | async-start | bytes 1327104 | tf_op jit(solution)/shard_map/all_gather | solution.py:513
  16.4 122.6 %all-gather.11.cloned.1.call-start = ((), (), s32[]{:S(2)}) async-start(), calls=%async_computation.7 | async-start | bytes 1966080 | tf_op jit(solution)/shard_map/all_gather | solution.py:585
  58.6 38.7 %collective-permute-start.8 = (bf16[864,512]{1,0:T(8,128)(2,1)S(1)}, bf16[864,512]{1,0:T(8,128)(2,1)}, u32[]{:S(2)}, u32[]{:S(2)}) collective-permute-start(bf16[864,512]{1,0:T(8,128)(2,1)S(1)} %pad_maximum_fusion.3), channel_id=1, source_target_pairs={{0,16},{16,0},{1,17},{17,1},{2,18},{18,2},{3,19},{19,3},{4,20},{20... | collective-permute-start | bytes 2654216 | tf_op jit(solution)/shard_map/ppermute | solution.py:454
  61.1 54.9 %collective-permute-start.12 = (bf16[1152,384]{1,0:T(8,128)(2,1)S(1)}, bf16[1152,384]{1,0:T(8,128)(2,1)}, u32[]{:S(2)}, u32[]{:S(2)}) collective-permute-start(bf16[1152,384]{1,0:T(8,128)(2,1)S(1)} %pad_maximum_fusion.4), channel_id=1, source_target_pairs={{0,16},{16,0},{1,17},{17,1},{2,18},{18,2},{3,19},{19,3},{4,20},{20... | collective-permute-start | bytes 2654216 | tf_op jit(solution)/shard_map/ppermute | solution.py:454
  75.6 170.7 %reduce-scatter.6.cloned.1.call-start = ((), (), s32[]{:S(2)}) async-start(), calls=%async_computation.5 | async-start | bytes 2088960 | tf_op jit(solution)/shard_map/reduce_scatter | solution.py:673
  78.3 39.1 %collective-permute-start.5 = (bf16[864,512]{1,0:T(8,128)(2,1)S(1)}, bf16[864,512]{1,0:T(8,128)(2,1)S(1)}, u32[]{:S(2)}, u32[]{:S(2)}) collective-permute-start(bf16[864,512]{1,0:T(8,128)(2,1)S(1)} %collective-permute-done.4.g0), channel_id=1, source_target_pairs={{0,4},{4,0},{8,12},{12,8},{1,5},{5,1},{9,13},{13,9},{2,6},{6,2},{1... | collective-permute-start | bytes 2654216 | tf_op jit(solution)/shard_map/ppermute | solution.py:457
  78.3 39.6 %collective-permute-start.6 = (bf16[864,512]{1,0:T(8,128)(2,1)S(1)}, bf16[864,512]{1,0:T(8,128)(2,1)}, u32[]{:S(2)}, u32[]{:S(2)}) collective-permute-start(bf16[864,512]{1,0:T(8,128)(2,1)S(1)} %collective-permute-done.4.g0), channel_id=1, source_target_pairs={{0,8},{4,12},{8,0},{12,4},{1,9},{5,13},{9,1},{13,5},{2,10},{6,14},... | collective-permute-start | bytes 2654216 | tf_op jit(solution)/shard_map/ppermute | solution.py:457
  97.4 22.6 %collective-permute-start.10 = (bf16[864,512]{1,0:T(8,128)(2,1)}, bf16[864,512]{1,0:T(8,128)(2,1)S(1)}, u32[]{:S(2)}, u32[]{:S(2)}) collective-permute-start(bf16[864,512]{1,0:T(8,128)(2,1)} %collective-permute-done.8.u0), channel_id=1, source_target_pairs={{0,8},{4,12},{8,0},{12,4},{1,9},{5,13},{9,1},{13,5},{2,10},{6,14},... | collective-permute-start | bytes 2654216 | tf_op jit(solution)/shard_map/ppermute | solution.py:457
  117.4 28.9 %collective-permute-start.9 = (bf16[864,512]{1,0:T(8,128)(2,1)}, bf16[864,512]{1,0:T(8,128)(2,1)}, u32[]{:S(2)}, u32[]{:S(2)}) collective-permute-start(bf16[864,512]{1,0:T(8,128)(2,1)} %collective-permute-done.8.u0), channel_id=1, source_target_pairs={{0,4},{4,0},{8,12},{12,8},{1,5},{5,1},{9,13},{13,9},{2,6},{6,2},{1... | collective-permute-start | bytes 2654216 | tf_op jit(solution)/shard_map/ppermute | solution.py:457
  117.4 28.9 %collective-permute-start.13 = (bf16[1152,384]{1,0:T(8,128)(2,1)}, bf16[1152,384]{1,0:T(8,128)(2,1)}, u32[]{:S(2)}, u32[]{:S(2)}) collective-permute-start(bf16[1152,384]{1,0:T(8,128)(2,1)} %collective-permute-done.12.d0), channel_id=1, source_target_pairs={{0,4},{4,0},{8,12},{12,8},{1,5},{5,1},{9,13},{13,9},{2,6},{6,2},{1... | collective-permute-start | bytes 2654216 | tf_op jit(solution)/shard_map/ppermute | solution.py:457
  117.9 28.4 %collective-permute-start.7 = (bf16[864,512]{1,0:T(8,128)(2,1)}, bf16[864,512]{1,0:T(8,128)(2,1)}, u32[]{:S(2)}, u32[]{:S(2)}) collective-permute-start(bf16[864,512]{1,0:T(8,128)(2,1)} %collective-permute-done.6.g2), channel_id=1, source_target_pairs={{0,4},{4,0},{8,12},{12,8},{1,5},{5,1},{9,13},{13,9},{2,6},{6,2},{1... | collective-permute-start | bytes 2654216 | tf_op jit(solution)/shard_map/ppermute | solution.py:457
  119.9 26.4 %collective-permute-start.11 = (bf16[864,512]{1,0:T(8,128)(2,1)S(1)}, bf16[864,512]{1,0:T(8,128)(2,1)}, u32[]{:S(2)}, u32[]{:S(2)}) collective-permute-start(bf16[864,512]{1,0:T(8,128)(2,1)S(1)} %collective-permute-done.10.u2), channel_id=1, source_target_pairs={{0,4},{4,0},{8,12},{12,8},{1,5},{5,1},{9,13},{13,9},{2,6},{6,2},{1... | collective-permute-start | bytes 2654216 | tf_op jit(solution)/shard_map/ppermute | solution.py:457
  207.6 107.0 %all-gather.17.cloned.1.call-start = ((), (), s32[]{:S(2)}) async-start(), calls=%async_computation.10 | async-start | bytes 1966080 | tf_op jit(solution)/shard_map/all_gather | solution.py:704
  207.7 126.0 %collective-permute-start.27 = (bf16[4,9,288,512]{3,2,1,0:T(8,128)(2,1)}, bf16[4,9,288,512]{3,2,1,0:T(8,128)(2,1)}, u32[]{:S(2)}, u32[]{:S(2)}) collective-permute-start(bf16[4,9,288,512]{3,2,1,0:T(8,128)(2,1)} %get-tuple-element.80), channel_id=1, source_target_pairs={{0,4},{4,0},{8,12},{12,8},{1,5},{5,1},{9,13},{13,9},{2,6},{6,2},{1... | collective-permute-start | bytes 31850504 | tf_op jit(solution)/shard_map/ppermute | solution.py:457
  251.0 22.8 %all-to-all-start = ((bf16[4,128,384]{2,1,0:T(8,128)(2,1)}), bf16[4,128,384]{2,1,0:T(8,128)(2,1)S(1)}, u32[]{:S(2)}, u32[]{:S(2)}) async-start(bf16[4,128,384]{2,1,0:T(8,128)(2,1)} %get-tuple-element.63), calls=%async_computation.2 | async-start | bytes 786432 | tf_op jit(solution)/shard_map/all_to_all | solution.py:703
  254.5 74.0 %reduce-scatter.4.cloned.1.call-start = ((), (), s32[]{:S(2)}) async-start(), calls=%async_computation.4 | async-start | bytes 1966080 | tf_op jit(solution)/shard_map/reduce_scatter | solution.py:706
  255.0 110.5 %reduce-scatter.8.cloned.1.call-start = ((), (), s32[]{:S(2)}) async-start(), calls=%async_computation.6 | async-start | bytes 1966080 | tf_op jit(solution)/shard_map/reduce_scatter | solution.py:795
  326.4 77.3 %all-gather.15.cloned.1.call-start = ((), (), s32[]{:S(2)}) async-start(), calls=%async_computation.9 | async-start | bytes 1966080 | tf_op jit(solution)/shard_map/all_gather | solution.py:707
  330.3 113.1 %all-gather.19.cloned.1.call-start = ((), (), s32[]{:S(2)}) async-start(), calls=%async_computation.11 | async-start | bytes 1966080 | tf_op jit(solution)/shard_map/all_gather | solution.py:810
  342.5 83.9 %collective-permute-start.30 = (bf16[2,5,288,512]{3,2,1,0:T(8,128)(2,1)}, bf16[2,5,288,512]{3,2,1,0:T(8,128)(2,1)S(1)}, u32[]{:S(2)}, u32[]{:S(2)}) collective-permute-start(bf16[2,5,288,512]{3,2,1,0:T(8,128)(2,1)} %fusion), channel_id=1, source_target_pairs={{0,16},{16,0},{1,17},{17,1},{2,18},{18,2},{3,19},{19,3},{4,20},{20... | collective-permute-start | bytes 8847368 | tf_op jit(solution)/shard_map/ppermute | solution.py:454
  354.1 68.4 %collective-permute-start.28 = (bf16[2,4,288,512]{3,2,1,0:T(8,128)(2,1)}, bf16[2,4,288,512]{3,2,1,0:T(8,128)(2,1)}, u32[]{:S(2)}, u32[]{:S(2)}) collective-permute-start(bf16[2,4,288,512]{3,2,1,0:T(8,128)(2,1)} %fusion.3), channel_id=1, source_target_pairs={{0,8},{4,12},{8,0},{12,4},{1,9},{5,13},{9,1},{13,5},{2,10},{6,14},... | collective-permute-start | bytes 7077896 | tf_op jit(solution)/shard_map/ppermute | solution.py:457
  377.4 41.0 %collective-permute-start.25 = (bf16[2,1,96,896]{2,3,1,0:T(8,128)(2,1)}, bf16[2,1,96,896]{2,3,1,0:T(8,128)(2,1)}, u32[]{:S(2)}, u32[]{:S(2)}) collective-permute-start(bf16[2,1,96,896]{2,3,1,0:T(8,128)(2,1)} %fusion.8), channel_id=1, source_target_pairs={{0,8},{4,12},{8,0},{12,4},{1,9},{5,13},{9,1},{13,5},{2,10},{6,14},... | collective-permute-start | bytes 1032200 | tf_op jit(solution)/shard_map/ppermute | solution.py:457
  426.1 25.6 %collective-permute-start.29 = (bf16[4,288,512]{2,1,0:T(8,128)(2,1)}, bf16[4,288,512]{2,1,0:T(8,128)(2,1)}, u32[]{:S(2)}, u32[]{:S(2)}) collective-permute-start(bf16[4,288,512]{2,1,0:T(8,128)(2,1)} %fusion.4), channel_id=1, source_target_pairs={{0,16},{16,0},{1,17},{17,1},{2,18},{18,2},{3,19},{19,3},{4,20},{20... | collective-permute-start | bytes 3538952 | tf_op jit(solution)/shard_map/ppermute | solution.py:454
  430.0 31.8 %collective-permute-start.31 = (bf16[5,288,512]{2,1,0:T(8,128)(2,1)}, bf16[5,288,512]{2,1,0:T(8,128)(2,1)}, u32[]{:S(2)}, u32[]{:S(2)}) collective-permute-start(bf16[5,288,512]{2,1,0:T(8,128)(2,1)} %fusion.1), channel_id=1, source_target_pairs={{0,8},{4,12},{8,0},{12,4},{1,9},{5,13},{9,1},{13,5},{2,10},{6,14},... | collective-permute-start | bytes 4423688 | tf_op jit(solution)/shard_map/ppermute | solution.py:457
  (34 other events, 516.6 us)
Sparse Core Ops, SparseCore 0:
  16.5 42.2 all-gather.12
  75.7 37.4 all-gather.10
  207.7 38.5 reduce-scatter.5
  251.1 40.9 all-gather.16
  294.2 34.2 reduce-scatter.3
  331.2 34.2 reduce-scatter.7
  367.7 36.0 all-gather.14
  405.3 38.0 all-gather.18

commit v2 on v1

v2 whole, which is shorter than its diff:
```python
import functools
import math

import jax
import jax.numpy as jnp
from jax import lax
from jax.experimental import pallas as pl
from jax.experimental.pallas import tpu as pltpu
from jax.sharding import PartitionSpec as P

HD = 64
SLOTS = 80
EPS = 1e-06
F32 = jnp.float32
BF16 = jnp.bfloat16
VMEM_BYTES = 56 * 1024 * 1024


def mm(a, b):
    return lax.dot_general(a, b, (((1,), (0,)), ((), ())), preferred_element_type=F32)


def mm_nt(a, b):
    return lax.dot_general(a, b, (((1,), (1,)), ((), ())), preferred_element_type=F32)


def mm_tn(a, b):
    return lax.dot_general(a, b, (((0,), (0,)), ((), ())), preferred_element_type=F32)


def params(steps=1):
    return pltpu.CompilerParams(
        dimension_semantics=("arbitrary",) * steps, vmem_limit_bytes=VMEM_BYTES
    )


def rotation(width):
    row = lax.broadcasted_iota(jnp.int32, (width, width), 0)
    col = lax.broadcasted_iota(jnp.int32, (width, width), 1)
    first = (col % HD) < HD // 2
    minus = first & (row == col + HD // 2)
    plus = jnp.logical_not(first) & (row == col - HD // 2)
    return jnp.where(minus, -1.0, jnp.where(plus, 1.0, 0.0)).astype(BF16)


def row_scale(value):
    return lax.rsqrt(jnp.mean(value * value, -1, keepdims=True) + EPS)


def qkv_kernel(scal, x_ref, own_ref, oth_ref, cos_ref, sin_ref, n1_ref, q_ref, kv_ref, all_ref, w_ref, small_ref, swap):
    half = own_ref.shape[0]

    @pl.when(pl.program_id(0) == 0)
    def _():
        mine = pl.multiple_of(scal[0] * half, half)
        other = pl.multiple_of((1 - scal[0]) * half, half)
        w_ref[pl.ds(mine, half), :] = own_ref[...]
        w_ref[pl.ds(other, half), :] = oth_ref[...]
        swap[...] = mm(w_ref[...], rotation(w_ref.shape[1])).astype(BF16)
        turned = jnp.transpose(w_ref[:, 128:256].astype(F32))
        small_ref[...] = turned[64:80, :]

    x = x_ref[0].astype(F32)
    n1 = (x * row_scale(x) * small_ref[8:9, :]).astype(BF16)
    n1_ref[0] = n1
    turned = (mm(n1, w_ref[...]) * cos_ref[...] + mm(n1, swap[...]) * sin_ref[...]).astype(BF16)
    q_ref[0] = turned[:, :192]
    kv_ref[0] = turned[:, 256:640]
    all_ref[0] = turned


def visible(scal, prefix, keys, rows):
    key_pos = lax.broadcasted_iota(jnp.int32, (keys, rows), 0) ^ (scal[1] * rows)
    row_pos = lax.broadcasted_iota(jnp.int32, (keys, rows), 1) + scal[1] * rows
    return (key_pos <= row_pos) | (key_pos < prefix)


def only_head(rows, head):
    lane = lax.broadcasted_iota(jnp.int32, rows.shape, 1)
    return jnp.where((lane >= head * HD) & (lane < (head + 1) * HD), rows, jnp.zeros_like(rows))


def softmax(scores, seen):
    scores = jnp.where(seen, scores, -1e30)
    expo = jnp.exp(scores - jnp.max(scores, 0, keepdims=True))
    return expo * (1.0 / jnp.sum(expo, 0, keepdims=True))


def attn_fwd_kernel(scal, prefix, q_ref, kv0, kv1, kv2, kv3, o_ref):
    q = q_ref[0]
    rows, width = q.shape
    heads = width // HD
    kv = jnp.concatenate([kv0[0], kv1[0], kv2[0], kv3[0]], axis=0)
    k = kv[:, :width]
    value_t = jnp.transpose(kv[:, width:].astype(F32)).astype(BF16)
    seen = visible(scal, prefix[pl.program_id(0)], kv.shape[0], rows)
    outs = []
    for head in range(heads):
        probs = softmax(mm_nt(k, only_head(q, head) * (HD ** -0.5)), seen).astype(BF16)
        outs.append(mm(value_t[head * HD:(head + 1) * HD], probs))
    o = jnp.transpose(jnp.concatenate(outs, axis=0))
    o_ref[0] = jnp.concatenate([o[: rows // 2], o[rows // 2:]], axis=1).astype(BF16)


def fill_out_weights(scal, wo, wo_ref):
    pieces, _, width, half = wo_ref.shape
    for piece in range(pieces):
        for index, side in enumerate((scal[0], 1 - scal[0])):
            at = pl.ds(pl.multiple_of(side * half, half), half)
            wo[piece * width:(piece + 1) * width, at] = wo_ref[piece, index]


def post_kernel(scal, o_ref, wo_ref, x_ref, small_ref, routes_ref, n2_ref, h2_ref, gates_ref, slots_ref, wo):
    step = pl.program_id(0)
    width = wo_ref.shape[2]

    @pl.when(step == 0)
    def _():
        fill_out_weights(scal, wo, wo_ref)

    low = jnp.zeros((o_ref.shape[2], wo.shape[1]), F32)
    high = low
    for piece in range(o_ref.shape[0]):
        block = o_ref[piece, 0]
        weights = wo[piece * width:(piece + 1) * width, :]
        low += mm(block[:, :width], weights)
        high += mm(block[:, width:], weights)
    h2 = x_ref[0].astype(F32) + jnp.concatenate([low, high], axis=0)
    n2 = (h2 * row_scale(h2) * small_ref[9:10, :]).astype(BF16)
    n2_ref[0] = n2

    @pl.when(step == scal[2])
    def _():
        h2_ref[...] = h2

    expo = jnp.exp(mm_nt(small_ref[0:8, :].astype(BF16), n2))
    gates_ref[0] = expo / jnp.sum(expo, 0, keepdims=True)
    rows = n2.shape[0]
    expert = lax.broadcasted_iota(jnp.int32, (8, rows), 0)
    named = (routes_ref[0, 0:1, :] == expert) | (routes_ref[0, 1:2, :] == expert)
    before = lax.broadcasted_iota(jnp.int32, (rows, rows), 0) < lax.broadcasted_iota(jnp.int32, (rows, rows), 1)
    place = mm(named.astype(BF16), before.astype(BF16))
    slots_ref[0] = jnp.where(named, place.astype(jnp.int32), -1)


def silu_parts(value):
    sigma = 1.0 / (1.0 + jnp.exp(-value))
    return sigma, value * sigma


def split_blocks(core, value, blocks):
    rows = value.shape[0] // (2 * blocks)
    value = value.astype(BF16).reshape(blocks, 2, rows, value.shape[1])
    first = core == 0
    return jnp.where(first, value[:, 0], value[:, 1]), jnp.where(first, value[:, 1], value[:, 0])


def put_grads(core, keep_ref, send_ref, index, value):
    keep, send = split_blocks(core, value, keep_ref.shape[0])
    at = slice(index * keep.shape[1], (index + 1) * keep.shape[1])
    keep_ref[:, 0, at, :] = keep
    send_ref[:, 0, at, :] = send


def shared_kernel(
    scal, n2_ref, dy_ref, go_ref, uo_ref, do_ref, g0, g1, g2, g3, u0, u1, u2, u3, d0, d1, d2, d3,
    ys_ref, dn_ref, hid_ref, da_ref, db_ref, wg, wu, wd,
):
    step = pl.program_id(0)
    half = go_ref.shape[0]
    hidden = go_ref.shape[1]

    @pl.when(step == 0)
    def _():
        mine = pl.multiple_of(scal[0] * half, half)
        other = (1 - scal[0]) * half
        wg[pl.ds(mine, half), :] = go_ref[...]
        wu[pl.ds(mine, half), :] = uo_ref[...]
        wd[:, pl.ds(mine, half)] = do_ref[...]
        for piece, (g, u, d) in enumerate(((g0, u0, d0), (g1, u1, d1), (g2, u2, d2), (g3, u3, d3))):
            quarter = scal[3] ^ piece
            at = pl.multiple_of(other + quarter * (half // 4), half // 4)
            wg[pl.ds(at, half // 4), :] = g[...]
            wu[pl.ds(at, half // 4), :] = u[...]
            at = pl.multiple_of(quarter * (hidden // 4), hidden // 4)
            wd[pl.ds(at, hidden // 4), pl.ds(pl.multiple_of(other, half), half)] = d[...]

    n2 = n2_ref[0]
    dy = dy_ref[0]
    gate = mm(n2, wg[...])
    up = mm(n2, wu[...])
    sigma, silu = silu_parts(gate)
    hid = (silu * up).astype(BF16)
    ys_ref[0] = mm(hid, wd[...]).astype(BF16)
    back = mm_nt(dy, wd[...])
    da = (back * up * (sigma * (1.0 + gate * (1.0 - sigma)))).astype(BF16)
    db = (back * silu).astype(BF16)
    dn_ref[0] = (mm_nt(da, wg[...]) + mm_nt(db, wu[...])).astype(BF16)
    hid_ref[0] = hid
    da_ref[0] = da
    db_ref[0] = db


def shared_grads_kernel(scal, n2_ref, dy_ref, hid_ref, da_ref, db_ref, keep_ref, send_ref):
    n2, dy, hid, da, db = [
        ref[...].reshape(-1, ref.shape[-1]) for ref in (n2_ref, dy_ref, hid_ref, da_ref, db_ref)
    ]
    put_grads(scal[4], keep_ref, send_ref, 0, mm_tn(n2, da))
    put_grads(scal[4], keep_ref, send_ref, 1, mm_tn(n2, db))
    put_grads(scal[4], keep_ref, send_ref, 2, mm_tn(dy, hid))


def moe_kernel(
    scal, n2_ref, dy_ref, slots_ref, gates_ref, ys_ref, dn_in_ref, go_ref, uo_ref, do_ref,
    g0, g1, g2, g3, u0, u1, u2, u3, v0, v1, v2, v3, d0, d1, d2, d3,
    y_ref, dn_ref, keep_ref, send_ref, wg, wu, wd, pick_s, ye_s, dx_s, xe_s, dy_s, de_s, gs_s, dprob_s,
):
    step = pl.program_id(0)
    seqs, rows, width = n2_ref.shape
    half = go_ref.shape[1]
    experts = slots_ref.shape[1]

    @pl.when(step < experts)
    def _():
        piece = step // 2
        expert = 2 * (piece ^ scal[3]) + step % 2
        mine = pl.multiple_of(scal[0] * half, half)
        other = pl.multiple_of((1 - scal[0]) * half, half)
        wg[pl.ds(mine, half), :] = go_ref[0]
        wu[pl.ds(mine, half), :] = uo_ref[0]
        wd[:, pl.ds(mine, half)] = do_ref[0]
        arrived = ((g0, u0, v0, d0), (g1, u1, v1, d1), (g2, u2, v2, d2), (g3, u3, v3, d3))
        for index, (g, u, v, d) in enumerate(arrived):
            @pl.when(piece == index)
            def _(g=g, d=d):
                wg[pl.ds(other, half), :] = g[...]
                wd[:, pl.ds(other, half)] = d[...]

            for odd, ref in enumerate((u, v)):
                @pl.when((piece == index) & (step % 2 == odd))
                def _(ref=ref):
                    wu[pl.ds(other, half), :] = ref[...]

        slot_at = pl.ds(pl.multiple_of(step * SLOTS, 16), SLOTS)
        slot = lax.broadcasted_iota(jnp.int32, (SLOTS, rows), 0)
        for s in range(seqs):
            at = slice(s * SLOTS, (s + 1) * SLOTS)
            hit = slots_ref[s, pl.ds(expert, 1), :] == slot
            gate_slot = jnp.sum(jnp.where(hit, gates_ref[s, pl.ds(expert, 1), :], 0.0), 1, keepdims=True)
            pick = hit.astype(BF16)
            pick_s[s, slot_at, :] = pick
            xe_s[at, :] = mm(pick, n2_ref[s]).astype(BF16)
            upstream = mm(pick, dy_ref[s])
            dy_s[at, :] = upstream.astype(BF16)
            de_s[at, :] = (gate_slot * upstream).astype(BF16)
            gs_s[at, :] = jnp.broadcast_to(gate_slot, (SLOTS, 128))

        xe = xe_s[...]
        gate = mm(xe, wg[...])
        up = mm(xe, wu[...])
        sigma, silu = silu_parts(gate)
        hid = (silu * up).astype(BF16)
        ye = mm(hid, wd[...])
        dots = jnp.sum(ye * dy_s[...].astype(F32), 1, keepdims=True)
        ye = (ye * gs_s[:, 0:1]).astype(BF16)
        for s in range(seqs):
            at = slice(s * SLOTS, (s + 1) * SLOTS)
            ye_s[s, slot_at, :] = ye[at]
            hit = slots_ref[s, pl.ds(expert, 1), :] == slot
            dprob_s[s, pl.ds(expert, 1), :] = jnp.sum(jnp.where(hit, dots[at], 0.0), 0, keepdims=True)
        back = mm_nt(de_s[...], wd[...])
        da = (back * up * (sigma * (1.0 + gate * (1.0 - sigma)))).astype(BF16)
        db = (back * silu).astype(BF16)
        dx = (mm_nt(da, wg[...]) + mm_nt(db, wu[...])).astype(BF16)
        for s in range(seqs):
            dx_s[s, slot_at, :] = dx[s * SLOTS:(s + 1) * SLOTS]
        put_grads(scal[4], keep_ref, send_ref, 0, mm_tn(xe_s[...], da))
        put_grads(scal[4], keep_ref, send_ref, 1, mm_tn(xe_s[...], db))
        put_grads(scal[4], keep_ref, send_ref, 2, mm_tn(de_s[...], hid))

    @pl.when(step >= experts)
    def _():
        s = step - experts
        pick = pick_s[s]
        y_ref[0] = (ys_ref[0].astype(F32) + mm_tn(pick, ye_s[s])).astype(BF16)
        dn_ref[0, 0:rows, :] = (dn_in_ref[0].astype(F32) + mm_tn(pick, dx_s[s])).astype(BF16)
        tail = jnp.concatenate([dprob_s[s], jnp.zeros((dn_ref.shape[1] - rows - experts, rows), F32)], axis=0)
        tail = jnp.concatenate([tail, jnp.zeros((tail.shape[0], width - rows), F32)], axis=1)
        dn_ref[0, rows:, :] = tail.astype(BF16)


def norm_back(grad_out, value, scale, gain):
    weighted = grad_out * gain
    return scale * weighted - value * (scale * scale * scale) * jnp.mean(weighted * value, -1, keepdims=True)


def mid_kernel(scal, dn_ref, gates_ref, h2_ref, n2_ref, dy_ref, small_ref, wo_ref, dh2_ref, do_ref, low_ref, sums_ref, wo):
    rows = h2_ref.shape[0]
    pieces, _, width, _ = wo_ref.shape
    fill_out_weights(scal, wo, wo_ref)
    parts = dn_ref[0].astype(F32)
    gates = gates_ref[0]
    dprob = parts[rows:rows + 8, 0:rows]
    dlogits = (gates * (dprob - jnp.sum(dprob * gates, 0, keepdims=True))).astype(BF16)
    dn2 = parts[0:rows, :] + mm_tn(dlogits, small_ref[0:8, :].astype(BF16))
    h2 = h2_ref[...]
    scale = row_scale(h2)
    sums_ref[0:8, :] = mm(dlogits, n2_ref[0])
    sums_ref[8:16, :] = jnp.zeros((8, h2.shape[1]), F32)
    sums_ref[9:10, :] = jnp.sum(dn2 * h2 * scale, 0, keepdims=True)
    dh2 = dy_ref[0].astype(F32) + norm_back(dn2, h2, scale, small_ref[9:10, :])
    dh2_ref[...] = dh2
    low = dh2.astype(BF16)
    low_ref[...] = low
    for piece in range(pieces):
        do = mm_nt(low, wo[piece * width:(piece + 1) * width, :])
        do_ref[piece] = jnp.concatenate([do[: rows // 2], do[rows // 2:]], axis=1).astype(BF16)


def attn_bwd_kernel(
    scal, prefix, q_ref, kv0, kv1, kv2, kv3, do_ref, cos_ref, sin_ref, dq_ref, e0, e1, e2, e3
):
    rows, width = dq_ref.shape[1:]
    q = q_ref[0][:, :width]
    heads = width // HD
    kv = jnp.concatenate([kv0[0], kv1[0], kv2[0], kv3[0]], axis=0)
    k = kv[:, :width]
    v = kv[:, width:]
    key_t = jnp.transpose(k.astype(F32)).astype(BF16)
    do = jnp.concatenate([do_ref[0][:, :width], do_ref[0][:, width:]], axis=0)
    seen = visible(scal, prefix[scal[2]], kv.shape[0], rows)
    cosine, sine = cos_ref[...], sin_ref[...]
    turned, ds_all, probs_all, q_all, do_all = [], [], [], [], []
    for head in range(heads):
        q_head = only_head(q, head) * (HD ** -0.5)
        do_head = only_head(do, head)
        probs = softmax(mm_nt(k, q_head), seen)
        dp = mm_nt(v, do_head)
        ds = (probs * (dp - jnp.sum(dp * probs, 0, keepdims=True))).astype(BF16)
        dq = mm(key_t[head * HD:(head + 1) * HD], ds) * (HD ** -0.5)
        first, second = dq[: HD // 2], dq[HD // 2:]
        turned += [first * cosine + second * sine, second * cosine - first * sine]
        ds_all.append(ds)
        probs_all.append(probs.astype(BF16))
        q_all.append(q_head)
        do_all.append(do_head)
    dq_ref[0] = jnp.transpose(jnp.concatenate(turned, axis=0)).astype(BF16)
    dk = mm(jnp.concatenate(ds_all, axis=1), jnp.concatenate(q_all, axis=0))
    dv = mm(jnp.concatenate(probs_all, axis=1), jnp.concatenate(do_all, axis=0))
    dkv = jnp.concatenate([dk, dv], axis=1).astype(BF16)
    for piece, out in enumerate((e0, e1, e2, e3)):
        out[0] = dkv[piece * rows:(piece + 1) * rows]


def swing_kernel(a_ref, b_ref, c_ref, cos_ref, sin_ref, out_ref):
    dkv = a_ref[0].astype(F32) + b_ref[0].astype(F32) + c_ref[0].astype(F32)
    swung = dkv * sin_ref[:, 256:]
    high = swung.astype(BF16)
    low = (swung - high.astype(F32)).astype(BF16)
    turn = rotation(dkv.shape[1])
    out_ref[0] = (dkv * cos_ref[:, 256:] + mm_nt(high, turn) + mm_nt(low, turn)).astype(BF16)


def end_kernel(scal, dq_ref, dkv_ref, w0, w1, w2, w3, dh2_ref, x_ref, small_ref, sums_in, gi_ref, sums_ref, w, total):
    step = pl.program_id(0)
    quarter = w0.shape[1]
    head_cols = dq_ref.shape[2]
    for piece, ref in enumerate((w0, w1, w2, w3)):
        at = pl.multiple_of((scal[1] ^ piece) * quarter, quarter)
        w[pl.ds(at, quarter), :] = ref[0]
    part = mm_nt(dq_ref[0], w[:, :head_cols]) + mm_nt(dkv_ref[0], w[:, 256:])

    @pl.when(step == 0)
    def _():
        total[...] = part

    @pl.when(step > 0)
    def _():
        total[...] += part

    @pl.when(step == pl.num_programs(0) - 1)
    def _():
        x = x_ref[0].astype(F32)
        dn1 = total[...]
        scale = row_scale(x)
        sums_ref[...] = sums_in[...]
        sums_ref[8:9, :] = jnp.sum(dn1 * x * scale, 0, keepdims=True)
        gi_ref[...] = (dh2_ref[...] + norm_back(dn1, x, scale, small_ref[8:9, :])).astype(BF16)


def first_grads_kernel(scal, n1_ref, dq_ref, low_ref, o_ref, keep_ref, send_ref):
    head_cols = dq_ref.shape[2]
    block = o_ref[0, 0]
    o = jnp.concatenate([block[:, :head_cols], block[:, head_cols:]], axis=0)
    grads = jnp.concatenate([mm_tn(n1_ref[0], dq_ref[0]), mm_tn(low_ref[...], o)], axis=1)
    keep_ref[:, 0], send_ref[:, 0] = split_blocks(scal[4], grads, keep_ref.shape[0])


def second_grads_kernel(scal, n1_ref, dkv_ref, sums_ref, keep_ref, send_ref):
    step = pl.program_id(0)
    last = pl.num_programs(0) - 1

    @pl.when(step < last)
    def _():
        keep_ref[:, 0], send_ref[:, 0] = split_blocks(scal[4], mm_tn(n1_ref[0], dkv_ref[0]), keep_ref.shape[0])

    @pl.when(step == last)
    def _():
        sums = sums_ref[...]
        sums = jnp.concatenate([sums, jnp.zeros((keep_ref.shape[3] - sums.shape[0], sums.shape[1]), F32)], axis=0)
        keep_ref[:, 0], send_ref[:, 0] = split_blocks(scal[4], jnp.transpose(sums), keep_ref.shape[0])


def whole(shape):
    return pl.BlockSpec(shape, lambda *_: (0,) * len(shape))


def by_step(shape):
    return pl.BlockSpec((1,) + shape, lambda i, *_: (i,) + (0,) * len(shape))


def call(kernel, grid, in_specs, out_specs, out_shape, scratch=(), prefetch=1, aliases=None):
    return pl.pallas_call(
        kernel,
        grid_spec=pltpu.PrefetchScalarGridSpec(
            num_scalar_prefetch=prefetch,
            grid=grid,
            in_specs=in_specs,
            out_specs=out_specs,
            scratch_shapes=scratch,
        ),
        out_shape=out_shape,
        input_output_aliases=aliases or {},
        compiler_params=params(len(grid)),
        cost_estimate=pl.CostEstimate(flops=1, bytes_accessed=1, transcendentals=0),
    )


def fence(values, *others):
    values = list(values)
    return list(lax.optimization_barrier((*values, *others))[: len(values)])


def shape_of(shape, dtype=BF16):
    return jax.ShapeDtypeStruct(shape, dtype)


def body(
    fsdp_size,
    layer_input,
    gain_attn,
    query_weight,
    key_weight,
    value_weight,
    output_weight,
    gain_ffn,
    router,
    exp_gate,
    exp_up,
    exp_down,
    shared_gate_weight,
    shared_up_weight,
    shared_down_weight,
    routes,
    prefix,
    cotangent,
):
    seqs, rows, width = layer_input.shape
    experts = exp_gate.shape[0]
    hidden = exp_gate.shape[2]
    head_cols = query_weight.shape[1]
    half = width // 2
    paired = fsdp_size == 2
    ctx = lax.axis_index("ctx")
    tp = lax.axis_index("tp")
    ctx_size = lax.axis_size("ctx")
    tp_size = lax.axis_size("tp")
    side = lax.axis_index("fsdp") if paired else jnp.int32(0)
    weight_ctx = ctx if paired else jnp.int32(0)
    blocks = fsdp_size * ctx_size
    direct = paired and ctx_size == 4 and tp_size == 4
    core = ctx % 2 if direct else jnp.int32(0)
    scal = jnp.stack([side, ctx, tp, weight_ctx, core]).astype(jnp.int32)

    def over_x(value):
        return lax.ppermute(value, "fsdp", [(0, 1), (1, 0)])

    def over_tp(value, bit):
        return lax.ppermute(value, "tp", [(i, i ^ bit) for i in range(tp_size)])

    def over_ctx(value, bit):
        return lax.ppermute(value, "ctx", [(i, i ^ bit) for i in range(ctx_size)])

    columns = jnp.concatenate(
        [
            query_weight,
            router,
            gain_attn[:, None],
            gain_ffn[:, None],
            jnp.zeros((query_weight.shape[0], 54), BF16),
            key_weight,
            value_weight,
        ],
        axis=1,
    )
    if paired:
        columns_own, columns_other = columns, over_x(columns)
    else:
        columns = lax.all_gather(columns, "fsdp", axis=0, tiled=True)
        columns_own, columns_other = columns[:half], columns[half:]

    shared_own = (shared_gate_weight, shared_up_weight, shared_down_weight)
    experts_own = (exp_gate, exp_up, exp_down)
    if paired:

        def quarter(value, parts):
            size = value.shape[0] // parts
            return lax.dynamic_slice_in_dim(value, size * ctx, size, 0).reshape(-1, value.shape[-1])

        gate, up, down = [quarter(stack, 4) for stack in experts_own]
        shared_gate, shared_up, shared_down = [quarter(stack, 4) for stack in shared_own]
        wide = jnp.concatenate([gate, up[:half], shared_gate, shared_up], axis=0)
        rest = up[half:]
        down = jnp.concatenate([down, shared_down], axis=0)
        own = experts_own + shared_own
    else:
        gate_all = lax.all_gather(exp_gate, "fsdp", axis=1, tiled=True)
        up_all = lax.all_gather(exp_up, "fsdp", axis=1, tiled=True)
        down_all = lax.all_gather(exp_down, "fsdp", axis=2, tiled=True)
        sg_all = lax.all_gather(shared_gate_weight, "fsdp", axis=0, tiled=True)
        su_all = lax.all_gather(shared_up_weight, "fsdp", axis=0, tiled=True)
        sd_all = lax.all_gather(shared_down_weight, "fsdp", axis=1, tiled=True)
        own = (gate_all[:, :half], up_all[:, :half], down_all[:, :, :half], sg_all[:half], su_all[:half], sd_all[:, :half])

        def split(value):
            return value.reshape((4, value.shape[0] // 4) + value.shape[1:])

        gate_all, up_all, sg_all, su_all = [
            split(value) for value in (gate_all[:, half:], up_all[:, half:], sg_all[half:], su_all[half:])
        ]
        down_all, sd_all = split(down_all[:, :, half:]), split(sd_all[:, half:])
        wide_p = [
            jnp.concatenate([gate_all[p, 0], gate_all[p, 1], up_all[p, 0], sg_all[p], su_all[p]], axis=0) for p in range(4)
        ]
        rest_p = [up_all[p, 1] for p in range(4)]
        down_p = [jnp.concatenate([down_all[p, 0], down_all[p, 1], sd_all[p]], axis=0) for p in range(4)]

    if paired:
        out_pieces = [output_weight, over_x(fence([output_weight], columns)[0])]
    else:
        out_pieces = lax.all_gather(output_weight, "fsdp", axis=1, tiled=True)
        out_pieces = [out_pieces[:, :half], out_pieces[:, half:]]

    positions = (ctx * rows + jnp.arange(rows, dtype=jnp.int32)).astype(F32)
    inverse = jnp.exp(jnp.arange(HD // 2, dtype=F32) * (-math.log(10000.0) / (HD // 2)))
    angles = positions[:, None] * inverse[None, :]
    cosine, sine = jnp.cos(angles), jnp.sin(angles)
    heads = head_cols // HD

    def table(value, rest):
        turned = jnp.tile(value, (1, 2 * heads))
        plain = jnp.full((rows, head_cols), rest, F32)
        return jnp.concatenate([turned, plain[:, :64], turned, plain], axis=1)

    cos_table, sin_table = table(cosine, 1.0), table(sine, 0.0)
    routes_t = jnp.pad(jnp.transpose(routes, (0, 2, 1)), ((0, 0), (0, 6), (0, 0)))

    columns_other, cos_table, sin_table = fence([columns_other, cos_table, sin_table], routes_t)
    if paired:
        out_own, out_other = out_pieces
        columns_other, out_other, cos_table, wide, rest, down = fence(
            [columns_other, out_other, cos_table, wide, rest, down]
        )
        out_pieces = [out_own, out_other]
        wide_0 = over_x(wide)
    out_pieces = lax.all_gather(jnp.stack(out_pieces), "tp", axis=0)
    packed = cos_table.shape[1]

    n1, q, kv, qkv, w_qkv, small = call(
        qkv_kernel,
        (seqs,),
        [
            by_step((rows, width)),
            whole((half, packed)),
            whole((half, packed)),
            whole((rows, packed)),
            whole((rows, packed)),
        ],
        [
            by_step((rows, width)),
            by_step((rows, head_cols)),
            by_step((rows, 2 * head_cols)),
            by_step((rows, packed)),
            whole((width, packed)),
            whole((16, width)),
        ],
        [
            shape_of((seqs, rows, width)),
            shape_of((seqs, rows, head_cols)),
            shape_of((seqs, rows, 2 * head_cols)),
            shape_of((seqs, rows, packed)),
            shape_of((width, packed)),
            shape_of((16, width), F32),
        ],
        [pltpu.VMEM((width, packed), BF16)],
    )(scal, layer_input, columns_own, columns_other, cos_table, sin_table)

    kv_0 = kv
    kv_2 = over_ctx(kv_0, 2)
    kv_1 = over_ctx(kv_0, 1)
    q_now, kv_2 = fence([q, kv_2], kv_1)
    w_part = lax.dynamic_slice_in_dim(w_qkv, (width // 4) * ctx, width // 4, 0)
    w_part = jnp.pad(w_part, ((0, 16), (0, 0)))
    if paired:
        kv_2, wide_0, rest, down, w_part = fence([kv_2, wide_0, rest, down, w_part])
        wide_2 = over_ctx(wide_0, 2)
        down_0, rest_0 = over_x(down), over_x(rest)
    kv_3 = over_ctx(kv_2, 1)
    q_now, kv_3, out_pieces = fence([q_now, kv_3, out_pieces])

    o = call(
        attn_fwd_kernel,
        (seqs,),
        [by_step((rows, head_cols))] + [by_step((rows, 2 * head_cols))] * 4,
        by_step((rows // 2, 2 * head_cols)),
        shape_of((seqs, rows // 2, 2 * head_cols)),
        prefetch=2,
    )(scal, prefix, q_now, kv_0, kv_1, kv_2, kv_3)

    o_all = lax.all_gather(o, "tp", axis=0)
    if paired:
        wide_0, rest_0, down_0, wide_2 = fence([wide_0, rest_0, down_0, wide_2], o)
        down_2, rest_2, wide_1, wide_3 = over_ctx(down_0, 2), over_ctx(rest_0, 2), over_ctx(wide_0, 1), over_ctx(wide_2, 1)
        o_all, wide_1, wide_3 = fence([o_all, wide_1, wide_3])
        down_1, rest_1 = over_ctx(down_0, 1), over_ctx(rest_0, 1)
    w_0 = lax.all_gather(fence([w_part], o_all)[0], "tp", axis=0)
    n2, h2, gates, slots = call(
        post_kernel,
        (seqs,),
        [
            pl.BlockSpec((tp_size, 1, rows // 2, 2 * head_cols), lambda i, *_: (0, i, 0, 0)),
            whole((tp_size, 2, head_cols, half)),
            by_step((rows, width)),
            whole((16, width)),
            by_step((8, rows)),
        ],
        [by_step((rows, width)), whole((rows, width)), by_step((8, rows)), by_step((8, rows))],
        [
            shape_of((seqs, rows, width)),
            shape_of((rows, width), F32),
            shape_of((seqs, 8, rows), F32),
            shape_of((seqs, 8, rows), jnp.int32),
        ],
        [pltpu.VMEM((width, width), BF16)],
    )(scal, o_all, out_pieces, layer_input, small, routes_t)

    if paired:
        down_2, rest_2, n2 = fence([down_2, rest_2, n2])
        down_3, rest_3 = over_ctx(down_2, 1), over_ctx(rest_2, 1)
        wide_p = (wide_0, wide_1, wide_2, wide_3)
        rest_p = (rest_0, rest_1, rest_2, rest_3)
        down_p = (down_0, down_1, down_2, down_3)

    full = pl.BlockSpec((seqs, rows, width), lambda *_: (0, 0, 0), pipeline_mode=pl.Buffered(1))
    part_rows = 3 * (width // 8)
    upper = [pl.BlockSpec((half // 4, hidden), lambda *_, at=at: (at, 0)) for at in (12, 13)]
    lower = pl.BlockSpec((hidden // 4, half), lambda *_: (8, 0))
    weights = [pltpu.VMEM((width, hidden), BF16)] * 2 + [pltpu.VMEM((hidden, width), BF16)]
    hidden_shape = shape_of((seqs, rows, hidden))
    ys, dn_shared, *shared_hidden = call(
        shared_kernel,
        (seqs,),
        [by_step((rows, width))] * 2
        + [whole((half, hidden)), whole((half, hidden)), whole((hidden, half))]
        + [upper[0]] * 4
        + [upper[1]] * 4
        + [lower] * 4,
        [by_step((rows, width))] * 2 + [by_step((rows, hidden))] * 3,
        [shape_of((seqs, rows, width))] * 2 + [hidden_shape] * 3,
        weights,
    )(scal, n2, cotangent, *own[3:], *wide_p, *wide_p, *down_p)

    qkv_late, w_0, ys = fence([qkv, w_0, ys])
    qkv_seq = lax.all_to_all(qkv_late, "tp", 0, 0, tiled=True)
    w_2, w_1 = over_ctx(w_0, 2), over_ctx(w_0, 1)

    def expert_of(i, scal):
        i = jnp.minimum(i, experts - 1)
        return 2 * ((i // 2) ^ scal[3]) + i % 2

    def of_expert(shape):
        return pl.BlockSpec((1,) + shape, lambda i, scal: (expert_of(i, scal), 0, 0))

    def piece_specs(shape):
        return [
            pl.BlockSpec(shape, lambda i, scal, p=p: (jnp.clip(i - 2 * p, 0, 1), 0)) for p in range(4)
        ]

    late = pl.BlockSpec((1, rows, width), lambda i, scal: (jnp.maximum(i - experts, 0), 0, 0))

    dn_rows = rows + 16
    slot_rows = seqs * SLOTS
    block = (4, 1, part_rows, hidden)

    expert_grads = pl.BlockSpec(block, lambda i, scal: (0, expert_of(i, scal), 0, 0))
    y, dn, *expert_group = call(
        moe_kernel,
        (experts + seqs,),
        [full, full, whole((seqs, 8, rows)), whole((seqs, 8, rows)), late, late]
        + [of_expert((half, hidden)), of_expert((half, hidden)), of_expert((hidden, half))]
        + piece_specs((half, hidden))
        + [pl.BlockSpec((half, hidden), lambda *_: (2, 0))] * 4
        + [pl.BlockSpec((half, hidden), lambda *_: (0, 0))] * 4
        + piece_specs((hidden, half)),
        [late, pl.BlockSpec((1, dn_rows, width), lambda i, *_: (jnp.maximum(i - experts, 0), 0, 0))]
        + [expert_grads] * 2,
        [shape_of((seqs, rows, width)), shape_of((seqs, dn_rows, width))]
        + [shape_of((4, experts, part_rows, hidden))] * 2,
        weights
        + [pltpu.VMEM((seqs, experts * SLOTS, rows), BF16)]
        + [pltpu.VMEM((seqs, experts * SLOTS, width), BF16)] * 2
        + [pltpu.VMEM((slot_rows, width), BF16)] * 3
        + [pltpu.VMEM((slot_rows, 128), F32), pltpu.VMEM((seqs, 8, rows), F32)],
    )(scal, n2, cotangent, slots, gates, ys, dn_shared, *own[:3], *wide_p, *wide_p, *rest_p, *down_p)

    dn, qkv_seq, w_2, w_1, n2_late, *expert_group = fence([dn, qkv_seq, w_2, w_1, n2, *expert_group])
    w_pieces = (w_0, w_1, w_2, over_ctx(w_2, 1))
    dn_own = lax.psum_scatter(dn, "tp", scatter_dimension=0, tiled=True)
    kv_seq = qkv_seq[:, :, 256:]
    kv_seq_2, kv_seq_1 = over_ctx(kv_seq, 2), over_ctx(kv_seq, 1)

    shared_group = call(
        shared_grads_kernel,
        (1,),
        [full] * 2 + [whole((seqs, rows, hidden))] * 3,
        [whole(block)] * 2,
        [shape_of(block)] * 2,
    )(scal, n2_late, cotangent, *shared_hidden)

    part = width // blocks
    along_x, along_y = side, ctx // 2

    def pick(value, x, y, first, count):
        value = value.reshape((2, 2) + value.shape[1:])
        sizes = (2 if x is None else 1, 2 if y is None else 1, count) + value.shape[3:]
        begin = (0 if x is None else x, 0 if y is None else y, first, 0, 0)
        value = lax.dynamic_slice(value, begin, sizes)
        value = value.reshape(tuple(n for n, at in zip(sizes[:2], (x, y)) if at is None) + sizes[2:])
        return value.astype(F32)

    def indexed(value, index):
        return lax.dynamic_index_in_dim(value, index, 0, False).astype(F32)

    class Sum:
        def __init__(self, keep, got, y_first, first=0, count=None):
            self.keep, self.got, self.y_first = keep, got, y_first
            self.range = (first, count or keep.shape[1])

        def fence(self, *others):
            (self.got,) = fence([self.got], *others)

        def both(self, x, y):
            return pick(self.keep, x, y, *self.range) + pick(self.got, x, y, *self.range)

        def first(self):
            if self.y_first:
                self.sent = self.both(None, 1 - along_y).astype(BF16)
            else:
                self.sent = self.both(1 - along_x, None).astype(BF16)
            self.far = over_ctx(self.sent, 2) if self.y_first else over_x(self.sent)
            return self.sent

        def second(self):
            if self.y_first:
                self.away = (self.both(1 - along_x, along_y) + indexed(self.far, 1 - along_x)).astype(BF16)
                self.last = over_x(self.away)
            else:
                self.away = (self.both(along_x, 1 - along_y) + indexed(self.far, 1 - along_y)).astype(BF16)
                self.last = over_ctx(self.away, 2)
            return self.away

        def result(self):
            mine = indexed(self.far, along_x if self.y_first else along_y)
            return self.both(along_x, along_y) + mine + self.last.astype(F32)

    def scatter_plain(keep, send):
        count, cols = keep.shape[1], keep.shape[3]
        triples = keep.shape[2] // (width // 8)
        both = jnp.stack([keep, send], axis=1).reshape(8, count, triples, width // 8, cols)
        both = jnp.transpose(both, (0, 3, 1, 2, 4)).reshape(blocks, part, count * triples, cols)
        both = jnp.transpose(both, (0, 2, 1, 3)).reshape(blocks, count * triples * part, cols)
        both = lax.psum_scatter(both, ("fsdp", "ctx"), scatter_dimension=0, tiled=True)
        return both.reshape(count, triples * part, cols).astype(F32)

    if direct:
        got, shared_got = over_ctx(expert_group[1], 1), over_ctx(shared_group[1], 1)
        cuts = ((0, 2, True), (2, 2, False), (4, 4, False))
        sums_of = [Sum(expert_group[0], got, y_first, first, count) for first, count, y_first in cuts]
        sums_of.append(Sum(shared_group[0], shared_got, True))
        sent = [sums_of[1].first(), sums_of[0].first()]
        sums_of[2].fence(*sent)
        sent.append(sums_of[2].first())
        sums_of[3].fence(*sent)
        sent.append(sums_of[3].first())
        (kv_seq_2,) = fence([kv_seq_2], *sent)
    kv_seq_3 = over_ctx(kv_seq_2, 1)
    kv_seqs = (kv_seq, kv_seq_1, kv_seq_2, kv_seq_3)
    (dn_own,) = fence([dn_own], kv_seq_1, kv_seq_3)
    (y_late,) = fence([y], dn_own)
    y_own = lax.psum_scatter(y_late, "tp", scatter_dimension=0, tiled=True)

    mine = pl.BlockSpec((1, rows, width), lambda i, scal: (scal[2], 0, 0))
    dh2, do, dh2_low, sums = call(
        mid_kernel,
        (1,),
        [
            whole((1, dn_rows, width)),
            pl.BlockSpec((1, 8, rows), lambda i, scal: (scal[2], 0, 0)),
            whole((rows, width)),
            mine,
            mine,
            whole((16, width)),
            whole((tp_size, 2, head_cols, half)),
        ],
        [
            whole((rows, width)),
            whole((tp_size, rows // 2, 2 * head_cols)),
            whole((rows, width)),
            whole((16, width)),
        ],
        [
            shape_of((rows, width), F32),
            shape_of((tp_size, rows // 2, 2 * head_cols)),
            shape_of((rows, width)),
            shape_of((16, width), F32),
        ],
        [pltpu.VMEM((width, width), BF16)],
    )(scal, dn_own, gates, h2, n2, cotangent, small, out_pieces)

    cos_t, sin_t = jnp.transpose(cosine), jnp.transpose(sine)
    kv_block = by_step((rows, 2 * head_cols))
    kv_shape = shape_of((tp_size, rows, 2 * head_cols))
    dq, e0, e1, e2, e3 = call(
        attn_bwd_kernel,
        (tp_size,),
        [by_step((rows, packed))]
        + [kv_block] * 4
        + [by_step((rows // 2, 2 * head_cols)), whole((HD // 2, rows)), whole((HD // 2, rows))],
        [by_step((rows, head_cols))] + [kv_block] * 4,
        [shape_of((tp_size, rows, head_cols))] + [kv_shape] * 4,
        prefetch=2,
    )(scal, prefix, qkv_seq, *kv_seqs, do, cos_t, sin_t)
    if direct:
        early = [sums_of[index] for index in (1, 0)]
        flat = fence([total.far for total in early] + [e1, e3])
        for total, value in zip(early, flat):
            total.far = value
        e1, e3 = flat[2:]
    from_core_1 = over_ctx(e1, 1)
    from_core_3 = over_ctx(e3, 1)
    far = (e2.astype(F32) + from_core_3.astype(F32)).astype(BF16)
    dq, far, dh2_low = fence([dq, far, dh2_low], from_core_1)
    from_y = over_ctx(far, 2)
    if direct:
        away = [total.second() for total in early]
        (dh2_low,) = fence([dh2_low], *away)

    pair_out = pl.BlockSpec((4, 1, width // 8, 2 * head_cols), lambda i, *_: (0, i, 0, 0))
    pair_shape = shape_of((4, tp_size, width // 8, 2 * head_cols))
    first_grads = call(
        first_grads_kernel,
        (tp_size,),
        [
            mine,
            by_step((rows, head_cols)),
            whole((rows, width)),
            pl.BlockSpec((1, 1, rows // 2, 2 * head_cols), lambda i, scal: (i, scal[2], 0, 0)),
        ],
        [pair_out] * 2,
        [pair_shape] * 2,
    )(scal, n1, dq, dh2_low, o_all)

    if direct:
        sum_qo = Sum(first_grads[0], over_ctx(first_grads[1], 1), True)
        (from_y,) = fence([from_y], sum_qo.first())
    dkv = call(
        swing_kernel,
        (tp_size,),
        [kv_block] * 3 + [whole((rows, packed))] * 2,
        kv_block,
        kv_shape,
        prefetch=0,
    )(e0, from_core_1, from_y, cos_table, sin_table)

    def by_group(shape):
        return pl.BlockSpec((1,) + shape, lambda i, *_: (i, 0, 0))

    gi, sums = call(
        end_kernel,
        (tp_size,),
        [by_group((rows, head_cols)), by_group((rows, 2 * head_cols))]
        + [by_group((width // 4, packed))] * 4
        + [whole((rows, width)), mine, whole((16, width)), whole((16, width))],
        [whole((rows, width)), whole((16, width))],
        [shape_of((rows, width)), shape_of((16, width), F32)],
        [pltpu.VMEM((width, packed), BF16), pltpu.VMEM((rows, width), F32)],
    )(scal, dq, dkv, *w_pieces, dh2, layer_input, small, sums)
    dkv_late, n1_late, sums, gi = fence([dkv, n1, sums, gi])
    if direct:
        dkv_late, sums_of[1].last = fence([dkv_late, sums_of[1].last])
    gi_all = lax.all_gather(gi, "tp", axis=0)
    last_shape = shape_of((4, tp_size + 1, width // 8, 2 * head_cols))
    second_grads = call(
        second_grads_kernel,
        (tp_size + 1,),
        [
            mine,
            pl.BlockSpec((1, rows, 2 * head_cols), lambda i, *_: (jnp.minimum(i, tp_size - 1), 0, 0)),
            whole((16, width)),
        ],
        [pair_out] * 2,
        [last_shape] * 2,
    )(scal, n1_late, dkv_late, sums)

    if direct:
        sum_kv = Sum(second_grads[0], over_ctx(second_grads[1], 1), False)
        (sum_qo.got,) = fence([sum_qo.got], *second_grads)
        sum_kv.fence(sum_qo.first())
        sums_of[2].far, sums_of[3].far, y_own = fence([sums_of[2].far, sums_of[3].far, y_own], sum_kv.first())
        away = [sums_of[2].second(), sums_of[3].second()]
        early = (1, 0)
        flat = fence([sums_of[index].last for index in early] + [y_own], *away)
        for index, value in zip(early, flat):
            sums_of[index].last = value
        y_own = flat[-1]
        results = [sums_of[index].result() for index in (0, 1)]
        (sum_qo.far,) = fence([sum_qo.far], *results)
        away = sum_qo.second()
        sum_kv.far, gi_all = fence([sum_kv.far, gi_all], away)
        away = sum_kv.second()
        sums_of[2].last, sums_of[3].last = fence([sums_of[2].last, sums_of[3].last], away)
        results += [sums_of[2].result(), sums_of[3].result()]
        sum_kv.last, sum_qo.last = fence([sum_kv.last, sum_qo.last], *results)
        grads_qo, grads_kv = sum_qo.result(), sum_kv.result()
    else:
        grads_qo, grads_kv = scatter_plain(*first_grads), scatter_plain(*second_grads)
        results = [scatter_plain(*expert_group), scatter_plain(*shared_group)]
    activations = lax.all_gather((h2 + y_own[0].astype(F32)).astype(BF16), "tp", axis=0)
    grads_all = jnp.concatenate(
        [grads_qo, grads_kv[:tp_size], jnp.broadcast_to(grads_kv[tp_size:, :, :128], (tp_size, part, 128))], axis=-1
    )
    grads_all, gi_all = fence([grads_all.astype(BF16), gi_all])
    grads_all = jnp.sum(lax.all_to_all(grads_all, "tp", 0, 0, tiled=True).astype(F32), 0)
    grads_qo, grads_kv = grads_all[:, :2 * head_cols], grads_all[:, 2 * head_cols:4 * head_cols]
    sums = jnp.transpose(grads_all[:, 4 * head_cols:4 * head_cols + 16])
    grad_input = gi_all.astype(F32)
    results = [value.reshape(value.shape[0], 3, part, hidden) for value in results]
    grads_shared = results[-1][0]
    results = results[:-1]
    grads_exp = [jnp.concatenate([value[:, i] for value in results], axis=0) for i in range(3)]

    return (
        activations.reshape(layer_input.shape),
        grad_input.reshape(layer_input.shape),
        sums[8],
        grads_qo[:, :head_cols],
        grads_kv[:, :head_cols],
        grads_kv[:, head_cols:],
        jnp.transpose(grads_qo[:, head_cols:]),
        sums[9],
        jnp.transpose(sums[0:8]),
        grads_exp[0],
        grads_exp[1],
        jnp.transpose(grads_exp[2], (0, 2, 1)),
        grads_shared[0],
        grads_shared[1],
        jnp.transpose(grads_shared[2]),
    )


def solution(mesh):
    placed = (
        P("fsdp", "ctx", None),
        P("fsdp"),
        P("fsdp", "tp"),
        P("fsdp", "tp"),
        P("fsdp", "tp"),
        P("tp", "fsdp"),
        P("fsdp"),
        P("fsdp", None),
        P(None, "fsdp", "tp"),
        P(None, "fsdp", "tp"),
        P(None, "tp", "fsdp"),
        P("fsdp", "tp"),
        P("fsdp", "tp"),
        P("tp", "fsdp"),
        P("fsdp", "ctx", None),
        P("fsdp"),
        P("fsdp", "ctx", None),
    )
    return jax.shard_map(
        functools.partial(body, mesh.shape["fsdp"]),
        mesh=mesh,
        in_specs=placed,
        out_specs=(
            P("fsdp", "ctx", None),
            P("fsdp", "ctx", None),
            P(("fsdp", "ctx")),
            P(("fsdp", "ctx"), "tp"),
            P(("fsdp", "ctx"), "tp"),
            P(("fsdp", "ctx"), "tp"),
            P("tp", ("fsdp", "ctx")),
            P(("fsdp", "ctx")),
            P(("fsdp", "ctx"), None),
            P(None, ("fsdp", "ctx"), "tp"),
            P(None, ("fsdp", "ctx"), "tp"),
            P(None, "tp", ("fsdp", "ctx")),
            P(("fsdp", "ctx"), "tp"),
            P(("fsdp", "ctx"), "tp"),
            P("tp", ("fsdp", "ctx")),
        ),
        check_vma=False,
    )
```

time: 480 us -> 426 us (0.89)
  waiting for transfers between devices: 219 us -> 142 us
  local copies, waits for them, and re-layouts: 51.6 us -> 29.5 us
  other arithmetic: 36.1 us -> 55.7 us
  Pallas kernels: 125 us -> 139 us
  starting transfers between devices: 32.6 us -> 43.8 us
    reduce_scatter x1, waiting for transfers between devices: 38.1 us -> 7.67 us  [body(): dn_own = lax.psum_scatter(dn, 'tp', scatter_dimension=0, tiled=True)]
    all_gather x1, waiting for transfers between devices: 24.9 us -> 0.01 us  [body(): lax.all_gather((h2 + y_own[0].astype(F32)).astype(BF16), 'tp', axis=0)]
    pallas_call x4 -> x7, Pallas kernels: 45.9 us -> 59.4 us  [the longest x1 17.9 us: body(): call(attn_bwd_kernel, (tp_size,), [by_step((rows, packed))] + [kv_block]...]
    slice x4, local copies, waits for them, and re-layouts: 15.7 us -> 2.72 us  [the longest x1 1.91 us: body(): rest = up[half:]]
    reduce_scatter x2 -> x1, waiting for transfers between devices: 11.9 us -> 0.01 us  [body(): y_own = lax.psum_scatter(y_late, 'tp', scatter_dimension=0, tiled=True)]
    ppermute x8 -> x11, waiting for transfers between devices: 52.7 us -> 41.3 us  [over_x(): return lax.ppermute(value, 'fsdp', [(0, 1), (1, 0)])]
    ppermute x22 -> x31, waiting for transfers between devices: 68.3 us -> 79.1 us  [over_ctx(): return lax.ppermute(value, 'ctx', [(i, i ^ bit) for i in range(ctx_size)])]
    convert_element_type x7 -> x12, other arithmetic: 19.4 us -> 29.5 us  [the longest x3 9.84 us: first(): self.sent = self.both(1 - along_x, None).astype(BF16)]
  transfers between devices with their start and end apart: 41 -> 51, of which waited for: 20 -> 24; matrix products, arithmetic and copies ran while one was open for 14% -> 17% of each run, Pallas kernels for 13% -> 33%
where the time goes in v2:
time: 426 us; the launch traced here: 425 us
  waiting for transfers between devices  142 us (33%)
  Pallas kernels  139 us (33%)
  other arithmetic  55.7 us (13%)
  starting transfers between devices  43.8 us (10%)
  local copies, waits for them, and re-layouts  29.5 us (7%)
  between operations  14.6 us (3%)
    ppermute x31, waiting for transfers between devices, over_ctx(): return lax.ppermute(value, 'ctx', [(i, i ^ bit) for i in range(ctx_size)])  79.1 us
    pallas_call x1, Pallas kernels, body(): call(moe_kernel, (experts + seqs,), [full, full, whole((seqs, 8, rows)),...  46.4 us
    ppermute x11, waiting for transfers between devices, over_x(): return lax.ppermute(value, 'fsdp', [(0, 1), (1, 0)])  41.3 us
    ppermute x31, starting transfers between devices, over_ctx(): return lax.ppermute(value, 'ctx', [(i, i ^ bit) for i in range(ctx_size)])  18.6 us
    pallas_call x1, Pallas kernels, body(): call(attn_bwd_kernel, (tp_size,), [by_step((rows, packed))] + [kv_block]...  17.9 us
    ppermute x11, starting transfers between devices, over_x(): return lax.ppermute(value, 'fsdp', [(0, 1), (1, 0)])  15.3 us
    unnamed x73, local copies, waits for them, and re-layouts  13.9 us
    pallas_call x1, Pallas kernels, body(): call(attn_fwd_kernel, (seqs,), [by_step((rows, head_cols))] + [by_step((r...  12.4 us
  transfers between devices with their start and end apart: 51, of which 24 were waited for; matrix products, arithmetic and copies ran while one was open for 17% of the time, Pallas kernels for 33%

profile of v2, /device:TPU:0, one launch (start us, length us, event | category | flops | bytes accessed | tf_op | source)
XLA Modules:
  0.0 424.7 jit_solution(1678238751383944331)
XLA Ops:
  35.0 8.5 %shard_map.280 = (bf16[4,256,768]{2,1,0:T(8,128)(2,1)}, bf16[4,256,192]{2,1,0:T(8,128)(2,1)}, bf16[4,256,384]{2,1,0:T(8,128)(2,1)}, bf16[4,256,640]{2,1,0:T(8,12...) custom-call(s32[5]{0:T(128)} %stack.29.scal, bf16[4,256,768]{2,1,0:T(8,128)(2,1)} %x_ref.5, ...), custom_call_target="tpu_custom_call" | custom-call | flops 1 | bytes 1 | tf_op jit(solution)/shard_map/pallas_call | solution.py:579
  46.8 15.1 %collective-permute-done.2.kv2 = bf16[4,256,384]{2,1,0:T(8,128)(2,1)S(1)} collective-permute-done((bf16[4,256,384]{2,1,0:T(8,128)(2,1)}, bf16[4,256,384]{2,1,0:T(8,128)(2,1)S(1)}, u32[]{:S(2)}, u32[]{:S(2)}) %collective-permute-start.2) | collective-permute-done | bytes 786464 | tf_op jit(solution)/shard_map/ppermute | solution.py:492
  65.3 12.4 %shard_map.281 = bf16[4,128,384]{2,1,0:T(8,128)(2,1)} custom-call(s32[5]{0:T(128)} %stack.29.scal, s32[4]{0:T(128)} %prefix.3, bf16[4,256,192]{2,1,0:T(8,128)(2,1)} %get-tuple-element.144.q_ref, bf16[4,256,384]{2,1,0:T(8,128)(2,1)} %get-tuple-element.135.kv0, bf16[4,256,384]{2,1,0:T(8,128)(2,1)} %copy-done.23, bf16[4,256,384]{2,1,0:T(8,128)(2,1)} %copy-done.22, ...), custom_call_target="tpu_custom_call" | custom-call | flops 1 | bytes 1 | tf_op jit(solution)/shard_map/pallas_call | solution.py:621
  79.9 28.2 %collective-permute-done.6.v0 = bf16[384,512]{1,0:T(8,128)(2,1)S(1)} collective-permute-done((bf16[384,512]{1,0:T(8,128)(2,1)}, bf16[384,512]{1,0:T(8,128)(2,1)S(1)}, u32[]{:S(2)}, u32[]{:S(2)}) %collective-permute-start.6) | collective-permute-done | bytes 393248 | tf_op jit(solution)/shard_map/ppermute | solution.py:486
  117.3 7.3 %shard_map.282 = (bf16[4,256,768]{2,1,0:T(8,128)(2,1)}, f32[256,768]{1,0:T(8,128)}, f32[4,8,256]{2,1,0:T(8,128)}, s32[4,8,256]{2,1,0:T(8,128)}) custom-call(s32[5]{0:T(128)} %stack.29.scal, bf16[4,4,128,384]{3,2,1,0:T(8,128)(2,1)} %bitcast.159, bf16[4,2,192,384]{3,2,1,0:T(8,128)(2,1)} %bitcast.161, bf16[4,256,768]{2,1,0:T(8,128)(2,1)} %x_ref.5, ...), custom_call_target="tpu_custom_call" | custom-call | flops 1 | bytes 1 | tf_op jit(solution)/shard_map/pallas_call | solution.py:637
  124.6 14.4 %collective-permute-done.12.v2 = bf16[384,512]{1,0:T(8,128)(2,1)S(1)} collective-permute-done((bf16[384,512]{1,0:T(8,128)(2,1)S(1)}, bf16[384,512]{1,0:T(8,128)(2,1)S(1)}, u32[]{:S(2)}, u32[]{:S(2)}) %collective-permute-start.12) | collective-permute-done | bytes 393248 | tf_op jit(solution)/shard_map/ppermute | solution.py:492
  142.6 10.8 %shard_map.283 = (bf16[4,256,768]{2,1,0:T(8,128)(2,1)}, bf16[4,256,768]{2,1,0:T(8,128)(2,1)}, bf16[4,256,512]{2,1,0:T(8,128)(2,1)}, bf16[4,256,512]{2,1,0:T(8,128)(2,1)}, bf16[4,256,512]{2,1,0:T(8,128)(2,1)}) custom-call(s32[5]{0:T(128)} %stack.29.scal, bf16[4,256,768]{2,1,0:T(8,128)(2,1)} %get-tuple-element.180.n2_ref, bf16[4,256,768]{2,1,0:T(8,128)(2,1)} %dy_ref.7, ...), custom_call_target="tpu_custom_call" | custom-call | flops 1 | bytes 1 | tf_op jit(solution)/shard_map/pallas_call | solution.py:670
  153.4 5.0 %all-to-all-start = ((bf16[4,256,640]{2,1,0:T(8,128)(2,1)}), bf16[4,256,640]{2,1,0:T(8,128)(2,1)S(1)}, u32[]{:S(2)}, u32[]{:S(2)}) async-start(bf16[4,256,640]{2,1,0:T(8,128)(2,1)} %get-tuple-element.172), calls=%async_computation | async-start | bytes 2621440 | tf_op jit(solution)/shard_map/all_to_all | solution.py:684
  164.2 46.4 %shard_map.284 = (bf16[4,256,768]{2,1,0:T(8,128)(2,1)}, bf16[4,272,768]{2,1,0:T(8,128)(2,1)}, bf16[4,8,288,512]{3,2,1,0:T(8,128)(2,1)}, bf16[4,8,288,512]{3,2,1,0:T(8,128)(2,1)}) custom-call(s32[5]{0:T(128)} %stack.29.scal, bf16[4,256,768]{2,1,0:T(8,128)(2,1)} %get-tuple-element.180.n2_ref, bf16[4,256,768]{2,1,0:T(8,128)(2,1)} %dy_ref.7, ...), custom_call_target="tpu_custom_call" | custom-call | flops 1 | bytes 1 | tf_op jit(solution)/shard_map/pallas_call | solution.py:706
  212.0 7.5 %shard_map.285 = (bf16[4,1,288,512]{3,2,1,0:T(8,128)(2,1)}, bf16[4,1,288,512]{3,2,1,0:T(8,128)(2,1)}) custom-call(s32[5]{0:T(128)} %stack.29.scal, bf16[4,256,768]{2,1,0:T(8,128)(2,1)} %get-tuple-element.180.n2_ref, bf16[4,256,768]{2,1,0:T(8,128)(2,1)} %dy_ref.7, bf16[4,256,512]{2,1,0:T(8,128)(2,1)} %get-tuple-element.181.hid_ref, ...), custom_call_target="tpu_custom_call" | custom-call | flops 1 | bytes 1 | tf_op jit(solution)/shard_map/pallas_call | solution.py:732
  220.5 6.2 %collective-permute-done.21 = bf16[4,8,288,512]{3,2,1,0:T(8,128)(2,1)} collective-permute-done((bf16[4,8,288,512]{3,2,1,0:T(8,128)(2,1)}, bf16[4,8,288,512]{3,2,1,0:T(8,128)(2,1)}, u32[]{:S(2)}, u32[]{:S(2)}) %collective-permute-start.21) | collective-permute-done | bytes 9437216 | tf_op jit(solution)/shard_map/ppermute | solution.py:492
  232.7 4.6 %fusion = bf16[2,4,288,512]{3,2,1,0:T(8,128)(2,1)} fusion(bf16[2,2,8,288,512]{4,3,2,1,0:T(8,128)(2,1)} %bitcast.20, s32[]{:T(128)S(6)} %select_n.47, bf16[2,2,8,288,512]{4,3,2,1,0:T(8,128)(2,1)} %bitcast.154), kind=kLoop, calls=%fused_computation.1 | loop fusion | flops 4718592 | bytes 7077892 | tf_op jit(solution)/shard_map/convert_element_type | solution.py:769
  241.3 7.7 %reduce-scatter.3.cloned.1.call-done.dn_ref = bf16[1,272,768]{2,1,0:T(8,128)(2,1)} async-done(((bf16[4,272,768]{2,1,0:T(8,128)(2,1)}), bf16[1,272,768]{2,1,0:T(8,128)(2,1)}) %reduce-scatter.3.cloned.1.call-update) | async-done | bytes 417808 | tf_op jit(solution)/shard_map/reduce_scatter | solution.py:728
  250.1 4.7 %shard_map.286 = (f32[256,768]{1,0:T(8,128)}, bf16[4,128,384]{2,1,0:T(8,128)(2,1)}, bf16[256,768]{1,0:T(8,128)(2,1)}, f32[16,768]{1,0:T(8,128)}) custom-call(s32[5]{0:T(128)} %stack.29.scal, bf16[1,272,768]{2,1,0:T(8,128)(2,1)} %reduce-scatter.3.cloned.1.call-done.dn_ref, f32[4,8,256]{2,1,0:T(8,128)} %get-tuple-element.160.gates_ref, ...), custom_call_target="tpu_custom_call" | custom-call | flops 1 | bytes 1 | tf_op jit(solution)/shard_map/pallas_call | solution.py:813
  254.8 17.9 %shard_map.287 = (bf16[4,256,192]{2,1,0:T(8,128)(2,1)}, bf16[4,256,384]{2,1,0:T(8,128)(2,1)}, bf16[4,256,384]{2,1,0:T(8,128)(2,1)}, bf16[4,256,384]{2,1,0:T(8,128)(2,1)}, bf16[4,256,384]{2,1,0:T(8,128)(2,1)}) custom-call(s32[5]{0:T(128)} %stack.29.scal, s32[4]{0:T(128)} %prefix.3, bf16[4,256,640]{2,1,0:T(8,128)(2,1)} %copy-done.3, ...), custom_call_target="tpu_custom_call" | custom-call | flops 1 | bytes 1 | tf_op jit(solution)/shard_map/pallas_call | solution.py:843
  285.5 13.6 %collective-permute-done.28.c_ref = bf16[4,256,384]{2,1,0:T(8,128)(2,1)} collective-permute-done((bf16[4,256,384]{2,1,0:T(8,128)(2,1)}, bf16[4,256,384]{2,1,0:T(8,128)(2,1)}, u32[]{:S(2)}, u32[]{:S(2)}) %collective-permute-start.28) | collective-permute-done | bytes 786464 | tf_op jit(solution)/shard_map/ppermute | solution.py:492
  299.1 5.0 %shard_map.288.dkv_ref = bf16[4,256,384]{2,1,0:T(8,128)(2,1)} custom-call(bf16[4,256,384]{2,1,0:T(8,128)(2,1)} %get-tuple-element.191.a_ref, bf16[4,256,384]{2,1,0:T(8,128)(2,1)} %copy-done.25, bf16[4,256,384]{2,1,0:T(8,128)(2,1)} %collective-permute-done.28.c_ref, f32[256,640]{1,0:T(8,128)} %get-tuple-element.132.cos_ref, f32[256,640]{1,0:T(8,128)} %get-tuple-element.133.sin_ref), custom_call_target="tpu_custom_call" | custom-call | flops 1 | bytes 1 | tf_op jit(solution)/shard_map/pallas_call | solution.py:886
  304.1 7.2 %shard_map.289 = (bf16[256,768]{1,0:T(8,128)(2,1)}, f32[16,768]{1,0:T(8,128)}) custom-call(s32[5]{0:T(128)} %stack.29.scal, bf16[4,256,192]{2,1,0:T(8,128)(2,1)} %get-tuple-element.201.dq_ref, bf16[4,256,384]{2,1,0:T(8,128)(2,1)} %shard_map.288.dkv_ref, bf16[4,208,640]{2,1,0:T(8,128)(2,1)} %bitcast.184, bf16[4,208,640]{2,1,0:T(8,128)(2,1)} %collective-permute-done.18.w1, ...), custom_call_target="tpu_custom_call" | custom-call | flops 1 | bytes 1 | tf_op jit(solution)/shard_map/pallas_call | solution.py:898
  311.2 5.5 %shard_map.290 = (bf16[4,5,96,384]{3,2,1,0:T(8,128)(2,1)}, bf16[4,5,96,384]{3,2,1,0:T(8,128)(2,1)}) custom-call(s32[5]{0:T(128)} %stack.29.scal, bf16[4,256,768]{2,1,0:T(8,128)(2,1)} %get-tuple-element.214.n1_ref, bf16[4,256,384]{2,1,0:T(8,128)(2,1)} %shard_map.288.dkv_ref, f32[16,768]{1,0:T(8,128)} %get-tuple-element.216.sums_ref), custom_call_target="tpu_custom_call" | custom-call | flops 1 | bytes 1 | tf_op jit(solution)/shard_map/pallas_call | solution.py:913
  316.7 5.6 %shard_map.291 = (bf16[4,4,96,384]{3,2,1,0:T(8,128)(2,1)}, bf16[4,4,96,384]{3,2,1,0:T(8,128)(2,1)}) custom-call(s32[5]{0:T(128)} %stack.29.scal, bf16[4,256,768]{2,1,0:T(8,128)(2,1)} %get-tuple-element.214.n1_ref, bf16[4,256,192]{2,1,0:T(8,128)(2,1)} %get-tuple-element.201.dq_ref, bf16[256,768]{1,0:T(8,128)(2,1)} %get-tuple-element.220.low_ref, ...), custom_call_target="tpu_custom_call" | custom-call | flops 1 | bytes 1 | tf_op jit(solution)/shard_map/pallas_call | solution.py:870
  333.2 6.6 %collective-permute-done.33 = bf16[2,1,288,512]{3,2,1,0:T(8,128)(2,1)} collective-permute-done((bf16[2,1,288,512]{3,2,1,0:T(8,128)(2,1)}, bf16[2,1,288,512]{3,2,1,0:T(8,128)(2,1)}, u32[]{:S(2)}, u32[]{:S(2)}) %collective-permute-start.33) | collective-permute-done | bytes 589856 | tf_op jit(solution)/shard_map/ppermute | solution.py:492
  357.9 4.8 %collective-permute-done.37 = bf16[2,5,96,384]{3,2,1,0:T(8,128)(2,1)} collective-permute-done((bf16[2,5,96,384]{3,2,1,0:T(8,128)(2,1)}, bf16[2,5,96,384]{3,2,1,0:T(8,128)(2,1)}, u32[]{:S(2)}, u32[]{:S(2)}) %collective-permute-start.37) | collective-permute-done | bytes 737312 | tf_op jit(solution)/shard_map/ppermute | solution.py:486
  369.0 8.7 %collective-permute-done.40 = bf16[4,288,512]{2,1,0:T(8,128)(2,1)} collective-permute-done((bf16[4,288,512]{2,1,0:T(8,128)(2,1)S(1)}, bf16[4,288,512]{2,1,0:T(8,128)(2,1)}, u32[]{:S(2)}, u32[]{:S(2)}) %collective-permute-start.40) | collective-permute-done | bytes 1179680 | tf_op jit(solution)/shard_map/ppermute | solution.py:492
  400.3 10.7 %all-to-all-done.1 = bf16[4,96,896]{2,1,0:T(8,128)(2,1)} async-done(((bf16[4,96,896]{2,1,0:T(8,128)(2,1)}), bf16[4,96,896]{2,1,0:T(8,128)(2,1)}, u32[]{:S(2)}, u32[]{:S(2)}) %all-to-all-start.1) | async-done | bytes 688160 | tf_op jit(solution)/shard_map/all_to_all | solution.py:953
  (239 shorter events, 145.6 us)
Async XLA Ops:
  7.2 58.1 %all-gather.11.cloned.1.call-start = ((), (), s32[]{:S(2)}) async-start(), calls=%async_computation.6 | async-start | bytes 1474560 | tf_op jit(solution)/shard_map/all_gather | solution.py:576
  30.9 31.6 %collective-permute-start.4 = (bf16[1344,512]{1,0:T(8,128)(2,1)}, bf16[1344,512]{1,0:T(8,128)(2,1)S(1)}, u32[]{:S(2)}, u32[]{:S(2)}) collective-permute-start(bf16[1344,512]{1,0:T(8,128)(2,1)} %pad_maximum_fusion.2), channel_id=1, source_target_pairs={{0,16},{16,0},{1,17},{17,1},{2,18},{18,2},{3,19},{19,3},{4,20},{20... | collective-permute-start | bytes 4128776 | tf_op jit(solution)/shard_map/ppermute | solution.py:486
  34.4 81.4 %all-gather.13.cloned.1.call-start = ((), (), s32[]{:S(2)}) async-start(), calls=%async_computation.7 | async-start | bytes 1966080 | tf_op jit(solution)/shard_map/all_gather | solution.py:630
  62.8 45.3 %collective-permute-start.8 = (bf16[1344,512]{1,0:T(8,128)(2,1)S(1)}, bf16[1344,512]{1,0:T(8,128)(2,1)S(1)}, u32[]{:S(2)}, u32[]{:S(2)}) collective-permute-start(bf16[1344,512]{1,0:T(8,128)(2,1)S(1)} %collective-permute-done.4.g0.u0), channel_id=1, source_target_pairs={{0,8},{4,12},{8,0},{12,4},{1,9},{5,13},{9,1},{13,5},{2,10},{6,14},... | collective-permute-start | bytes 4128776 | tf_op jit(solution)/shard_map/ppermute | solution.py:492
  77.7 75.6 %all-gather.15.cloned.1.call-start = ((), (), s32[]{:S(2)}) async-start(), calls=%async_computation.8 | async-start | bytes 1331200 | tf_op jit(solution)/shard_map/all_gather | solution.py:636
  77.8 30.3 %collective-permute-start.7 = (bf16[1152,384]{1,0:T(8,128)(2,1)}, bf16[1152,384]{1,0:T(8,128)(2,1)}, u32[]{:S(2)}, u32[]{:S(2)}) collective-permute-start(bf16[1152,384]{1,0:T(8,128)(2,1)} %pad_maximum_fusion.3), channel_id=1, source_target_pairs={{0,16},{16,0},{1,17},{17,1},{2,18},{18,2},{3,19},{19,3},{4,20},{20... | collective-permute-start | bytes 2654216 | tf_op jit(solution)/shard_map/ppermute | solution.py:486
  79.3 28.8 %collective-permute-start.6 = (bf16[384,512]{1,0:T(8,128)(2,1)}, bf16[384,512]{1,0:T(8,128)(2,1)S(1)}, u32[]{:S(2)}, u32[]{:S(2)}) collective-permute-start(bf16[384,512]{1,0:T(8,128)(2,1)} %get-tuple-element.147), channel_id=1, source_target_pairs={{0,16},{16,0},{1,17},{17,1},{2,18},{18,2},{3,19},{19,3},{4,20},{20... | collective-permute-start | bytes 1179656 | tf_op jit(solution)/shard_map/ppermute | solution.py:486
  108.7 30.3 %collective-permute-start.11 = (bf16[1152,384]{1,0:T(8,128)(2,1)}, bf16[1152,384]{1,0:T(8,128)(2,1)}, u32[]{:S(2)}, u32[]{:S(2)}) collective-permute-start(bf16[1152,384]{1,0:T(8,128)(2,1)} %collective-permute-done.7.d0), channel_id=1, source_target_pairs={{0,8},{4,12},{8,0},{12,4},{1,9},{5,13},{9,1},{13,5},{2,10},{6,14},... | collective-permute-start | bytes 2654216 | tf_op jit(solution)/shard_map/ppermute | solution.py:492
  153.4 58.3 %all-to-all-start = ((bf16[4,256,640]{2,1,0:T(8,128)(2,1)}), bf16[4,256,640]{2,1,0:T(8,128)(2,1)S(1)}, u32[]{:S(2)}, u32[]{:S(2)}) async-start(bf16[4,256,640]{2,1,0:T(8,128)(2,1)} %get-tuple-element.172), calls=%async_computation | async-start | bytes 2621440 | tf_op jit(solution)/shard_map/all_to_all | solution.py:684
  158.4 90.6 %reduce-scatter.3.cloned.1.call-start = ((), (), s32[]{:S(2)}) async-start(), calls=%async_computation.4 | async-start | bytes 2088960 | tf_op jit(solution)/shard_map/reduce_scatter | solution.py:728
  158.4 52.2 %collective-permute-start.17 = (bf16[4,208,640]{2,1,0:T(8,128)(2,1)S(1)}, bf16[4,208,640]{2,1,0:T(8,128)(2,1)S(1)}, u32[]{:S(2)}, u32[]{:S(2)}) collective-permute-start(bf16[4,208,640]{2,1,0:T(8,128)(2,1)S(1)} %bitcast.185), channel_id=1, source_target_pairs={{0,8},{4,12},{8,0},{12,4},{1,9},{5,13},{9,1},{13,5},{2,10},{6,14},... | collective-permute-start | bytes 3194888 | tf_op jit(solution)/shard_map/ppermute | solution.py:492
  160.0 51.6 %collective-permute-start.18 = (bf16[4,208,640]{2,1,0:T(8,128)(2,1)S(1)}, bf16[4,208,640]{2,1,0:T(8,128)(2,1)}, u32[]{:S(2)}, u32[]{:S(2)}) collective-permute-start(bf16[4,208,640]{2,1,0:T(8,128)(2,1)S(1)} %bitcast.186), channel_id=1, source_target_pairs={{0,4},{4,0},{8,12},{12,8},{1,5},{5,1},{9,13},{13,9},{2,6},{6,2},{1... | collective-permute-start | bytes 3194888 | tf_op jit(solution)/shard_map/ppermute | solution.py:492
  211.9 127.9 %reduce-scatter.5.cloned.1.call-start = ((), (), s32[]{:S(2)}) async-start(), calls=%async_computation.5 | async-start | bytes 1966080 | tf_op jit(solution)/shard_map/reduce_scatter | solution.py:810
  239.6 33.0 %collective-permute-start.25 = (bf16[2,2,288,512]{3,2,1,0:T(8,128)(2,1)}, bf16[2,2,288,512]{3,2,1,0:T(8,128)(2,1)}, u32[]{:S(2)}, u32[]{:S(2)}) collective-permute-start(bf16[2,2,288,512]{3,2,1,0:T(8,128)(2,1)} %fusion.4), channel_id=1, source_target_pairs={{0,8},{4,12},{8,0},{12,4},{1,9},{5,13},{9,1},{13,5},{2,10},{6,14},... | collective-permute-start | bytes 3538952 | tf_op jit(solution)/shard_map/ppermute | solution.py:492
  240.2 32.4 %collective-permute-start.24 = (bf16[2,2,288,512]{3,2,1,0:T(8,128)(2,1)}, bf16[2,2,288,512]{3,2,1,0:T(8,128)(2,1)}, u32[]{:S(2)}, u32[]{:S(2)}) collective-permute-start(bf16[2,2,288,512]{3,2,1,0:T(8,128)(2,1)} %fusion.3), channel_id=1, source_target_pairs={{0,16},{16,0},{1,17},{17,1},{2,18},{18,2},{3,19},{19,3},{4,20},{20... | collective-permute-start | bytes 3538952 | tf_op jit(solution)/shard_map/ppermute | solution.py:486
  249.0 113.6 %all-gather.19.cloned.1.call-start = ((), (), s32[]{:S(2)}) async-start(), calls=%async_computation.10 | async-start | bytes 1966080 | tf_op jit(solution)/shard_map/all_gather | solution.py:911
  273.3 30.8 %collective-permute-start.29 = (bf16[4,208,640]{2,1,0:T(8,128)(2,1)S(1)}, bf16[4,208,640]{2,1,0:T(8,128)(2,1)}, u32[]{:S(2)}, u32[]{:S(2)}) collective-permute-start(bf16[4,208,640]{2,1,0:T(8,128)(2,1)S(1)} %copy-done.21), channel_id=1, source_target_pairs={{0,4},{4,0},{8,12},{12,8},{1,5},{5,1},{9,13},{13,9},{2,6},{6,2},{1... | collective-permute-start | bytes 3194888 | tf_op jit(solution)/shard_map/ppermute | solution.py:492
  280.0 59.8 %collective-permute-start.32 = (bf16[2,4,288,512]{3,2,1,0:T(8,128)(2,1)S(1)}, bf16[2,4,288,512]{3,2,1,0:T(8,128)(2,1)}, u32[]{:S(2)}, u32[]{:S(2)}) collective-permute-start(bf16[2,4,288,512]{3,2,1,0:T(8,128)(2,1)S(1)} %copy-done.8), channel_id=1, source_target_pairs={{0,16},{16,0},{1,17},{17,1},{2,18},{18,2},{3,19},{19,3},{4,20},{20... | collective-permute-start | bytes 7077896 | tf_op jit(solution)/shard_map/ppermute | solution.py:486
  284.9 26.3 %collective-permute-start.30 = (bf16[2,288,512]{2,1,0:T(8,128)(2,1)}, bf16[2,288,512]{2,1,0:T(8,128)(2,1)}, u32[]{:S(2)}, u32[]{:S(2)}) collective-permute-start(bf16[2,288,512]{2,1,0:T(8,128)(2,1)} %get-tuple-element.306), channel_id=1, source_target_pairs={{0,8},{4,12},{8,0},{12,4},{1,9},{5,13},{9,1},{13,5},{2,10},{6,14},... | collective-permute-start | bytes 1769480 | tf_op jit(solution)/shard_map/ppermute | solution.py:492
  322.9 92.3 %all-gather.17.cloned.1.call-start = ((), (), s32[]{:S(2)}) async-start(), calls=%async_computation.9 | async-start | bytes 1966080 | tf_op jit(solution)/shard_map/all_gather | solution.py:948
  328.8 23.7 %collective-permute-start.36 = (bf16[2,4,96,384]{3,2,1,0:T(8,128)(2,1)}, bf16[2,4,96,384]{3,2,1,0:T(8,128)(2,1)}, u32[]{:S(2)}, u32[]{:S(2)}) collective-permute-start(bf16[2,4,96,384]{3,2,1,0:T(8,128)(2,1)} %fusion.14), channel_id=1, source_target_pairs={{0,8},{4,12},{8,0},{12,4},{1,9},{5,13},{9,1},{13,5},{2,10},{6,14},... | collective-permute-start | bytes 1769480 | tf_op jit(solution)/shard_map/ppermute | solution.py:492
  331.8 30.8 %collective-permute-start.37 = (bf16[2,5,96,384]{3,2,1,0:T(8,128)(2,1)}, bf16[2,5,96,384]{3,2,1,0:T(8,128)(2,1)}, u32[]{:S(2)}, u32[]{:S(2)}) collective-permute-start(bf16[2,5,96,384]{3,2,1,0:T(8,128)(2,1)} %fusion.10), channel_id=1, source_target_pairs={{0,16},{16,0},{1,17},{17,1},{2,18},{18,2},{3,19},{19,3},{4,20},{20... | collective-permute-start | bytes 2211848 | tf_op jit(solution)/shard_map/ppermute | solution.py:486
  342.3 35.4 %collective-permute-start.40 = (bf16[4,288,512]{2,1,0:T(8,128)(2,1)S(1)}, bf16[4,288,512]{2,1,0:T(8,128)(2,1)}, u32[]{:S(2)}, u32[]{:S(2)}) collective-permute-start(bf16[4,288,512]{2,1,0:T(8,128)(2,1)S(1)} %fusion.2), channel_id=1, source_target_pairs={{0,8},{4,12},{8,0},{12,4},{1,9},{5,13},{9,1},{13,5},{2,10},{6,14},... | collective-permute-start | bytes 3538952 | tf_op jit(solution)/shard_map/ppermute | solution.py:492
  354.4 28.5 %collective-permute-start.39 = (bf16[4,96,384]{2,1,0:T(8,128)(2,1)}, bf16[4,96,384]{2,1,0:T(8,128)(2,1)}, u32[]{:S(2)}, u32[]{:S(2)}) collective-permute-start(bf16[4,96,384]{2,1,0:T(8,128)(2,1)} %fusion.16), channel_id=1, source_target_pairs={{0,16},{16,0},{1,17},{17,1},{2,18},{18,2},{3,19},{19,3},{4,20},{20... | collective-permute-start | bytes 884744 | tf_op jit(solution)/shard_map/ppermute | solution.py:486
  (60 other events, 639.9 us)
Sparse Core Ops, SparseCore 0:
  34.5 30.7 all-gather.10
  77.9 37.8 all-gather.12
  117.3 27.1 all-gather.14
  212.1 36.8 reduce-scatter.2
  251.1 34.3 reduce-scatter.4
  323.0 35.9 all-gather.18
  360.6 36.3 all-gather.16

commit v3 on v2

--- a/solution.py
+++ b/solution.py
@@ -48,22 +48,22 @@
 
 
 def qkv_kernel(scal, x_ref, own_ref, oth_ref, cos_ref, sin_ref, n1_ref, q_ref, kv_ref, all_ref, w_ref, small_ref, swap):
-    half = own_ref.shape[0]
+    half = own_ref.shape[1]
+    packed = w_ref.shape[0]
 
     @pl.when(pl.program_id(0) == 0)
     def _():
         mine = pl.multiple_of(scal[0] * half, half)
         other = pl.multiple_of((1 - scal[0]) * half, half)
-        w_ref[pl.ds(mine, half), :] = own_ref[...]
-        w_ref[pl.ds(other, half), :] = oth_ref[...]
-        swap[...] = mm(w_ref[...], rotation(w_ref.shape[1])).astype(BF16)
-        turned = jnp.transpose(w_ref[:, 128:256].astype(F32))
-        small_ref[...] = turned[64:80, :]
+        w_ref[:, pl.ds(mine, half)] = own_ref[:packed, :]
+        w_ref[:, pl.ds(other, half)] = oth_ref[:packed, :]
+        swap[...] = mm_tn(rotation(packed), w_ref[...]).astype(BF16)
+        small_ref[...] = w_ref[192:208, :].astype(F32)
 
     x = x_ref[0].astype(F32)
     n1 = (x * row_scale(x) * small_ref[8:9, :]).astype(BF16)
     n1_ref[0] = n1
-    turned = (mm(n1, w_ref[...]) * cos_ref[...] + mm(n1, swap[...]) * sin_ref[...]).astype(BF16)
+    turned = (mm_nt(n1, w_ref[...]) * cos_ref[...] + mm_nt(n1, swap[...]) * sin_ref[...]).astype(BF16)
     q_ref[0] = turned[:, :192]
     kv_ref[0] = turned[:, 256:640]
     all_ref[0] = turned
@@ -83,7 +83,7 @@
 def softmax(scores, seen):
     scores = jnp.where(seen, scores, -1e30)
     expo = jnp.exp(scores - jnp.max(scores, 0, keepdims=True))
-    return expo * (1.0 / jnp.sum(expo, 0, keepdims=True))
+    return expo, 1.0 / jnp.sum(expo, 0, keepdims=True)
 
 
 def attn_fwd_kernel(scal, prefix, q_ref, kv0, kv1, kv2, kv3, o_ref):
@@ -96,8 +96,8 @@
     seen = visible(scal, prefix[pl.program_id(0)], kv.shape[0], rows)
     outs = []
     for head in range(heads):
-        probs = softmax(mm_nt(k, only_head(q, head) * (HD ** -0.5)), seen).astype(BF16)
-        outs.append(mm(value_t[head * HD:(head + 1) * HD], probs))
+        expo, factor = softmax(mm_nt(k, only_head(q, head) * (HD ** -0.5)), seen)
+        outs.append(mm(value_t[head * HD:(head + 1) * HD], expo.astype(BF16)) * factor)
     o = jnp.transpose(jnp.concatenate(outs, axis=0))
     o_ref[0] = jnp.concatenate([o[: rows // 2], o[rows // 2:]], axis=1).astype(BF16)
 
@@ -164,7 +164,7 @@
 
 def shared_kernel(
     scal, n2_ref, dy_ref, go_ref, uo_ref, do_ref, g0, g1, g2, g3, u0, u1, u2, u3, d0, d1, d2, d3,
-    ys_ref, dn_ref, hid_ref, da_ref, db_ref, wg, wu, wd,
+    ys_ref, dn_ref, hid_ref, dab_ref, wgu, wd,
 ):
     step = pl.program_id(0)
     half = go_ref.shape[0]
@@ -174,46 +174,50 @@
     def _():
         mine = pl.multiple_of(scal[0] * half, half)
         other = (1 - scal[0]) * half
-        wg[pl.ds(mine, half), :] = go_ref[...]
-        wu[pl.ds(mine, half), :] = uo_ref[...]
+        wgu[pl.ds(mine, half), :hidden] = go_ref[...]
+        wgu[pl.ds(mine, half), hidden:] = uo_ref[...]
         wd[:, pl.ds(mine, half)] = do_ref[...]
         for piece, (g, u, d) in enumerate(((g0, u0, d0), (g1, u1, d1), (g2, u2, d2), (g3, u3, d3))):
             quarter = scal[3] ^ piece
             at = pl.multiple_of(other + quarter * (half // 4), half // 4)
-            wg[pl.ds(at, half // 4), :] = g[...]
-            wu[pl.ds(at, half // 4), :] = u[...]
+            wgu[pl.ds(at, half // 4), :hidden] = g[...]
+            wgu[pl.ds(at, half // 4), hidden:] = u[...]
             at = pl.multiple_of(quarter * (hidden // 4), hidden // 4)
             wd[pl.ds(at, hidden // 4), pl.ds(pl.multiple_of(other, half), half)] = d[...]
 
     n2 = n2_ref[0]
     dy = dy_ref[0]
-    gate = mm(n2, wg[...])
-    up = mm(n2, wu[...])
+    both = mm(n2, wgu[...])
+    gate, up = both[:, :hidden], both[:, hidden:]
     sigma, silu = silu_parts(gate)
     hid = (silu * up).astype(BF16)
     ys_ref[0] = mm(hid, wd[...]).astype(BF16)
     back = mm_nt(dy, wd[...])
     da = (back * up * (sigma * (1.0 + gate * (1.0 - sigma)))).astype(BF16)
     db = (back * silu).astype(BF16)
-    dn_ref[0] = (mm_nt(da, wg[...]) + mm_nt(db, wu[...])).astype(BF16)
+    dab = jnp.concatenate([da, db], axis=1)
+    dn_ref[0] = mm_nt(dab, wgu[...]).astype(BF16)
     hid_ref[0] = hid
-    da_ref[0] = da
-    db_ref[0] = db
-
-
-def shared_grads_kernel(scal, n2_ref, dy_ref, hid_ref, da_ref, db_ref, keep_ref, send_ref):
-    n2, dy, hid, da, db = [
-        ref[...].reshape(-1, ref.shape[-1]) for ref in (n2_ref, dy_ref, hid_ref, da_ref, db_ref)
-    ]
-    put_grads(scal[4], keep_ref, send_ref, 0, mm_tn(n2, da))
-    put_grads(scal[4], keep_ref, send_ref, 1, mm_tn(n2, db))
-    put_grads(scal[4], keep_ref, send_ref, 2, mm_tn(dy, hid))
+    dab_ref[0] = dab
+
+
+def put_all_grads(core, keep_ref, send_ref, value, upstream, hid, dab):
+    wide = mm_tn(value, dab)
+    hidden = hid.shape[1]
+    put_grads(core, keep_ref, send_ref, 0, wide[:, :hidden])
+    put_grads(core, keep_ref, send_ref, 1, wide[:, hidden:])
+    put_grads(core, keep_ref, send_ref, 2, mm_tn(upstream, hid))
+
+
+def shared_grads_kernel(scal, n2_ref, dy_ref, hid_ref, dab_ref, keep_ref, send_ref):
+    values = [ref[...].reshape(-1, ref.shape[-1]) for ref in (n2_ref, dy_ref, hid_ref, dab_ref)]
+    put_all_grads(scal[4], keep_ref, send_ref, *values)
 
 
 def moe_kernel(
     scal, n2_ref, dy_ref, slots_ref, gates_ref, ys_ref, dn_in_ref, go_ref, uo_ref, do_ref,
     g0, g1, g2, g3, u0, u1, u2, u3, v0, v1, v2, v3, d0, d1, d2, d3,
-    y_ref, dn_ref, keep_ref, send_ref, wg, wu, wd, pick_s, ye_s, dx_s, xe_s, dy_s, de_s, gs_s, dprob_s,
+    y_ref, dn_ref, keep_ref, send_ref, wgu, wd, pick_s, ye_s, dx_s, xe_s, dy_s, de_s, gs_s, dprob_s,
 ):
     step = pl.program_id(0)
     seqs, rows, width = n2_ref.shape
@@ -226,20 +230,21 @@
         expert = 2 * (piece ^ scal[3]) + step % 2
         mine = pl.multiple_of(scal[0] * half, half)
         other = pl.multiple_of((1 - scal[0]) * half, half)
-        wg[pl.ds(mine, half), :] = go_ref[0]
-        wu[pl.ds(mine, half), :] = uo_ref[0]
+        hidden = go_ref.shape[2]
+        wgu[pl.ds(mine, half), :hidden] = go_ref[0]
+        wgu[pl.ds(mine, half), hidden:] = uo_ref[0]
         wd[:, pl.ds(mine, half)] = do_ref[0]
         arrived = ((g0, u0, v0, d0), (g1, u1, v1, d1), (g2, u2, v2, d2), (g3, u3, v3, d3))
         for index, (g, u, v, d) in enumerate(arrived):
             @pl.when(piece == index)
             def _(g=g, d=d):
-                wg[pl.ds(other, half), :] = g[...]
+                wgu[pl.ds(other, half), :hidden] = g[...]
                 wd[:, pl.ds(other, half)] = d[...]
 
             for odd, ref in enumerate((u, v)):
                 @pl.when((piece == index) & (step % 2 == odd))
                 def _(ref=ref):
-                    wu[pl.ds(other, half), :] = ref[...]
+                    wgu[pl.ds(other, half), hidden:] = ref[...]
 
         slot_at = pl.ds(pl.multiple_of(step * SLOTS, 16), SLOTS)
         slot = lax.broadcasted_iota(jnp.int32, (SLOTS, rows), 0)
@@ -256,8 +261,8 @@
             gs_s[at, :] = jnp.broadcast_to(gate_slot, (SLOTS, 128))
 
         xe = xe_s[...]
-        gate = mm(xe, wg[...])
-        up = mm(xe, wu[...])
+        both = mm(xe, wgu[...])
+        gate, up = both[:, :hidden], both[:, hidden:]
         sigma, silu = silu_parts(gate)
         hid = (silu * up).astype(BF16)
         ye = mm(hid, wd[...])
@@ -271,12 +276,11 @@
         back = mm_nt(de_s[...], wd[...])
         da = (back * up * (sigma * (1.0 + gate * (1.0 - sigma)))).astype(BF16)
         db = (back * silu).astype(BF16)
-        dx = (mm_nt(da, wg[...]) + mm_nt(db, wu[...])).astype(BF16)
+        dab = jnp.concatenate([da, db], axis=1)
+        dx = mm_nt(dab, wgu[...]).astype(BF16)
         for s in range(seqs):
             dx_s[s, slot_at, :] = dx[s * SLOTS:(s + 1) * SLOTS]
-        put_grads(scal[4], keep_ref, send_ref, 0, mm_tn(xe_s[...], da))
-        put_grads(scal[4], keep_ref, send_ref, 1, mm_tn(xe_s[...], db))
-        put_grads(scal[4], keep_ref, send_ref, 2, mm_tn(de_s[...], hid))
+        put_all_grads(scal[4], keep_ref, send_ref, xe, de_s[...], hid, dab)
 
     @pl.when(step >= experts)
     def _():
@@ -334,7 +338,8 @@
     for head in range(heads):
         q_head = only_head(q, head) * (HD ** -0.5)
         do_head = only_head(do, head)
-        probs = softmax(mm_nt(k, q_head), seen)
+        expo, factor = softmax(mm_nt(k, q_head), seen)
+        probs = expo * factor
         dp = mm_nt(v, do_head)
         ds = (probs * (dp - jnp.sum(dp * probs, 0, keepdims=True))).astype(BF16)
         dq = mm(key_t[head * HD:(head + 1) * HD], ds) * (HD ** -0.5)
@@ -363,12 +368,12 @@
 
 def end_kernel(scal, dq_ref, dkv_ref, w0, w1, w2, w3, dh2_ref, x_ref, small_ref, sums_in, gi_ref, sums_ref, w, total):
     step = pl.program_id(0)
-    quarter = w0.shape[1]
     head_cols = dq_ref.shape[2]
+    quarter = w.shape[0] // 4
     for piece, ref in enumerate((w0, w1, w2, w3)):
         at = pl.multiple_of((scal[1] ^ piece) * quarter, quarter)
         w[pl.ds(at, quarter), :] = ref[0]
-    part = mm_nt(dq_ref[0], w[:, :head_cols]) + mm_nt(dkv_ref[0], w[:, 256:])
+    part = mm(dq_ref[0], w[:head_cols, :]) + mm(dkv_ref[0], w[256:, :])
 
     @pl.when(step == 0)
     def _():
@@ -493,21 +498,22 @@
 
     columns = jnp.concatenate(
         [
-            query_weight,
-            router,
-            gain_attn[:, None],
-            gain_ffn[:, None],
-            jnp.zeros((query_weight.shape[0], 54), BF16),
-            key_weight,
-            value_weight,
+            query_weight.T,
+            router.T,
+            gain_attn[None],
+            gain_ffn[None],
+            jnp.zeros((54, query_weight.shape[0]), BF16),
+            key_weight.T,
+            value_weight.T,
+            output_weight,
         ],
-        axis=1,
+        axis=0,
     )
     if paired:
         columns_own, columns_other = columns, over_x(columns)
     else:
-        columns = lax.all_gather(columns, "fsdp", axis=0, tiled=True)
-        columns_own, columns_other = columns[:half], columns[half:]
+        columns = lax.all_gather(columns, "fsdp", axis=1, tiled=True)
+        columns_own, columns_other = columns[:, :half], columns[:, half:]
 
     shared_own = (shared_gate_weight, shared_up_weight, shared_down_weight)
     experts_own = (exp_gate, exp_up, exp_down)
@@ -545,12 +551,6 @@
         rest_p = [up_all[p, 1] for p in range(4)]
         down_p = [jnp.concatenate([down_all[p, 0], down_all[p, 1], sd_all[p]], axis=0) for p in range(4)]
 
-    if paired:
-        out_pieces = [output_weight, over_x(fence([output_weight], columns)[0])]
-    else:
-        out_pieces = lax.all_gather(output_weight, "fsdp", axis=1, tiled=True)
-        out_pieces = [out_pieces[:, :half], out_pieces[:, half:]]
-
     positions = (ctx * rows + jnp.arange(rows, dtype=jnp.int32)).astype(F32)
     inverse = jnp.exp(jnp.arange(HD // 2, dtype=F32) * (-math.log(10000.0) / (HD // 2)))
     angles = positions[:, None] * inverse[None, :]
@@ -565,15 +565,13 @@
     cos_table, sin_table = table(cosine, 1.0), table(sine, 0.0)
     routes_t = jnp.pad(jnp.transpose(routes, (0, 2, 1)), ((0, 0), (0, 6), (0, 0)))
 
-    columns_other, cos_table, sin_table = fence([columns_other, cos_table, sin_table], routes_t)
+    cos_t, sin_t = jnp.transpose(cosine), jnp.transpose(sine)
+    columns_other, cos_table, sin_table, cos_t, sin_t = fence([columns_other, cos_table, sin_table, cos_t, sin_t], routes_t)
     if paired:
-        out_own, out_other = out_pieces
-        columns_other, out_other, cos_table, wide, rest, down = fence(
-            [columns_other, out_other, cos_table, wide, rest, down]
-        )
-        out_pieces = [out_own, out_other]
+        columns_other, cos_table, wide, rest, down = fence([columns_other, cos_table, wide, rest, down])
         wide_0 = over_x(wide)
-    out_pieces = lax.all_gather(jnp.stack(out_pieces), "tp", axis=0)
+    out_pieces = jnp.stack([columns_own[-head_cols:], columns_other[-head_cols:]])
+    out_pieces = lax.all_gather(out_pieces, "tp", axis=0)
     packed = cos_table.shape[1]
 
     n1, q, kv, qkv, w_qkv, small = call(
@@ -581,8 +579,8 @@
         (seqs,),
         [
             by_step((rows, width)),
-            whole((half, packed)),
-            whole((half, packed)),
+            whole((packed + head_cols, half)),
+            whole((packed + head_cols, half)),
             whole((rows, packed)),
             whole((rows, packed)),
         ],
@@ -591,7 +589,7 @@
             by_step((rows, head_cols)),
             by_step((rows, 2 * head_cols)),
             by_step((rows, packed)),
-            whole((width, packed)),
+            whole((packed, width)),
             whole((16, width)),
         ],
         [
@@ -599,22 +597,24 @@
             shape_of((seqs, rows, head_cols)),
             shape_of((seqs, rows, 2 * head_cols)),
             shape_of((seqs, rows, packed)),
-            shape_of((width, packed)),
+            shape_of((packed, width)),
             shape_of((16, width), F32),
         ],
-        [pltpu.VMEM((width, packed), BF16)],
+        [pltpu.VMEM((packed, width), BF16)],
     )(scal, layer_input, columns_own, columns_other, cos_table, sin_table)
 
     kv_0 = kv
     kv_2 = over_ctx(kv_0, 2)
     kv_1 = over_ctx(kv_0, 1)
     q_now, kv_2 = fence([q, kv_2], kv_1)
-    w_part = lax.dynamic_slice_in_dim(w_qkv, (width // 4) * ctx, width // 4, 0)
+    w_part = lax.dynamic_slice_in_dim(w_qkv, (packed // 4) * ctx, packed // 4, 0)
     w_part = jnp.pad(w_part, ((0, 16), (0, 0)))
     if paired:
         kv_2, wide_0, rest, down, w_part = fence([kv_2, wide_0, rest, down, w_part])
         wide_2 = over_ctx(wide_0, 2)
-        down_0, rest_0 = over_x(down), over_x(rest)
+        rest_0 = over_x(rest)
+        (down,) = fence([down], rest)
+        down_0 = over_x(down)
     kv_3 = over_ctx(kv_2, 1)
     q_now, kv_3, out_pieces = fence([q_now, kv_3, out_pieces])
 
@@ -629,10 +629,14 @@
 
     o_all = lax.all_gather(o, "tp", axis=0)
     if paired:
-        wide_0, rest_0, down_0, wide_2 = fence([wide_0, rest_0, down_0, wide_2], o)
-        down_2, rest_2, wide_1, wide_3 = over_ctx(down_0, 2), over_ctx(rest_0, 2), over_ctx(wide_0, 1), over_ctx(wide_2, 1)
-        o_all, wide_1, wide_3 = fence([o_all, wide_1, wide_3])
-        down_1, rest_1 = over_ctx(down_0, 1), over_ctx(rest_0, 1)
+        wide_0, rest_0 = fence([wide_0, rest_0], o)
+        rest_2, rest_1, wide_1 = over_ctx(rest_0, 2), over_ctx(rest_0, 1), over_ctx(wide_0, 1)
+        down_0, wide_2, rest_1, wide_1 = fence([down_0, wide_2, rest_1, wide_1])
+        down_2, down_1, wide_3 = over_ctx(down_0, 2), over_ctx(down_0, 1), over_ctx(wide_2, 1)
+        (rest_2,) = fence([rest_2], down_0, wide_2)
+        down_1, wide_3 = fence([down_1, wide_3], rest_2)
+        rest_3 = over_ctx(rest_2, 1)
+        o_all, down_1, wide_3 = fence([o_all, down_1, wide_3])
     w_0 = lax.all_gather(fence([w_part], o_all)[0], "tp", axis=0)
     n2, h2, gates, slots = call(
         post_kernel,
@@ -655,8 +659,8 @@
     )(scal, o_all, out_pieces, layer_input, small, routes_t)
 
     if paired:
-        down_2, rest_2, n2 = fence([down_2, rest_2, n2])
-        down_3, rest_3 = over_ctx(down_2, 1), over_ctx(rest_2, 1)
+        down_2, rest_3 = fence([down_2, rest_3], n2)
+        down_3 = over_ctx(down_2, 1)
         wide_p = (wide_0, wide_1, wide_2, wide_3)
         rest_p = (rest_0, rest_1, rest_2, rest_3)
         down_p = (down_0, down_1, down_2, down_3)
@@ -665,8 +669,7 @@
     part_rows = 3 * (width // 8)
     upper = [pl.BlockSpec((half // 4, hidden), lambda *_, at=at: (at, 0)) for at in (12, 13)]
     lower = pl.BlockSpec((hidden // 4, half), lambda *_: (8, 0))
-    weights = [pltpu.VMEM((width, hidden), BF16)] * 2 + [pltpu.VMEM((hidden, width), BF16)]
-    hidden_shape = shape_of((seqs, rows, hidden))
+    weights = [pltpu.VMEM((width, 2 * hidden), BF16), pltpu.VMEM((hidden, width), BF16)]
     ys, dn_shared, *shared_hidden = call(
         shared_kernel,
         (seqs,),
@@ -675,8 +678,8 @@
         + [upper[0]] * 4
         + [upper[1]] * 4
         + [lower] * 4,
-        [by_step((rows, width))] * 2 + [by_step((rows, hidden))] * 3,
-        [shape_of((seqs, rows, width))] * 2 + [hidden_shape] * 3,
+        [by_step((rows, width))] * 2 + [by_step((rows, hidden)), by_step((rows, 2 * hidden))],
+        [shape_of((seqs, rows, width))] * 2 + [shape_of((seqs, rows, hidden)), shape_of((seqs, rows, 2 * hidden))],
         weights,
     )(scal, n2, cotangent, *own[3:], *wide_p, *wide_p, *down_p)
 
@@ -732,7 +735,7 @@
     shared_group = call(
         shared_grads_kernel,
         (1,),
-        [full] * 2 + [whole((seqs, rows, hidden))] * 3,
+        [full] * 2 + [whole((seqs, rows, hidden)), whole((seqs, rows, 2 * hidden))],
         [whole(block)] * 2,
         [shape_of(block)] * 2,
     )(scal, n2_late, cotangent, *shared_hidden)
@@ -800,10 +803,11 @@
         sent = [sums_of[1].first(), sums_of[0].first()]
         sums_of[2].fence(*sent)
         sent.append(sums_of[2].first())
-        sums_of[3].fence(*sent)
-        sent.append(sums_of[3].first())
         (kv_seq_2,) = fence([kv_seq_2], *sent)
     kv_seq_3 = over_ctx(kv_seq_2, 1)
+    if direct:
+        sums_of[3].fence(*sent, kv_seq_2)
+        kv_seq_1, kv_seq_3 = fence([kv_seq_1, kv_seq_3], sums_of[3].first())
     kv_seqs = (kv_seq, kv_seq_1, kv_seq_2, kv_seq_3)
     (dn_own,) = fence([dn_own], kv_seq_1, kv_seq_3)
     (y_late,) = fence([y], dn_own)
@@ -837,7 +841,6 @@
         [pltpu.VMEM((width, width), BF16)],
     )(scal, dn_own, gates, h2, n2, cotangent, small, out_pieces)
 
-    cos_t, sin_t = jnp.transpose(cosine), jnp.transpose(sine)
     kv_block = by_step((rows, 2 * head_cols))
     kv_shape = shape_of((tp_size, rows, 2 * head_cols))
     dq, e0, e1, e2, e3 = call(
@@ -883,6 +886,8 @@
     if direct:
         sum_qo = Sum(first_grads[0], over_ctx(first_grads[1], 1), True)
         (from_y,) = fence([from_y], sum_qo.first())
+    from_y, y_own = fence([from_y, y_own])
+    activations = lax.all_gather((h2 + y_own[0].astype(F32)).astype(BF16), "tp", axis=0)
     dkv = call(
         swing_kernel,
         (tp_size,),
@@ -899,11 +904,11 @@
         end_kernel,
         (tp_size,),
         [by_group((rows, head_cols)), by_group((rows, 2 * head_cols))]
-        + [by_group((width // 4, packed))] * 4
+        + [by_group((packed // 4, width))] * 4
         + [whole((rows, width)), mine, whole((16, width)), whole((16, width))],
         [whole((rows, width)), whole((16, width))],
         [shape_of((rows, width)), shape_of((16, width), F32)],
-        [pltpu.VMEM((width, packed), BF16), pltpu.VMEM((rows, width), F32)],
+        [pltpu.VMEM((packed, width), BF16), pltpu.VMEM((rows, width), F32)],
     )(scal, dq, dkv, *w_pieces, dh2, layer_input, small, sums)
     dkv_late, n1_late, sums, gi = fence([dkv, n1, sums, gi])
     if direct:
@@ -924,28 +929,27 @@
 
     if direct:
         sum_kv = Sum(second_grads[0], over_ctx(second_grads[1], 1), False)
-        (sum_qo.got,) = fence([sum_qo.got], *second_grads)
-        sum_kv.fence(sum_qo.first())
-        sums_of[2].far, sums_of[3].far, y_own = fence([sums_of[2].far, sums_of[3].far, y_own], sum_kv.first())
-        away = [sums_of[2].second(), sums_of[3].second()]
+        (sums_of[3].far,) = fence([sums_of[3].far], *second_grads)
+        sum_kv.fence(sums_of[3].far)
+        (sums_of[2].far,) = fence([sums_of[2].far], sum_kv.first())
+        (sum_qo.far,) = fence([sum_qo.far], sums_of[2].second(), sums_of[3].second())
+        away = sum_qo.second()
         early = (1, 0)
-        flat = fence([sums_of[index].last for index in early] + [y_own], *away)
+        flat = fence([sums_of[index].last for index in early], away)
         for index, value in zip(early, flat):
             sums_of[index].last = value
-        y_own = flat[-1]
         results = [sums_of[index].result() for index in (0, 1)]
-        (sum_qo.far,) = fence([sum_qo.far], *results)
-        away = sum_qo.second()
-        sum_kv.far, gi_all = fence([sum_kv.far, gi_all], away)
+        (sum_kv.far,) = fence([sum_kv.far], *results)
         away = sum_kv.second()
-        sums_of[2].last, sums_of[3].last = fence([sums_of[2].last, sums_of[3].last], away)
-        results += [sums_of[2].result(), sums_of[3].result()]
+        (sums_of[3].last,) = fence([sums_of[3].last], away)
+        shared_result = sums_of[3].result()
+        (sums_of[2].last,) = fence([sums_of[2].last], away)
+        results += [sums_of[2].result(), shared_result]
         sum_kv.last, sum_qo.last = fence([sum_kv.last, sum_qo.last], *results)
         grads_qo, grads_kv = sum_qo.result(), sum_kv.result()
     else:
         grads_qo, grads_kv = scatter_plain(*first_grads), scatter_plain(*second_grads)
         results = [scatter_plain(*expert_group), scatter_plain(*shared_group)]
-    activations = lax.all_gather((h2 + y_own[0].astype(F32)).astype(BF16), "tp", axis=0)
     grads_all = jnp.concatenate(
         [grads_qo, grads_kv[:tp_size], jnp.broadcast_to(grads_kv[tp_size:, :, :128], (tp_size, part, 128))], axis=-1
     )

time: 426 us -> 406 us (0.953)
  waiting for transfers between devices: 142 us -> 128 us
    ppermute x31, waiting for transfers between devices: 79.1 us -> 71.3 us  [over_ctx(): return lax.ppermute(value, 'ctx', [(i, i ^ bit) for i in range(ctx_size)])]
    unnamed x73, local copies, waits for them, and re-layouts: 13.9 us -> 7.38 us
    all_to_all x1, waiting for transfers between devices: 10.7 us -> 5.02 us  [body(): lax.all_to_all(grads_all, 'tp', 0, 0, tiled=True).astype(F32)]
    concatenate x1, local copies, waits for them, and re-layouts: 0.5 us -> 4.77 us  [body(): jnp.concatenate([query_weight.T, router.T, gain_attn[None], gain_ffn[None...]
    ppermute x11 -> x10, waiting for transfers between devices: 41.3 us -> 40.4 us  [over_x(): return lax.ppermute(value, 'fsdp', [(0, 1), (1, 0)])]
    ppermute x11 -> x10, starting transfers between devices: 15.3 us -> 14.6 us  [over_x(): return lax.ppermute(value, 'fsdp', [(0, 1), (1, 0)])]
  transfers between devices with their start and end apart: 51 -> 50, of which waited for: 24 -> 17; matrix products, arithmetic and copies ran while one was open for 17% -> 16% of each run, Pallas kernels for 33% -> 34%
where the time goes in v3:
time: 406 us; the launch traced here: 404 us
  Pallas kernels  138 us (34%)
  waiting for transfers between devices  128 us (32%)
  other arithmetic  52.5 us (13%)
  starting transfers between devices  42.5 us (10%)
  local copies, waits for them, and re-layouts  28.9 us (7%)
  between operations  14.7 us (4%)
    ppermute x31, waiting for transfers between devices, over_ctx(): return lax.ppermute(value, 'ctx', [(i, i ^ bit) for i in range(ctx_size)])  71.3 us
    pallas_call x1, Pallas kernels, body(): call(moe_kernel, (experts + seqs,), [full, full, whole((seqs, 8, rows)),...  46.8 us
    ppermute x10, waiting for transfers between devices, over_x(): return lax.ppermute(value, 'fsdp', [(0, 1), (1, 0)])  40.4 us
    ppermute x31, starting transfers between devices, over_ctx(): return lax.ppermute(value, 'ctx', [(i, i ^ bit) for i in range(ctx_size)])  18 us
    pallas_call x1, Pallas kernels, body(): call(attn_bwd_kernel, (tp_size,), [by_step((rows, packed))] + [kv_block]...  17.6 us
    ppermute x10, starting transfers between devices, over_x(): return lax.ppermute(value, 'fsdp', [(0, 1), (1, 0)])  14.6 us
    pallas_call x1, Pallas kernels, body(): call(attn_fwd_kernel, (seqs,), [by_step((rows, head_cols))] + [by_step((r...  11.1 us
    pallas_call x1, Pallas kernels, body(): call(shared_kernel, (seqs,), [by_step((rows, width))] * 2 + [whole((half,...  10.8 us
  transfers between devices with their start and end apart: 50, of which 17 were waited for; matrix products, arithmetic and copies ran while one was open for 16% of the time, Pallas kernels for 34%

profile of v3, /device:TPU:0, one launch (start us, length us, event | category | flops | bytes accessed | tf_op | source)
XLA Modules:
  0.0 404.0 jit_solution(16287971497586695230)
XLA Ops:
  8.6 4.8 %concatenate.28.own_ref = bf16[832,384]{1,0:T(8,128)(2,1)S(1)} concatenate(bf16[192,384]{1,0:T(8,128)(2,1)} %bitcast.195, bf16[8,384]{1,0:T(8,128)(2,1)} %bitcast.199, bf16[1,384]{1,0:T(2,128)(2,1)S(1)} %broadcast_in_dim.24, bf16[1,384]{1,0:T(2,128)(2,1)S(1)} %broadcast_in_dim.25, bf16[54,384]{1,0:T(8,128)(2,1)S(1)} %broadcast_in_dim.26, bf16[192,384]{1,0:T(8,128)(2,1)} %bitcast.196, ...), dimensions={0} | concatenate | bytes 1277952 | tf_op jit(solution)/shard_map/concatenate | solution.py:499
  35.0 8.4 %shard_map.280 = (bf16[4,256,768]{2,1,0:T(8,128)(2,1)}, bf16[4,256,192]{2,1,0:T(8,128)(2,1)}, bf16[4,256,384]{2,1,0:T(8,128)(2,1)}, bf16[4,256,640]{2,1,0:T(8,12...) custom-call(s32[5]{0:T(128)} %stack.29.scal, bf16[4,256,768]{2,1,0:T(8,128)(2,1)} %x_ref.5, ...), custom_call_target="tpu_custom_call" | custom-call | flops 1 | bytes 1 | tf_op jit(solution)/shard_map/pallas_call | solution.py:577
  46.6 15.1 %collective-permute-done.1.kv2 = bf16[4,256,384]{2,1,0:T(8,128)(2,1)S(1)} collective-permute-done((bf16[4,256,384]{2,1,0:T(8,128)(2,1)}, bf16[4,256,384]{2,1,0:T(8,128)(2,1)S(1)}, u32[]{:S(2)}, u32[]{:S(2)}) %collective-permute-start.1) | collective-permute-done | bytes 786464 | tf_op jit(solution)/shard_map/ppermute | solution.py:497
  65.5 11.1 %shard_map.281 = bf16[4,128,384]{2,1,0:T(8,128)(2,1)} custom-call(s32[5]{0:T(128)} %stack.29.scal, s32[4]{0:T(128)} %prefix.3, bf16[4,256,192]{2,1,0:T(8,128)(2,1)} %get-tuple-element.147.q_ref, bf16[4,256,384]{2,1,0:T(8,128)(2,1)} %get-tuple-element.139.kv0, bf16[4,256,384]{2,1,0:T(8,128)(2,1)} %copy-done.23, bf16[4,256,384]{2,1,0:T(8,128)(2,1)} %copy-done.22, ...), custom_call_target="tpu_custom_call" | custom-call | flops 1 | bytes 1 | tf_op jit(solution)/shard_map/pallas_call | solution.py:621
  78.3 20.9 %collective-permute-done.5.d0 = bf16[1152,384]{1,0:T(8,128)(2,1)} collective-permute-done((bf16[1152,384]{1,0:T(8,128)(2,1)}, bf16[1152,384]{1,0:T(8,128)(2,1)}, u32[]{:S(2)}, u32[]{:S(2)}) %collective-permute-start.5) | collective-permute-done | bytes 884768 | tf_op jit(solution)/shard_map/ppermute | solution.py:491
  101.9 10.2 %collective-permute-done.12.v2 = bf16[384,512]{1,0:T(8,128)(2,1)S(1)} collective-permute-done((bf16[384,512]{1,0:T(8,128)(2,1)}, bf16[384,512]{1,0:T(8,128)(2,1)S(1)}, u32[]{:S(2)}, u32[]{:S(2)}) %collective-permute-start.12) | collective-permute-done | bytes 393248 | tf_op jit(solution)/shard_map/ppermute | solution.py:497
  114.8 7.3 %shard_map.282 = (bf16[4,256,768]{2,1,0:T(8,128)(2,1)}, f32[256,768]{1,0:T(8,128)}, f32[4,8,256]{2,1,0:T(8,128)}, s32[4,8,256]{2,1,0:T(8,128)}) custom-call(s32[5]{0:T(128)} %stack.29.scal, bf16[4,4,128,384]{3,2,1,0:T(8,128)(2,1)} %bitcast.164, bf16[4,2,192,384]{3,2,1,0:T(8,128)(2,1)} %bitcast.166, bf16[4,256,768]{2,1,0:T(8,128)(2,1)} %x_ref.5, ...), custom_call_target="tpu_custom_call" | custom-call | flops 1 | bytes 1 | tf_op jit(solution)/shard_map/pallas_call | solution.py:641
  122.2 8.0 %collective-permute-done.13.d2 = bf16[1152,384]{1,0:T(8,128)(2,1)} collective-permute-done((bf16[1152,384]{1,0:T(8,128)(2,1)}, bf16[1152,384]{1,0:T(8,128)(2,1)}, u32[]{:S(2)}, u32[]{:S(2)}) %collective-permute-start.13) | collective-permute-done | bytes 884768 | tf_op jit(solution)/shard_map/ppermute | solution.py:497
  133.8 10.8 %shard_map.283 = (bf16[4,256,768]{2,1,0:T(8,128)(2,1)}, bf16[4,256,768]{2,1,0:T(8,128)(2,1)}, bf16[4,256,512]{2,1,0:T(8,128)(2,1)}, bf16[4,256,1024]{2,1,0:T(8,128)(2,1)}) custom-call(s32[5]{0:T(128)} %stack.29.scal, bf16[4,256,768]{2,1,0:T(8,128)(2,1)} %get-tuple-element.189.n2_ref, bf16[4,256,768]{2,1,0:T(8,128)(2,1)} %dy_ref.7, bf16[384,512]{1,0:T(8,128)(2,1)} %go_ref.2, ...), custom_call_target="tpu_custom_call" | custom-call | flops 1 | bytes 1 | tf_op jit(solution)/shard_map/pallas_call | solution.py:673
  144.6 5.0 %all-to-all-start = ((bf16[4,256,640]{2,1,0:T(8,128)(2,1)}), bf16[4,256,640]{2,1,0:T(8,128)(2,1)S(1)}, u32[]{:S(2)}, u32[]{:S(2)}) async-start(bf16[4,256,640]{2,1,0:T(8,128)(2,1)} %get-tuple-element.180), calls=%async_computation | async-start | bytes 2621440 | tf_op jit(solution)/shard_map/all_to_all | solution.py:687
  150.6 46.8 %shard_map.284 = (bf16[4,256,768]{2,1,0:T(8,128)(2,1)}, bf16[4,272,768]{2,1,0:T(8,128)(2,1)}, bf16[4,8,288,512]{3,2,1,0:T(8,128)(2,1)}, bf16[4,8,288,512]{3,2,1,0:T(8,128)(2,1)}) custom-call(s32[5]{0:T(128)} %stack.29.scal, bf16[4,256,768]{2,1,0:T(8,128)(2,1)} %get-tuple-element.189.n2_ref, bf16[4,256,768]{2,1,0:T(8,128)(2,1)} %dy_ref.7, ...), custom_call_target="tpu_custom_call" | custom-call | flops 1 | bytes 1 | tf_op jit(solution)/shard_map/pallas_call | solution.py:709
  199.6 7.6 %shard_map.285 = (bf16[4,1,288,512]{3,2,1,0:T(8,128)(2,1)}, bf16[4,1,288,512]{3,2,1,0:T(8,128)(2,1)}) custom-call(s32[5]{0:T(128)} %stack.29.scal, bf16[4,256,768]{2,1,0:T(8,128)(2,1)} %get-tuple-element.189.n2_ref, bf16[4,256,768]{2,1,0:T(8,128)(2,1)} %dy_ref.7, bf16[4,256,512]{2,1,0:T(8,128)(2,1)} %get-tuple-element.190.hid_ref, ...), custom_call_target="tpu_custom_call" | custom-call | flops 1 | bytes 1 | tf_op jit(solution)/shard_map/pallas_call | solution.py:735
  207.7 4.8 %collective-permute-done.20 = bf16[4,8,288,512]{3,2,1,0:T(8,128)(2,1)} collective-permute-done((bf16[4,8,288,512]{3,2,1,0:T(8,128)(2,1)}, bf16[4,8,288,512]{3,2,1,0:T(8,128)(2,1)}, u32[]{:S(2)}, u32[]{:S(2)}) %collective-permute-start.20) | collective-permute-done | bytes 9437216 | tf_op jit(solution)/shard_map/ppermute | solution.py:497
  227.2 8.2 %reduce-scatter.3.cloned.1.call-done.dn_ref = bf16[1,272,768]{2,1,0:T(8,128)(2,1)} async-done(((bf16[4,272,768]{2,1,0:T(8,128)(2,1)}), bf16[1,272,768]{2,1,0:T(8,128)(2,1)}) %reduce-scatter.3.cloned.1.call-update) | async-done | bytes 417808 | tf_op jit(solution)/shard_map/reduce_scatter | solution.py:731
  235.6 4.7 %shard_map.286 = (f32[256,768]{1,0:T(8,128)}, bf16[4,128,384]{2,1,0:T(8,128)(2,1)}, bf16[256,768]{1,0:T(8,128)(2,1)}, f32[16,768]{1,0:T(8,128)}) custom-call(s32[5]{0:T(128)} %stack.29.scal, bf16[1,272,768]{2,1,0:T(8,128)(2,1)} %reduce-scatter.3.cloned.1.call-done.dn_ref, f32[4,8,256]{2,1,0:T(8,128)} %get-tuple-element.166.gates_ref, ...), custom_call_target="tpu_custom_call" | custom-call | flops 1 | bytes 1 | tf_op jit(solution)/shard_map/pallas_call | solution.py:817
  240.3 17.6 %shard_map.287 = (bf16[4,256,192]{2,1,0:T(8,128)(2,1)}, bf16[4,256,384]{2,1,0:T(8,128)(2,1)}, bf16[4,256,384]{2,1,0:T(8,128)(2,1)}, bf16[4,256,384]{2,1,0:T(8,128)(2,1)}, bf16[4,256,384]{2,1,0:T(8,128)(2,1)}) custom-call(s32[5]{0:T(128)} %stack.29.scal, s32[4]{0:T(128)} %prefix.3, bf16[4,256,640]{2,1,0:T(8,128)(2,1)} %copy-done.3, ...), custom_call_target="tpu_custom_call" | custom-call | flops 1 | bytes 1 | tf_op jit(solution)/shard_map/pallas_call | solution.py:846
  262.4 5.6 %shard_map.288 = (bf16[4,4,96,384]{3,2,1,0:T(8,128)(2,1)}, bf16[4,4,96,384]{3,2,1,0:T(8,128)(2,1)}) custom-call(s32[5]{0:T(128)} %stack.29.scal, bf16[4,256,768]{2,1,0:T(8,128)(2,1)} %get-tuple-element.230.n1_ref, bf16[4,256,192]{2,1,0:T(8,128)(2,1)} %get-tuple-element.211.dq_ref, bf16[256,768]{1,0:T(8,128)(2,1)} %get-tuple-element.215.low_ref, ...), custom_call_target="tpu_custom_call" | custom-call | flops 1 | bytes 1 | tf_op jit(solution)/shard_map/pallas_call | solution.py:873
  274.5 14.5 %collective-permute-done.27.c_ref = bf16[4,256,384]{2,1,0:T(8,128)(2,1)} collective-permute-done((bf16[4,256,384]{2,1,0:T(8,128)(2,1)S(1)}, bf16[4,256,384]{2,1,0:T(8,128)(2,1)}, u32[]{:S(2)}, u32[]{:S(2)}) %collective-permute-start.27) | collective-permute-done | bytes 786464 | tf_op jit(solution)/shard_map/ppermute | solution.py:497
  289.0 5.0 %shard_map.289.dkv_ref = bf16[4,256,384]{2,1,0:T(8,128)(2,1)} custom-call(bf16[4,256,384]{2,1,0:T(8,128)(2,1)} %get-tuple-element.222.a_ref, bf16[4,256,384]{2,1,0:T(8,128)(2,1)} %collective-permute-done.26.b_ref, bf16[4,256,384]{2,1,0:T(8,128)(2,1)} %collective-permute-done.27.c_ref, f32[256,640]{1,0:T(8,128)} %get-tuple-element.136.cos_ref, ...), custom_call_target="tpu_custom_call" | custom-call | flops 1 | bytes 1 | tf_op jit(solution)/shard_map/pallas_call | solution.py:891
  294.0 7.1 %shard_map.290 = (bf16[256,768]{1,0:T(8,128)(2,1)}, f32[16,768]{1,0:T(8,128)}) custom-call(s32[5]{0:T(128)} %stack.29.scal, bf16[4,256,192]{2,1,0:T(8,128)(2,1)} %get-tuple-element.211.dq_ref, bf16[4,256,384]{2,1,0:T(8,128)(2,1)} %shard_map.289.dkv_ref, bf16[4,176,768]{2,1,0:T(8,128)(2,1)} %bitcast.189, bf16[4,176,768]{2,1,0:T(8,128)(2,1)} %collective-permute-done.17.w1, ...), custom_call_target="tpu_custom_call" | custom-call | flops 1 | bytes 1 | tf_op jit(solution)/shard_map/pallas_call | solution.py:903
  301.4 5.7 %shard_map.291 = (bf16[4,5,96,384]{3,2,1,0:T(8,128)(2,1)}, bf16[4,5,96,384]{3,2,1,0:T(8,128)(2,1)}) custom-call(s32[5]{0:T(128)} %stack.29.scal, bf16[4,256,768]{2,1,0:T(8,128)(2,1)} %get-tuple-element.230.n1_ref, bf16[4,256,384]{2,1,0:T(8,128)(2,1)} %shard_map.289.dkv_ref, f32[16,768]{1,0:T(8,128)} %get-tuple-element.233.sums_ref), custom_call_target="tpu_custom_call" | custom-call | flops 1 | bytes 1 | tf_op jit(solution)/shard_map/pallas_call | solution.py:918
  310.6 12.7 %collective-permute-done.34 = bf16[2,1,288,512]{3,2,1,0:T(8,128)(2,1)S(1)} collective-permute-done((bf16[2,1,288,512]{3,2,1,0:T(8,128)(2,1)S(1)}, bf16[2,1,288,512]{3,2,1,0:T(8,128)(2,1)S(1)}, u32[]{:S(2)}, u32[]{:S(2)}) %collective-permute-start.34) | collective-permute-done | bytes 589856 | tf_op jit(solution)/shard_map/ppermute | solution.py:497
  342.8 16.1 %collective-permute-done.35 = bf16[2,5,96,384]{3,2,1,0:T(8,128)(2,1)} collective-permute-done((bf16[2,5,96,384]{3,2,1,0:T(8,128)(2,1)}, bf16[2,5,96,384]{3,2,1,0:T(8,128)(2,1)}, u32[]{:S(2)}, u32[]{:S(2)}) %collective-permute-start.35) | collective-permute-done | bytes 737312 | tf_op jit(solution)/shard_map/ppermute | solution.py:491
  386.9 5.0 %all-to-all-done.1 = bf16[4,96,896]{2,1,0:T(8,128)(2,1)} async-done(((bf16[4,96,896]{2,1,0:T(8,128)(2,1)}), bf16[4,96,896]{2,1,0:T(8,128)(2,1)}, u32[]{:S(2)}, u32[]{:S(2)}) %all-to-all-start.1) | async-done | bytes 688160 | tf_op jit(solution)/shard_map/all_to_all | solution.py:957
  (238 shorter events, 126.3 us)
Async XLA Ops:
  7.2 58.3 %all-gather.11.cloned.1.call-start = ((), (), s32[]{:S(2)}) async-start(), calls=%async_computation.6 | async-start | bytes 1474560 | tf_op jit(solution)/shard_map/all_gather | solution.py:574
  30.9 31.6 %collective-permute-start.3 = (bf16[1344,512]{1,0:T(8,128)(2,1)}, bf16[1344,512]{1,0:T(8,128)(2,1)S(1)}, u32[]{:S(2)}, u32[]{:S(2)}) collective-permute-start(bf16[1344,512]{1,0:T(8,128)(2,1)} %pad_maximum_fusion.2), channel_id=1, source_target_pairs={{0,16},{16,0},{1,17},{17,1},{2,18},{18,2},{3,19},{19,3},{4,20},{20... | collective-permute-start | bytes 4128776 | tf_op jit(solution)/shard_map/ppermute | solution.py:491
  34.3 80.4 %all-gather.13.cloned.1.call-start = ((), (), s32[]{:S(2)}) async-start(), calls=%async_computation.7 | async-start | bytes 1966080 | tf_op jit(solution)/shard_map/all_gather | solution.py:630
  64.0 35.3 %collective-permute-start.6 = (bf16[1344,512]{1,0:T(8,128)(2,1)S(1)}, bf16[1344,512]{1,0:T(8,128)(2,1)S(1)}, u32[]{:S(2)}, u32[]{:S(2)}) collective-permute-start(bf16[1344,512]{1,0:T(8,128)(2,1)S(1)} %collective-permute-done.3.g0.u0), channel_id=1, source_target_pairs={{0,8},{4,12},{8,0},{12,4},{1,9},{5,13},{9,1},{13,5},{2,10},{6,14},... | collective-permute-start | bytes 4128776 | tf_op jit(solution)/shard_map/ppermute | solution.py:497
  76.7 67.9 %all-gather.15.cloned.1.call-start = ((), (), s32[]{:S(2)}) async-start(), calls=%async_computation.8 | async-start | bytes 1351680 | tf_op jit(solution)/shard_map/all_gather | solution.py:640
  101.1 29.1 %collective-permute-start.13 = (bf16[1152,384]{1,0:T(8,128)(2,1)}, bf16[1152,384]{1,0:T(8,128)(2,1)}, u32[]{:S(2)}, u32[]{:S(2)}) collective-permute-start(bf16[1152,384]{1,0:T(8,128)(2,1)} %collective-permute-done.5.d0), channel_id=1, source_target_pairs={{0,8},{4,12},{8,0},{12,4},{1,9},{5,13},{9,1},{13,5},{2,10},{6,14},... | collective-permute-start | bytes 2654216 | tf_op jit(solution)/shard_map/ppermute | solution.py:497
  144.6 52.7 %all-to-all-start = ((bf16[4,256,640]{2,1,0:T(8,128)(2,1)}), bf16[4,256,640]{2,1,0:T(8,128)(2,1)S(1)}, u32[]{:S(2)}, u32[]{:S(2)}) async-start(bf16[4,256,640]{2,1,0:T(8,128)(2,1)} %get-tuple-element.180), calls=%async_computation | async-start | bytes 2621440 | tf_op jit(solution)/shard_map/all_to_all | solution.py:687
  149.7 85.7 %reduce-scatter.3.cloned.1.call-start = ((), (), s32[]{:S(2)}) async-start(), calls=%async_computation.4 | async-start | bytes 2088960 | tf_op jit(solution)/shard_map/reduce_scatter | solution.py:731
  149.7 47.7 %collective-permute-start.16 = (bf16[4,176,768]{2,1,0:T(8,128)(2,1)S(1)}, bf16[4,176,768]{2,1,0:T(8,128)(2,1)}, u32[]{:S(2)}, u32[]{:S(2)}) collective-permute-start(bf16[4,176,768]{2,1,0:T(8,128)(2,1)S(1)} %bitcast.190), channel_id=1, source_target_pairs={{0,8},{4,12},{8,0},{12,4},{1,9},{5,13},{9,1},{13,5},{2,10},{6,14},... | collective-permute-start | bytes 3244040 | tf_op jit(solution)/shard_map/ppermute | solution.py:497
  150.6 46.8 %collective-permute-start.17 = (bf16[4,176,768]{2,1,0:T(8,128)(2,1)S(1)}, bf16[4,176,768]{2,1,0:T(8,128)(2,1)}, u32[]{:S(2)}, u32[]{:S(2)}) collective-permute-start(bf16[4,176,768]{2,1,0:T(8,128)(2,1)S(1)} %bitcast.191), channel_id=1, source_target_pairs={{0,4},{4,0},{8,12},{12,8},{1,5},{5,1},{9,13},{13,9},{2,6},{6,2},{1... | collective-permute-start | bytes 3244040 | tf_op jit(solution)/shard_map/ppermute | solution.py:497
  197.9 91.1 %reduce-scatter.5.cloned.1.call-start = ((), (), s32[]{:S(2)}) async-start(), calls=%async_computation.5 | async-start | bytes 1966080 | tf_op jit(solution)/shard_map/reduce_scatter | solution.py:814
  222.2 35.8 %collective-permute-start.24 = (bf16[2,2,288,512]{3,2,1,0:T(8,128)(2,1)}, bf16[2,2,288,512]{3,2,1,0:T(8,128)(2,1)}, u32[]{:S(2)}, u32[]{:S(2)}) collective-permute-start(bf16[2,2,288,512]{3,2,1,0:T(8,128)(2,1)} %fusion.4), channel_id=1, source_target_pairs={{0,8},{4,12},{8,0},{12,4},{1,9},{5,13},{9,1},{13,5},{2,10},{6,14},... | collective-permute-start | bytes 3538952 | tf_op jit(solution)/shard_map/ppermute | solution.py:497
  223.4 34.6 %collective-permute-start.23 = (bf16[2,2,288,512]{3,2,1,0:T(8,128)(2,1)}, bf16[2,2,288,512]{3,2,1,0:T(8,128)(2,1)}, u32[]{:S(2)}, u32[]{:S(2)}) collective-permute-start(bf16[2,2,288,512]{3,2,1,0:T(8,128)(2,1)} %fusion.3), channel_id=1, source_target_pairs={{0,16},{16,0},{1,17},{17,1},{2,18},{18,2},{3,19},{19,3},{4,20},{20... | collective-permute-start | bytes 3538952 | tf_op jit(solution)/shard_map/ppermute | solution.py:491
  235.4 136.7 %all-gather.19.cloned.1.call-start = ((), (), s32[]{:S(2)}) async-start(), calls=%async_computation.10 | async-start | bytes 1966080 | tf_op jit(solution)/shard_map/all_gather | solution.py:916
  268.0 25.9 %collective-permute-start.31 = (bf16[4,176,768]{2,1,0:T(8,128)(2,1)}, bf16[4,176,768]{2,1,0:T(8,128)(2,1)}, u32[]{:S(2)}, u32[]{:S(2)}) collective-permute-start(bf16[4,176,768]{2,1,0:T(8,128)(2,1)} %collective-permute-done.16.w2), channel_id=1, source_target_pairs={{0,4},{4,0},{8,12},{12,8},{1,5},{5,1},{9,13},{13,9},{2,6},{6,2},{1... | collective-permute-start | bytes 3244040 | tf_op jit(solution)/shard_map/ppermute | solution.py:497
  269.9 60.7 %collective-permute-start.30 = (bf16[2,4,288,512]{3,2,1,0:T(8,128)(2,1)S(1)}, bf16[2,4,288,512]{3,2,1,0:T(8,128)(2,1)}, u32[]{:S(2)}, u32[]{:S(2)}) collective-permute-start(bf16[2,4,288,512]{3,2,1,0:T(8,128)(2,1)S(1)} %fusion), channel_id=1, source_target_pairs={{0,16},{16,0},{1,17},{17,1},{2,18},{18,2},{3,19},{19,3},{4,20},{20... | collective-permute-start | bytes 7077896 | tf_op jit(solution)/shard_map/ppermute | solution.py:491
  271.4 30.0 %collective-permute-start.32 = (bf16[2,288,512]{2,1,0:T(8,128)(2,1)}, bf16[2,288,512]{2,1,0:T(8,128)(2,1)}, u32[]{:S(2)}, u32[]{:S(2)}) collective-permute-start(bf16[2,288,512]{2,1,0:T(8,128)(2,1)} %get-tuple-element.316), channel_id=1, source_target_pairs={{0,8},{4,12},{8,0},{12,4},{1,9},{5,13},{9,1},{13,5},{2,10},{6,14},... | collective-permute-start | bytes 1769480 | tf_op jit(solution)/shard_map/ppermute | solution.py:497
  301.1 77.4 %all-gather.17.cloned.1.call-start = ((), (), s32[]{:S(2)}) async-start(), calls=%async_computation.9 | async-start | bytes 1966080 | tf_op jit(solution)/shard_map/all_gather | solution.py:890
  308.6 30.1 %collective-permute-start.36 = (bf16[2,288,512]{2,1,0:T(8,128)(2,1)}, bf16[2,288,512]{2,1,0:T(8,128)(2,1)}, u32[]{:S(2)}, u32[]{:S(2)}) collective-permute-start(bf16[2,288,512]{2,1,0:T(8,128)(2,1)} %get-tuple-element.315), channel_id=1, source_target_pairs={{0,16},{16,0},{1,17},{17,1},{2,18},{18,2},{3,19},{19,3},{4,20},{20... | collective-permute-start | bytes 1769480 | tf_op jit(solution)/shard_map/ppermute | solution.py:491
  310.1 25.9 %collective-permute-start.29 = (bf16[2,4,96,384]{3,2,1,0:T(8,128)(2,1)}, bf16[2,4,96,384]{3,2,1,0:T(8,128)(2,1)}, u32[]{:S(2)}, u32[]{:S(2)}) collective-permute-start(bf16[2,4,96,384]{3,2,1,0:T(8,128)(2,1)} %fusion.14), channel_id=1, source_target_pairs={{0,8},{4,12},{8,0},{12,4},{1,9},{5,13},{9,1},{13,5},{2,10},{6,14},... | collective-permute-start | bytes 1769480 | tf_op jit(solution)/shard_map/ppermute | solution.py:497
  325.4 35.4 %collective-permute-start.40 = (bf16[1,288,512]{2,1,0:T(8,128)(2,1)}, bf16[1,288,512]{2,1,0:T(8,128)(2,1)}, u32[]{:S(2)}, u32[]{:S(2)}) collective-permute-start(bf16[1,288,512]{2,1,0:T(8,128)(2,1)} %fusion.19), channel_id=1, source_target_pairs={{0,16},{16,0},{1,17},{17,1},{2,18},{18,2},{3,19},{19,3},{4,20},{20... | collective-permute-start | bytes 884744 | tf_op jit(solution)/shard_map/ppermute | solution.py:491
  330.1 28.9 %collective-permute-start.35 = (bf16[2,5,96,384]{3,2,1,0:T(8,128)(2,1)}, bf16[2,5,96,384]{3,2,1,0:T(8,128)(2,1)}, u32[]{:S(2)}, u32[]{:S(2)}) collective-permute-start(bf16[2,5,96,384]{3,2,1,0:T(8,128)(2,1)} %fusion.10), channel_id=1, source_target_pairs={{0,16},{16,0},{1,17},{17,1},{2,18},{18,2},{3,19},{19,3},{4,20},{20... | collective-permute-start | bytes 2211848 | tf_op jit(solution)/shard_map/ppermute | solution.py:491
  333.2 29.7 %collective-permute-start.39 = (bf16[4,288,512]{2,1,0:T(8,128)(2,1)S(1)}, bf16[4,288,512]{2,1,0:T(8,128)(2,1)}, u32[]{:S(2)}, u32[]{:S(2)}) collective-permute-start(bf16[4,288,512]{2,1,0:T(8,128)(2,1)S(1)} %fusion.2), channel_id=1, source_target_pairs={{0,8},{4,12},{8,0},{12,4},{1,9},{5,13},{9,1},{13,5},{2,10},{6,14},... | collective-permute-start | bytes 3538952 | tf_op jit(solution)/shard_map/ppermute | solution.py:497
  337.2 28.7 %collective-permute-start.38 = (bf16[4,96,384]{2,1,0:T(8,128)(2,1)S(1)}, bf16[4,96,384]{2,1,0:T(8,128)(2,1)S(1)}, u32[]{:S(2)}, u32[]{:S(2)}) collective-permute-start(bf16[4,96,384]{2,1,0:T(8,128)(2,1)S(1)} %fusion.16), channel_id=1, source_target_pairs={{0,16},{16,0},{1,17},{17,1},{2,18},{18,2},{3,19},{19,3},{4,20},{20... | collective-permute-start | bytes 884744 | tf_op jit(solution)/shard_map/ppermute | solution.py:491
  (61 other events, 651.5 us)
Sparse Core Ops, SparseCore 0:
  34.4 30.7 all-gather.10
  76.9 37.8 all-gather.12
  116.3 27.3 all-gather.14
  198.0 37.2 reduce-scatter.2
  237.5 34.3 reduce-scatter.4
  301.2 36.1 all-gather.18
  338.9 35.9 all-gather.16

commit v4 on v3

--- a/solution.py
+++ b/solution.py
@@ -144,7 +144,7 @@
 
 
 def silu_parts(value):
-    sigma = 1.0 / (1.0 + jnp.exp(-value))
+    sigma = 0.5 * jnp.tanh(0.5 * value) + 0.5
     return sigma, value * sigma
 
 
@@ -215,36 +215,64 @@
 
 
 def moe_kernel(
-    scal, n2_ref, dy_ref, slots_ref, gates_ref, ys_ref, dn_in_ref, go_ref, uo_ref, do_ref,
-    g0, g1, g2, g3, u0, u1, u2, u3, v0, v1, v2, v3, d0, d1, d2, d3,
-    y_ref, dn_ref, keep_ref, send_ref, wgu, wd, pick_s, ye_s, dx_s, xe_s, dy_s, de_s, gs_s, dprob_s,
+    scal, n2_ref, dy_ref, slots_ref, gates_ref, ys_ref, dn_in_ref, gate_own, up_own, down_own,
+    w0, w1, w2, w3, r0, r1, r2, r3, d0, d1, d2, d3,
+    y_ref, dn_ref, keep_ref, send_ref, wgu_s, wd_s, sems, pick_s, ye_s, dx_s, xe_s, dy_s, de_s, gs_s, dprob_s,
 ):
     step = pl.program_id(0)
     seqs, rows, width = n2_ref.shape
-    half = go_ref.shape[1]
+    hidden, half = down_own.shape[1:]
     experts = slots_ref.shape[1]
+    slot_now = step % 2
+    mine = pl.multiple_of(scal[0] * half, half)
+    other = pl.multiple_of((1 - scal[0]) * half, half)
+
+    def expert_at(index):
+        return 2 * ((index // 2) ^ scal[3]) + index % 2
+
+    def place(slot, index):
+        at = pl.ds(mine if index < 3 else other, half)
+        if index % 3 == 2:
+            return wd_s.at[slot, :, at]
+        return wgu_s.at[slot, at, pl.ds(index % 3 * hidden, hidden)]
+
+    def fetch(index):
+        slot, piece, odd = index % 2, index // 2, index % 2
+
+        def start(number, source):
+            pltpu.make_async_copy(source, place(slot, number), sems.at[slot, number]).start()
+
+        for number, ref in enumerate((gate_own, up_own, down_own)):
+            start(number, ref.at[expert_at(index)])
+        for number, (wide, rest, down) in enumerate(((w0, r0, d0), (w1, r1, d1), (w2, r2, d2), (w3, r3, d3))):
+            @pl.when(piece == number)
+            def _(wide=wide, rest=rest, down=down):
+                start(3, wide.at[pl.ds(pl.multiple_of(odd * half, half), half), :])
+                start(5, down.at[pl.ds(pl.multiple_of(odd * hidden, hidden), hidden), :])
+
+                @pl.when(odd == 0)
+                def _():
+                    start(4, wide.at[pl.ds(2 * half, half), :])
+
+                @pl.when(odd == 1)
+                def _():
+                    start(4, rest)
+
+    @pl.when(step == 0)
+    def _():
+        fetch(step)
+
+    @pl.when(step + 1 < experts)
+    def _():
+        fetch(step + 1)
 
     @pl.when(step < experts)
     def _():
-        piece = step // 2
-        expert = 2 * (piece ^ scal[3]) + step % 2
-        mine = pl.multiple_of(scal[0] * half, half)
-        other = pl.multiple_of((1 - scal[0]) * half, half)
-        hidden = go_ref.shape[2]
-        wgu[pl.ds(mine, half), :hidden] = go_ref[0]
-        wgu[pl.ds(mine, half), hidden:] = uo_ref[0]
-        wd[:, pl.ds(mine, half)] = do_ref[0]
-        arrived = ((g0, u0, v0, d0), (g1, u1, v1, d1), (g2, u2, v2, d2), (g3, u3, v3, d3))
-        for index, (g, u, v, d) in enumerate(arrived):
-            @pl.when(piece == index)
-            def _(g=g, d=d):
-                wgu[pl.ds(other, half), :hidden] = g[...]
-                wd[:, pl.ds(other, half)] = d[...]
-
-            for odd, ref in enumerate((u, v)):
-                @pl.when((piece == index) & (step % 2 == odd))
-                def _(ref=ref):
-                    wgu[pl.ds(other, half), hidden:] = ref[...]
+        expert = expert_at(step)
+        for number in range(6):
+            source = down_own.at[0] if number % 3 == 2 else gate_own.at[0]
+            pltpu.make_async_copy(source, place(slot_now, number), sems.at[slot_now, number]).wait()
+        wgu, wd = wgu_s.at[slot_now], wd_s.at[slot_now]
 
         slot_at = pl.ds(pl.multiple_of(step * SLOTS, 16), SLOTS)
         slot = lax.broadcasted_iota(jnp.int32, (SLOTS, rows), 0)
@@ -691,14 +719,6 @@
         i = jnp.minimum(i, experts - 1)
         return 2 * ((i // 2) ^ scal[3]) + i % 2
 
-    def of_expert(shape):
-        return pl.BlockSpec((1,) + shape, lambda i, scal: (expert_of(i, scal), 0, 0))
-
-    def piece_specs(shape):
-        return [
-            pl.BlockSpec(shape, lambda i, scal, p=p: (jnp.clip(i - 2 * p, 0, 1), 0)) for p in range(4)
-        ]
-
     late = pl.BlockSpec((1, rows, width), lambda i, scal: (jnp.maximum(i - experts, 0), 0, 0))
 
     dn_rows = rows + 16
@@ -710,21 +730,18 @@
         moe_kernel,
         (experts + seqs,),
         [full, full, whole((seqs, 8, rows)), whole((seqs, 8, rows)), late, late]
-        + [of_expert((half, hidden)), of_expert((half, hidden)), of_expert((hidden, half))]
-        + piece_specs((half, hidden))
-        + [pl.BlockSpec((half, hidden), lambda *_: (2, 0))] * 4
-        + [pl.BlockSpec((half, hidden), lambda *_: (0, 0))] * 4
-        + piece_specs((hidden, half)),
+        + [pl.BlockSpec(memory_space=pl.ANY)] * 15,
         [late, pl.BlockSpec((1, dn_rows, width), lambda i, *_: (jnp.maximum(i - experts, 0), 0, 0))]
         + [expert_grads] * 2,
         [shape_of((seqs, rows, width)), shape_of((seqs, dn_rows, width))]
         + [shape_of((4, experts, part_rows, hidden))] * 2,
-        weights
+        [pltpu.VMEM((2, width, 2 * hidden), BF16), pltpu.VMEM((2, hidden, width), BF16)]
+        + [pltpu.SemaphoreType.DMA((2, 6))]
         + [pltpu.VMEM((seqs, experts * SLOTS, rows), BF16)]
         + [pltpu.VMEM((seqs, experts * SLOTS, width), BF16)] * 2
         + [pltpu.VMEM((slot_rows, width), BF16)] * 3
         + [pltpu.VMEM((slot_rows, 128), F32), pltpu.VMEM((seqs, 8, rows), F32)],
-    )(scal, n2, cotangent, slots, gates, ys, dn_shared, *own[:3], *wide_p, *wide_p, *rest_p, *down_p)
+    )(scal, n2, cotangent, slots, gates, ys, dn_shared, *own[:3], *wide_p, *rest_p, *down_p)
 
     dn, qkv_seq, w_2, w_1, n2_late, *expert_group = fence([dn, qkv_seq, w_2, w_1, n2, *expert_group])
     w_pieces = (w_0, w_1, w_2, over_ctx(w_2, 1))

time: 406 us -> 402 us (level)
  transfers between devices with their start and end apart: 50 -> 50, of which waited for: 17 -> 17; matrix products, arithmetic and copies ran while one was open for 16% -> 16% of each run, Pallas kernels for 34% -> 33%
where the time goes in v4:
time: 402 us; the launch traced here: 400 us
  Pallas kernels  134 us (33%)
  waiting for transfers between devices  128 us (32%)
  other arithmetic  52.5 us (13%)
  starting transfers between devices  42.5 us (11%)
  local copies, waits for them, and re-layouts  28.9 us (7%)
  between operations  14.7 us (4%)
    ppermute x31, waiting for transfers between devices, over_ctx(): return lax.ppermute(value, 'ctx', [(i, i ^ bit) for i in range(ctx_size)])  71.3 us
    pallas_call x1, Pallas kernels, body(): call(moe_kernel, (experts + seqs,), [full, full, whole((seqs, 8, rows)),...  42.8 us
    ppermute x10, waiting for transfers between devices, over_x(): return lax.ppermute(value, 'fsdp', [(0, 1), (1, 0)])  40.3 us
    ppermute x31, starting transfers between devices, over_ctx(): return lax.ppermute(value, 'ctx', [(i, i ^ bit) for i in range(ctx_size)])  18 us
    pallas_call x1, Pallas kernels, body(): call(attn_bwd_kernel, (tp_size,), [by_step((rows, packed))] + [kv_block]...  17.6 us
    ppermute x10, starting transfers between devices, over_x(): return lax.ppermute(value, 'fsdp', [(0, 1), (1, 0)])  14.6 us
    pallas_call x1, Pallas kernels, body(): call(attn_fwd_kernel, (seqs,), [by_step((rows, head_cols))] + [by_step((r...  11.1 us
    pallas_call x1, Pallas kernels, body(): call(shared_kernel, (seqs,), [by_step((rows, width))] * 2 + [whole((half,...  10.7 us
  transfers between devices with their start and end apart: 50, of which 17 were waited for; matrix products, arithmetic and copies ran while one was open for 16% of the time, Pallas kernels for 33%

profile of v4, /device:TPU:0, one launch (start us, length us, event | category | flops | bytes accessed | tf_op | source)
XLA Modules:
  0.0 400.0 jit_solution(3150399993761837594)
XLA Ops:
  8.6 4.8 %concatenate.28.own_ref = bf16[832,384]{1,0:T(8,128)(2,1)S(1)} concatenate(bf16[192,384]{1,0:T(8,128)(2,1)} %bitcast.195, bf16[8,384]{1,0:T(8,128)(2,1)} %bitcast.199, bf16[1,384]{1,0:T(2,128)(2,1)S(1)} %broadcast_in_dim.24, bf16[1,384]{1,0:T(2,128)(2,1)S(1)} %broadcast_in_dim.25, bf16[54,384]{1,0:T(8,128)(2,1)S(1)} %broadcast_in_dim.26, bf16[192,384]{1,0:T(8,128)(2,1)} %bitcast.196, ...), dimensions={0} | concatenate | bytes 1277952 | tf_op jit(solution)/shard_map/concatenate | solution.py:527
  35.0 8.4 %shard_map.280 = (bf16[4,256,768]{2,1,0:T(8,128)(2,1)}, bf16[4,256,192]{2,1,0:T(8,128)(2,1)}, bf16[4,256,384]{2,1,0:T(8,128)(2,1)}, bf16[4,256,640]{2,1,0:T(8,12...) custom-call(s32[5]{0:T(128)} %stack.29.scal, bf16[4,256,768]{2,1,0:T(8,128)(2,1)} %x_ref.5, ...), custom_call_target="tpu_custom_call" | custom-call | flops 1 | bytes 1 | tf_op jit(solution)/shard_map/pallas_call | solution.py:605
  46.6 15.1 %collective-permute-done.1.kv2 = bf16[4,256,384]{2,1,0:T(8,128)(2,1)S(1)} collective-permute-done((bf16[4,256,384]{2,1,0:T(8,128)(2,1)}, bf16[4,256,384]{2,1,0:T(8,128)(2,1)S(1)}, u32[]{:S(2)}, u32[]{:S(2)}) %collective-permute-start.1) | collective-permute-done | bytes 786464 | tf_op jit(solution)/shard_map/ppermute | solution.py:525
  65.5 11.1 %shard_map.281 = bf16[4,128,384]{2,1,0:T(8,128)(2,1)} custom-call(s32[5]{0:T(128)} %stack.29.scal, s32[4]{0:T(128)} %prefix.3, bf16[4,256,192]{2,1,0:T(8,128)(2,1)} %get-tuple-element.147.q_ref, bf16[4,256,384]{2,1,0:T(8,128)(2,1)} %get-tuple-element.139.kv0, bf16[4,256,384]{2,1,0:T(8,128)(2,1)} %copy-done.23, bf16[4,256,384]{2,1,0:T(8,128)(2,1)} %copy-done.22, ...), custom_call_target="tpu_custom_call" | custom-call | flops 1 | bytes 1 | tf_op jit(solution)/shard_map/pallas_call | solution.py:649
  78.3 20.9 %collective-permute-done.5.d0 = bf16[1152,384]{1,0:T(8,128)(2,1)} collective-permute-done((bf16[1152,384]{1,0:T(8,128)(2,1)}, bf16[1152,384]{1,0:T(8,128)(2,1)}, u32[]{:S(2)}, u32[]{:S(2)}) %collective-permute-start.5) | collective-permute-done | bytes 884768 | tf_op jit(solution)/shard_map/ppermute | solution.py:519
  101.9 10.2 %collective-permute-done.12.r2 = bf16[384,512]{1,0:T(8,128)(2,1)S(1)} collective-permute-done((bf16[384,512]{1,0:T(8,128)(2,1)}, bf16[384,512]{1,0:T(8,128)(2,1)S(1)}, u32[]{:S(2)}, u32[]{:S(2)}) %collective-permute-start.12) | collective-permute-done | bytes 393248 | tf_op jit(solution)/shard_map/ppermute | solution.py:525
  114.8 7.3 %shard_map.282 = (bf16[4,256,768]{2,1,0:T(8,128)(2,1)}, f32[256,768]{1,0:T(8,128)}, f32[4,8,256]{2,1,0:T(8,128)}, s32[4,8,256]{2,1,0:T(8,128)}) custom-call(s32[5]{0:T(128)} %stack.29.scal, bf16[4,4,128,384]{3,2,1,0:T(8,128)(2,1)} %bitcast.164, bf16[4,2,192,384]{3,2,1,0:T(8,128)(2,1)} %bitcast.166, bf16[4,256,768]{2,1,0:T(8,128)(2,1)} %x_ref.5, ...), custom_call_target="tpu_custom_call" | custom-call | flops 1 | bytes 1 | tf_op jit(solution)/shard_map/pallas_call | solution.py:669
  122.2 8.0 %collective-permute-done.13.d2 = bf16[1152,384]{1,0:T(8,128)(2,1)} collective-permute-done((bf16[1152,384]{1,0:T(8,128)(2,1)}, bf16[1152,384]{1,0:T(8,128)(2,1)}, u32[]{:S(2)}, u32[]{:S(2)}) %collective-permute-start.13) | collective-permute-done | bytes 884768 | tf_op jit(solution)/shard_map/ppermute | solution.py:525
  133.8 10.7 %shard_map.283 = (bf16[4,256,768]{2,1,0:T(8,128)(2,1)}, bf16[4,256,768]{2,1,0:T(8,128)(2,1)}, bf16[4,256,512]{2,1,0:T(8,128)(2,1)}, bf16[4,256,1024]{2,1,0:T(8,128)(2,1)}) custom-call(s32[5]{0:T(128)} %stack.29.scal, bf16[4,256,768]{2,1,0:T(8,128)(2,1)} %get-tuple-element.189.n2_ref, bf16[4,256,768]{2,1,0:T(8,128)(2,1)} %dy_ref.7, bf16[384,512]{1,0:T(8,128)(2,1)} %go_ref.1, ...), custom_call_target="tpu_custom_call" | custom-call | flops 1 | bytes 1 | tf_op jit(solution)/shard_map/pallas_call | solution.py:701
  144.6 5.0 %all-to-all-start = ((bf16[4,256,640]{2,1,0:T(8,128)(2,1)}), bf16[4,256,640]{2,1,0:T(8,128)(2,1)S(1)}, u32[]{:S(2)}, u32[]{:S(2)}) async-start(bf16[4,256,640]{2,1,0:T(8,128)(2,1)} %get-tuple-element.180), calls=%async_computation | async-start | bytes 2621440 | tf_op jit(solution)/shard_map/all_to_all | solution.py:715
  150.5 42.8 %shard_map.284 = (bf16[4,256,768]{2,1,0:T(8,128)(2,1)}, bf16[4,272,768]{2,1,0:T(8,128)(2,1)}, bf16[4,8,288,512]{3,2,1,0:T(8,128)(2,1)}, bf16[4,8,288,512]{3,2,1,0:T(8,128)(2,1)}) custom-call(s32[5]{0:T(128)} %stack.29.scal, bf16[4,256,768]{2,1,0:T(8,128)(2,1)} %get-tuple-element.189.n2_ref, bf16[4,256,768]{2,1,0:T(8,128)(2,1)} %dy_ref.7, ...), custom_call_target="tpu_custom_call" | custom-call | flops 1 | bytes 1 | tf_op jit(solution)/shard_map/pallas_call | solution.py:729
  195.6 7.6 %shard_map.285 = (bf16[4,1,288,512]{3,2,1,0:T(8,128)(2,1)}, bf16[4,1,288,512]{3,2,1,0:T(8,128)(2,1)}) custom-call(s32[5]{0:T(128)} %stack.29.scal, bf16[4,256,768]{2,1,0:T(8,128)(2,1)} %get-tuple-element.189.n2_ref, bf16[4,256,768]{2,1,0:T(8,128)(2,1)} %dy_ref.7, bf16[4,256,512]{2,1,0:T(8,128)(2,1)} %get-tuple-element.190.hid_ref, ...), custom_call_target="tpu_custom_call" | custom-call | flops 1 | bytes 1 | tf_op jit(solution)/shard_map/pallas_call | solution.py:752
  203.7 4.8 %collective-permute-done.20 = bf16[4,8,288,512]{3,2,1,0:T(8,128)(2,1)} collective-permute-done((bf16[4,8,288,512]{3,2,1,0:T(8,128)(2,1)}, bf16[4,8,288,512]{3,2,1,0:T(8,128)(2,1)}, u32[]{:S(2)}, u32[]{:S(2)}) %collective-permute-start.20) | collective-permute-done | bytes 9437216 | tf_op jit(solution)/shard_map/ppermute | solution.py:525
  223.2 8.1 %reduce-scatter.3.cloned.1.call-done.dn_ref = bf16[1,272,768]{2,1,0:T(8,128)(2,1)} async-done(((bf16[4,272,768]{2,1,0:T(8,128)(2,1)}), bf16[1,272,768]{2,1,0:T(8,128)(2,1)}) %reduce-scatter.3.cloned.1.call-update) | async-done | bytes 417808 | tf_op jit(solution)/shard_map/reduce_scatter | solution.py:748
  231.6 4.7 %shard_map.286 = (f32[256,768]{1,0:T(8,128)}, bf16[4,128,384]{2,1,0:T(8,128)(2,1)}, bf16[256,768]{1,0:T(8,128)(2,1)}, f32[16,768]{1,0:T(8,128)}) custom-call(s32[5]{0:T(128)} %stack.29.scal, bf16[1,272,768]{2,1,0:T(8,128)(2,1)} %reduce-scatter.3.cloned.1.call-done.dn_ref, f32[4,8,256]{2,1,0:T(8,128)} %get-tuple-element.166.gates_ref, ...), custom_call_target="tpu_custom_call" | custom-call | flops 1 | bytes 1 | tf_op jit(solution)/shard_map/pallas_call | solution.py:834
  236.3 17.6 %shard_map.287 = (bf16[4,256,192]{2,1,0:T(8,128)(2,1)}, bf16[4,256,384]{2,1,0:T(8,128)(2,1)}, bf16[4,256,384]{2,1,0:T(8,128)(2,1)}, bf16[4,256,384]{2,1,0:T(8,128)(2,1)}, bf16[4,256,384]{2,1,0:T(8,128)(2,1)}) custom-call(s32[5]{0:T(128)} %stack.29.scal, s32[4]{0:T(128)} %prefix.3, bf16[4,256,640]{2,1,0:T(8,128)(2,1)} %copy-done.3, ...), custom_call_target="tpu_custom_call" | custom-call | flops 1 | bytes 1 | tf_op jit(solution)/shard_map/pallas_call | solution.py:863
  258.3 5.6 %shard_map.288 = (bf16[4,4,96,384]{3,2,1,0:T(8,128)(2,1)}, bf16[4,4,96,384]{3,2,1,0:T(8,128)(2,1)}) custom-call(s32[5]{0:T(128)} %stack.29.scal, bf16[4,256,768]{2,1,0:T(8,128)(2,1)} %get-tuple-element.230.n1_ref, bf16[4,256,192]{2,1,0:T(8,128)(2,1)} %get-tuple-element.211.dq_ref, bf16[256,768]{1,0:T(8,128)(2,1)} %get-tuple-element.215.low_ref, ...), custom_call_target="tpu_custom_call" | custom-call | flops 1 | bytes 1 | tf_op jit(solution)/shard_map/pallas_call | solution.py:890
  270.5 14.5 %collective-permute-done.27.c_ref = bf16[4,256,384]{2,1,0:T(8,128)(2,1)} collective-permute-done((bf16[4,256,384]{2,1,0:T(8,128)(2,1)S(1)}, bf16[4,256,384]{2,1,0:T(8,128)(2,1)}, u32[]{:S(2)}, u32[]{:S(2)}) %collective-permute-start.27) | collective-permute-done | bytes 786464 | tf_op jit(solution)/shard_map/ppermute | solution.py:525
  285.0 5.0 %shard_map.289.dkv_ref = bf16[4,256,384]{2,1,0:T(8,128)(2,1)} custom-call(bf16[4,256,384]{2,1,0:T(8,128)(2,1)} %get-tuple-element.222.a_ref, bf16[4,256,384]{2,1,0:T(8,128)(2,1)} %collective-permute-done.26.b_ref, bf16[4,256,384]{2,1,0:T(8,128)(2,1)} %collective-permute-done.27.c_ref, f32[256,640]{1,0:T(8,128)} %get-tuple-element.136.cos_ref, ...), custom_call_target="tpu_custom_call" | custom-call | flops 1 | bytes 1 | tf_op jit(solution)/shard_map/pallas_call | solution.py:908
  289.9 7.1 %shard_map.290 = (bf16[256,768]{1,0:T(8,128)(2,1)}, f32[16,768]{1,0:T(8,128)}) custom-call(s32[5]{0:T(128)} %stack.29.scal, bf16[4,256,192]{2,1,0:T(8,128)(2,1)} %get-tuple-element.211.dq_ref, bf16[4,256,384]{2,1,0:T(8,128)(2,1)} %shard_map.289.dkv_ref, bf16[4,176,768]{2,1,0:T(8,128)(2,1)} %bitcast.189, bf16[4,176,768]{2,1,0:T(8,128)(2,1)} %collective-permute-done.17.w1, ...), custom_call_target="tpu_custom_call" | custom-call | flops 1 | bytes 1 | tf_op jit(solution)/shard_map/pallas_call | solution.py:920
  297.4 5.7 %shard_map.291 = (bf16[4,5,96,384]{3,2,1,0:T(8,128)(2,1)}, bf16[4,5,96,384]{3,2,1,0:T(8,128)(2,1)}) custom-call(s32[5]{0:T(128)} %stack.29.scal, bf16[4,256,768]{2,1,0:T(8,128)(2,1)} %get-tuple-element.230.n1_ref, bf16[4,256,384]{2,1,0:T(8,128)(2,1)} %shard_map.289.dkv_ref, f32[16,768]{1,0:T(8,128)} %get-tuple-element.233.sums_ref), custom_call_target="tpu_custom_call" | custom-call | flops 1 | bytes 1 | tf_op jit(solution)/shard_map/pallas_call | solution.py:935
  306.6 12.7 %collective-permute-done.34 = bf16[2,1,288,512]{3,2,1,0:T(8,128)(2,1)S(1)} collective-permute-done((bf16[2,1,288,512]{3,2,1,0:T(8,128)(2,1)S(1)}, bf16[2,1,288,512]{3,2,1,0:T(8,128)(2,1)S(1)}, u32[]{:S(2)}, u32[]{:S(2)}) %collective-permute-start.34) | collective-permute-done | bytes 589856 | tf_op jit(solution)/shard_map/ppermute | solution.py:525
  338.8 16.1 %collective-permute-done.35 = bf16[2,5,96,384]{3,2,1,0:T(8,128)(2,1)} collective-permute-done((bf16[2,5,96,384]{3,2,1,0:T(8,128)(2,1)}, bf16[2,5,96,384]{3,2,1,0:T(8,128)(2,1)}, u32[]{:S(2)}, u32[]{:S(2)}) %collective-permute-start.35) | collective-permute-done | bytes 737312 | tf_op jit(solution)/shard_map/ppermute | solution.py:519
  382.9 5.0 %all-to-all-done.1 = bf16[4,96,896]{2,1,0:T(8,128)(2,1)} async-done(((bf16[4,96,896]{2,1,0:T(8,128)(2,1)}), bf16[4,96,896]{2,1,0:T(8,128)(2,1)}, u32[]{:S(2)}, u32[]{:S(2)}) %all-to-all-start.1) | async-done | bytes 688160 | tf_op jit(solution)/shard_map/all_to_all | solution.py:974
  (238 shorter events, 126.4 us)
Async XLA Ops:
  7.2 58.3 %all-gather.11.cloned.1.call-start = ((), (), s32[]{:S(2)}) async-start(), calls=%async_computation.6 | async-start | bytes 1474560 | tf_op jit(solution)/shard_map/all_gather | solution.py:602
  30.9 31.6 %collective-permute-start.3 = (bf16[1344,512]{1,0:T(8,128)(2,1)}, bf16[1344,512]{1,0:T(8,128)(2,1)S(1)}, u32[]{:S(2)}, u32[]{:S(2)}) collective-permute-start(bf16[1344,512]{1,0:T(8,128)(2,1)} %pad_maximum_fusion.2), channel_id=1, source_target_pairs={{0,16},{16,0},{1,17},{17,1},{2,18},{18,2},{3,19},{19,3},{4,20},{20... | collective-permute-start | bytes 4128776 | tf_op jit(solution)/shard_map/ppermute | solution.py:519
  34.3 80.4 %all-gather.13.cloned.1.call-start = ((), (), s32[]{:S(2)}) async-start(), calls=%async_computation.7 | async-start | bytes 1966080 | tf_op jit(solution)/shard_map/all_gather | solution.py:658
  64.0 35.3 %collective-permute-start.6 = (bf16[1344,512]{1,0:T(8,128)(2,1)S(1)}, bf16[1344,512]{1,0:T(8,128)(2,1)S(1)}, u32[]{:S(2)}, u32[]{:S(2)}) collective-permute-start(bf16[1344,512]{1,0:T(8,128)(2,1)S(1)} %collective-permute-done.3.g0.u0.w0), channel_id=1, source_target_pairs={{0,8},{4,12},{8,0},{12,4},{1,9},{5,13},{9,1},{13,5},{2,10},{6,14},... | collective-permute-start | bytes 4128776 | tf_op jit(solution)/shard_map/ppermute | solution.py:525
  76.7 67.8 %all-gather.15.cloned.1.call-start = ((), (), s32[]{:S(2)}) async-start(), calls=%async_computation.8 | async-start | bytes 1351680 | tf_op jit(solution)/shard_map/all_gather | solution.py:668
  101.1 29.1 %collective-permute-start.13 = (bf16[1152,384]{1,0:T(8,128)(2,1)}, bf16[1152,384]{1,0:T(8,128)(2,1)}, u32[]{:S(2)}, u32[]{:S(2)}) collective-permute-start(bf16[1152,384]{1,0:T(8,128)(2,1)} %collective-permute-done.5.d0), channel_id=1, source_target_pairs={{0,8},{4,12},{8,0},{12,4},{1,9},{5,13},{9,1},{13,5},{2,10},{6,14},... | collective-permute-start | bytes 2654216 | tf_op jit(solution)/shard_map/ppermute | solution.py:525
  144.6 48.8 %all-to-all-start = ((bf16[4,256,640]{2,1,0:T(8,128)(2,1)}), bf16[4,256,640]{2,1,0:T(8,128)(2,1)S(1)}, u32[]{:S(2)}, u32[]{:S(2)}) async-start(bf16[4,256,640]{2,1,0:T(8,128)(2,1)} %get-tuple-element.180), calls=%async_computation | async-start | bytes 2621440 | tf_op jit(solution)/shard_map/all_to_all | solution.py:715
  149.6 81.8 %reduce-scatter.3.cloned.1.call-start = ((), (), s32[]{:S(2)}) async-start(), calls=%async_computation.4 | async-start | bytes 2088960 | tf_op jit(solution)/shard_map/reduce_scatter | solution.py:748
  149.6 43.7 %collective-permute-start.16 = (bf16[4,176,768]{2,1,0:T(8,128)(2,1)S(1)}, bf16[4,176,768]{2,1,0:T(8,128)(2,1)}, u32[]{:S(2)}, u32[]{:S(2)}) collective-permute-start(bf16[4,176,768]{2,1,0:T(8,128)(2,1)S(1)} %bitcast.190), channel_id=1, source_target_pairs={{0,8},{4,12},{8,0},{12,4},{1,9},{5,13},{9,1},{13,5},{2,10},{6,14},... | collective-permute-start | bytes 3244040 | tf_op jit(solution)/shard_map/ppermute | solution.py:525
  150.5 42.9 %collective-permute-start.17 = (bf16[4,176,768]{2,1,0:T(8,128)(2,1)S(1)}, bf16[4,176,768]{2,1,0:T(8,128)(2,1)}, u32[]{:S(2)}, u32[]{:S(2)}) collective-permute-start(bf16[4,176,768]{2,1,0:T(8,128)(2,1)S(1)} %bitcast.191), channel_id=1, source_target_pairs={{0,4},{4,0},{8,12},{12,8},{1,5},{5,1},{9,13},{13,9},{2,6},{6,2},{1... | collective-permute-start | bytes 3244040 | tf_op jit(solution)/shard_map/ppermute | solution.py:525
  193.9 91.1 %reduce-scatter.5.cloned.1.call-start = ((), (), s32[]{:S(2)}) async-start(), calls=%async_computation.5 | async-start | bytes 1966080 | tf_op jit(solution)/shard_map/reduce_scatter | solution.py:831
  218.1 35.8 %collective-permute-start.24 = (bf16[2,2,288,512]{3,2,1,0:T(8,128)(2,1)}, bf16[2,2,288,512]{3,2,1,0:T(8,128)(2,1)}, u32[]{:S(2)}, u32[]{:S(2)}) collective-permute-start(bf16[2,2,288,512]{3,2,1,0:T(8,128)(2,1)} %fusion.4), channel_id=1, source_target_pairs={{0,8},{4,12},{8,0},{12,4},{1,9},{5,13},{9,1},{13,5},{2,10},{6,14},... | collective-permute-start | bytes 3538952 | tf_op jit(solution)/shard_map/ppermute | solution.py:525
  219.4 34.6 %collective-permute-start.23 = (bf16[2,2,288,512]{3,2,1,0:T(8,128)(2,1)}, bf16[2,2,288,512]{3,2,1,0:T(8,128)(2,1)}, u32[]{:S(2)}, u32[]{:S(2)}) collective-permute-start(bf16[2,2,288,512]{3,2,1,0:T(8,128)(2,1)} %fusion.3), channel_id=1, source_target_pairs={{0,16},{16,0},{1,17},{17,1},{2,18},{18,2},{3,19},{19,3},{4,20},{20... | collective-permute-start | bytes 3538952 | tf_op jit(solution)/shard_map/ppermute | solution.py:519
  231.4 136.7 %all-gather.19.cloned.1.call-start = ((), (), s32[]{:S(2)}) async-start(), calls=%async_computation.10 | async-start | bytes 1966080 | tf_op jit(solution)/shard_map/all_gather | solution.py:933
  264.0 25.9 %collective-permute-start.31 = (bf16[4,176,768]{2,1,0:T(8,128)(2,1)}, bf16[4,176,768]{2,1,0:T(8,128)(2,1)}, u32[]{:S(2)}, u32[]{:S(2)}) collective-permute-start(bf16[4,176,768]{2,1,0:T(8,128)(2,1)} %collective-permute-done.16.w2), channel_id=1, source_target_pairs={{0,4},{4,0},{8,12},{12,8},{1,5},{5,1},{9,13},{13,9},{2,6},{6,2},{1... | collective-permute-start | bytes 3244040 | tf_op jit(solution)/shard_map/ppermute | solution.py:525
  265.9 60.8 %collective-permute-start.30 = (bf16[2,4,288,512]{3,2,1,0:T(8,128)(2,1)S(1)}, bf16[2,4,288,512]{3,2,1,0:T(8,128)(2,1)}, u32[]{:S(2)}, u32[]{:S(2)}) collective-permute-start(bf16[2,4,288,512]{3,2,1,0:T(8,128)(2,1)S(1)} %fusion), channel_id=1, source_target_pairs={{0,16},{16,0},{1,17},{17,1},{2,18},{18,2},{3,19},{19,3},{4,20},{20... | collective-permute-start | bytes 7077896 | tf_op jit(solution)/shard_map/ppermute | solution.py:519
  267.4 30.0 %collective-permute-start.32 = (bf16[2,288,512]{2,1,0:T(8,128)(2,1)}, bf16[2,288,512]{2,1,0:T(8,128)(2,1)}, u32[]{:S(2)}, u32[]{:S(2)}) collective-permute-start(bf16[2,288,512]{2,1,0:T(8,128)(2,1)} %get-tuple-element.316), channel_id=1, source_target_pairs={{0,8},{4,12},{8,0},{12,4},{1,9},{5,13},{9,1},{13,5},{2,10},{6,14},... | collective-permute-start | bytes 1769480 | tf_op jit(solution)/shard_map/ppermute | solution.py:525
  297.0 77.4 %all-gather.17.cloned.1.call-start = ((), (), s32[]{:S(2)}) async-start(), calls=%async_computation.9 | async-start | bytes 1966080 | tf_op jit(solution)/shard_map/all_gather | solution.py:907
  304.5 30.1 %collective-permute-start.36 = (bf16[2,288,512]{2,1,0:T(8,128)(2,1)}, bf16[2,288,512]{2,1,0:T(8,128)(2,1)}, u32[]{:S(2)}, u32[]{:S(2)}) collective-permute-start(bf16[2,288,512]{2,1,0:T(8,128)(2,1)} %get-tuple-element.315), channel_id=1, source_target_pairs={{0,16},{16,0},{1,17},{17,1},{2,18},{18,2},{3,19},{19,3},{4,20},{20... | collective-permute-start | bytes 1769480 | tf_op jit(solution)/shard_map/ppermute | solution.py:519
  306.0 26.0 %collective-permute-start.29 = (bf16[2,4,96,384]{3,2,1,0:T(8,128)(2,1)}, bf16[2,4,96,384]{3,2,1,0:T(8,128)(2,1)}, u32[]{:S(2)}, u32[]{:S(2)}) collective-permute-start(bf16[2,4,96,384]{3,2,1,0:T(8,128)(2,1)} %fusion.14), channel_id=1, source_target_pairs={{0,8},{4,12},{8,0},{12,4},{1,9},{5,13},{9,1},{13,5},{2,10},{6,14},... | collective-permute-start | bytes 1769480 | tf_op jit(solution)/shard_map/ppermute | solution.py:525
  321.3 35.4 %collective-permute-start.40 = (bf16[1,288,512]{2,1,0:T(8,128)(2,1)}, bf16[1,288,512]{2,1,0:T(8,128)(2,1)}, u32[]{:S(2)}, u32[]{:S(2)}) collective-permute-start(bf16[1,288,512]{2,1,0:T(8,128)(2,1)} %fusion.19), channel_id=1, source_target_pairs={{0,16},{16,0},{1,17},{17,1},{2,18},{18,2},{3,19},{19,3},{4,20},{20... | collective-permute-start | bytes 884744 | tf_op jit(solution)/shard_map/ppermute | solution.py:519
  326.1 28.8 %collective-permute-start.35 = (bf16[2,5,96,384]{3,2,1,0:T(8,128)(2,1)}, bf16[2,5,96,384]{3,2,1,0:T(8,128)(2,1)}, u32[]{:S(2)}, u32[]{:S(2)}) collective-permute-start(bf16[2,5,96,384]{3,2,1,0:T(8,128)(2,1)} %fusion.10), channel_id=1, source_target_pairs={{0,16},{16,0},{1,17},{17,1},{2,18},{18,2},{3,19},{19,3},{4,20},{20... | collective-permute-start | bytes 2211848 | tf_op jit(solution)/shard_map/ppermute | solution.py:519
  329.1 29.7 %collective-permute-start.39 = (bf16[4,288,512]{2,1,0:T(8,128)(2,1)S(1)}, bf16[4,288,512]{2,1,0:T(8,128)(2,1)}, u32[]{:S(2)}, u32[]{:S(2)}) collective-permute-start(bf16[4,288,512]{2,1,0:T(8,128)(2,1)S(1)} %fusion.2), channel_id=1, source_target_pairs={{0,8},{4,12},{8,0},{12,4},{1,9},{5,13},{9,1},{13,5},{2,10},{6,14},... | collective-permute-start | bytes 3538952 | tf_op jit(solution)/shard_map/ppermute | solution.py:525
  333.2 28.7 %collective-permute-start.38 = (bf16[4,96,384]{2,1,0:T(8,128)(2,1)S(1)}, bf16[4,96,384]{2,1,0:T(8,128)(2,1)S(1)}, u32[]{:S(2)}, u32[]{:S(2)}) collective-permute-start(bf16[4,96,384]{2,1,0:T(8,128)(2,1)S(1)} %fusion.16), channel_id=1, source_target_pairs={{0,16},{16,0},{1,17},{17,1},{2,18},{18,2},{3,19},{19,3},{4,20},{20... | collective-permute-start | bytes 884744 | tf_op jit(solution)/shard_map/ppermute | solution.py:519
  (61 other events, 651.6 us)
Sparse Core Ops, SparseCore 0:
  34.4 30.7 all-gather.10
  76.9 37.8 all-gather.12
  116.3 27.3 all-gather.14
  194.0 37.2 reduce-scatter.2
  233.5 34.2 reduce-scatter.4
  297.2 36.1 all-gather.18
  334.9 35.9 all-gather.16

commit v5 on v4

--- a/solution.py
+++ b/solution.py
@@ -57,7 +57,11 @@
         other = pl.multiple_of((1 - scal[0]) * half, half)
         w_ref[:, pl.ds(mine, half)] = own_ref[:packed, :]
         w_ref[:, pl.ds(other, half)] = oth_ref[:packed, :]
-        swap[...] = mm_tn(rotation(packed), w_ref[...]).astype(BF16)
+        swap[...] = jnp.zeros_like(swap)
+        for head in list(range(0, 192, HD)) + list(range(256, 448, HD)):
+            middle, end = head + HD // 2, head + HD
+            swap[head:middle, :] = -w_ref[middle:end, :]
+            swap[middle:end, :] = w_ref[head:middle, :]
         small_ref[...] = w_ref[192:208, :].astype(F32)
 
     x = x_ref[0].astype(F32)
@@ -185,20 +189,25 @@
             at = pl.multiple_of(quarter * (hidden // 4), hidden // 4)
             wd[pl.ds(at, hidden // 4), pl.ds(pl.multiple_of(other, half), half)] = d[...]
 
-    n2 = n2_ref[0]
-    dy = dy_ref[0]
+    shape = n2_ref.shape[:2]
+    n2 = n2_ref[...].reshape(-1, n2_ref.shape[2])
+    dy = dy_ref[...].reshape(-1, dy_ref.shape[2])
+
+    def put(ref, value):
+        ref[...] = value.astype(BF16).reshape(shape + (value.shape[1],))
+
     both = mm(n2, wgu[...])
     gate, up = both[:, :hidden], both[:, hidden:]
     sigma, silu = silu_parts(gate)
     hid = (silu * up).astype(BF16)
-    ys_ref[0] = mm(hid, wd[...]).astype(BF16)
+    put(ys_ref, mm(hid, wd[...]))
     back = mm_nt(dy, wd[...])
     da = (back * up * (sigma * (1.0 + gate * (1.0 - sigma)))).astype(BF16)
     db = (back * silu).astype(BF16)
     dab = jnp.concatenate([da, db], axis=1)
-    dn_ref[0] = mm_nt(dab, wgu[...]).astype(BF16)
-    hid_ref[0] = hid
-    dab_ref[0] = dab
+    put(dn_ref, mm_nt(dab, wgu[...]))
+    put(hid_ref, hid)
+    put(dab_ref, dab)
 
 
 def put_all_grads(core, keep_ref, send_ref, value, upstream, hid, dab):
@@ -276,39 +285,46 @@
 
         slot_at = pl.ds(pl.multiple_of(step * SLOTS, 16), SLOTS)
         slot = lax.broadcasted_iota(jnp.int32, (SLOTS, rows), 0)
-        for s in range(seqs):
-            at = slice(s * SLOTS, (s + 1) * SLOTS)
-            hit = slots_ref[s, pl.ds(expert, 1), :] == slot
-            gate_slot = jnp.sum(jnp.where(hit, gates_ref[s, pl.ds(expert, 1), :], 0.0), 1, keepdims=True)
-            pick = hit.astype(BF16)
-            pick_s[s, slot_at, :] = pick
-            xe_s[at, :] = mm(pick, n2_ref[s]).astype(BF16)
-            upstream = mm(pick, dy_ref[s])
-            dy_s[at, :] = upstream.astype(BF16)
-            de_s[at, :] = (gate_slot * upstream).astype(BF16)
-            gs_s[at, :] = jnp.broadcast_to(gate_slot, (SLOTS, 128))
-
-        xe = xe_s[...]
+        odd = step % 2
+
+        @pl.when(odd == 0)
+        def _():
+            for s in range(seqs):
+                at = slice(s * SLOTS, (s + 1) * SLOTS)
+                hits = [slots_ref[s, pl.ds(expert + k, 1), :] == slot for k in range(2)]
+                pick = jnp.concatenate([hit.astype(BF16) for hit in hits], axis=0)
+                pick_s[s, pl.ds(pl.multiple_of(step * SLOTS, 16), 2 * SLOTS), :] = pick
+                rows_in = mm(pick, n2_ref[s]).astype(BF16)
+                upstream = mm(pick, dy_ref[s])
+                for k, hit in enumerate(hits):
+                    part = slice(k * SLOTS, (k + 1) * SLOTS)
+                    gate_slot = jnp.sum(jnp.where(hit, gates_ref[s, pl.ds(expert + k, 1), :], 0.0), 1, keepdims=True)
+                    xe_s[k, at, :] = rows_in[part]
+                    dy_s[k, at, :] = upstream[part].astype(BF16)
+                    de_s[k, at, :] = (gate_slot * upstream[part]).astype(BF16)
+                    gs_s[k, at, :] = jnp.broadcast_to(gate_slot, (SLOTS, 128))
+
+        xe = xe_s[odd]
         both = mm(xe, wgu[...])
         gate, up = both[:, :hidden], both[:, hidden:]
         sigma, silu = silu_parts(gate)
         hid = (silu * up).astype(BF16)
         ye = mm(hid, wd[...])
-        dots = jnp.sum(ye * dy_s[...].astype(F32), 1, keepdims=True)
-        ye = (ye * gs_s[:, 0:1]).astype(BF16)
+        dots = jnp.sum(ye * dy_s[odd].astype(F32), 1, keepdims=True)
+        ye = (ye * gs_s[odd][:, 0:1]).astype(BF16)
         for s in range(seqs):
             at = slice(s * SLOTS, (s + 1) * SLOTS)
             ye_s[s, slot_at, :] = ye[at]
             hit = slots_ref[s, pl.ds(expert, 1), :] == slot
             dprob_s[s, pl.ds(expert, 1), :] = jnp.sum(jnp.where(hit, dots[at], 0.0), 0, keepdims=True)
-        back = mm_nt(de_s[...], wd[...])
+        back = mm_nt(de_s[odd], wd[...])
         da = (back * up * (sigma * (1.0 + gate * (1.0 - sigma)))).astype(BF16)
         db = (back * silu).astype(BF16)
         dab = jnp.concatenate([da, db], axis=1)
         dx = mm_nt(dab, wgu[...]).astype(BF16)
         for s in range(seqs):
             dx_s[s, slot_at, :] = dx[s * SLOTS:(s + 1) * SLOTS]
-        put_all_grads(scal[4], keep_ref, send_ref, xe, de_s[...], hid, dab)
+        put_all_grads(scal[4], keep_ref, send_ref, xe, de_s[odd], hid, dab)
 
     @pl.when(step >= experts)
     def _():
@@ -698,15 +714,19 @@
     upper = [pl.BlockSpec((half // 4, hidden), lambda *_, at=at: (at, 0)) for at in (12, 13)]
     lower = pl.BlockSpec((hidden // 4, half), lambda *_: (8, 0))
     weights = [pltpu.VMEM((width, 2 * hidden), BF16), pltpu.VMEM((hidden, width), BF16)]
+
+    def by_pair(cols):
+        return pl.BlockSpec((2, rows, cols), lambda i, *_: (i, 0, 0))
+
     ys, dn_shared, *shared_hidden = call(
         shared_kernel,
-        (seqs,),
-        [by_step((rows, width))] * 2
+        (seqs // 2,),
+        [by_pair(width)] * 2
         + [whole((half, hidden)), whole((half, hidden)), whole((hidden, half))]
         + [upper[0]] * 4
         + [upper[1]] * 4
         + [lower] * 4,
-        [by_step((rows, width))] * 2 + [by_step((rows, hidden)), by_step((rows, 2 * hidden))],
+        [by_pair(width)] * 2 + [by_pair(hidden), by_pair(2 * hidden)],
         [shape_of((seqs, rows, width))] * 2 + [shape_of((seqs, rows, hidden)), shape_of((seqs, rows, 2 * hidden))],
         weights,
     )(scal, n2, cotangent, *own[3:], *wide_p, *wide_p, *down_p)
@@ -739,8 +759,8 @@
         + [pltpu.SemaphoreType.DMA((2, 6))]
         + [pltpu.VMEM((seqs, experts * SLOTS, rows), BF16)]
         + [pltpu.VMEM((seqs, experts * SLOTS, width), BF16)] * 2
-        + [pltpu.VMEM((slot_rows, width), BF16)] * 3
-        + [pltpu.VMEM((slot_rows, 128), F32), pltpu.VMEM((seqs, 8, rows), F32)],
+        + [pltpu.VMEM((2, slot_rows, width), BF16)] * 3
+        + [pltpu.VMEM((2, slot_rows, 128), F32), pltpu.VMEM((seqs, 8, rows), F32)],
     )(scal, n2, cotangent, slots, gates, ys, dn_shared, *own[:3], *wide_p, *rest_p, *down_p)
 
     dn, qkv_seq, w_2, w_1, n2_late, *expert_group = fence([dn, qkv_seq, w_2, w_1, n2, *expert_group])

time: 402 us -> 400 us (level)
  no operation moved by 1% of the time
where the time goes in v5:
time: 400 us; the launch traced here: 398 us
  Pallas kernels  131 us (33%)
  waiting for transfers between devices  129 us (32%)
  other arithmetic  52.5 us (13%)
  starting transfers between devices  42.7 us (11%)
  local copies, waits for them, and re-layouts  28.7 us (7%)
  between operations  14.7 us (4%)
    ppermute x31, waiting for transfers between devices, over_ctx(): return lax.ppermute(value, 'ctx', [(i, i ^ bit) for i in range(ctx_size)])  71.3 us
    pallas_call x1, Pallas kernels, body(): call(moe_kernel, (experts + seqs,), [full, full, whole((seqs, 8, rows)),...  41.6 us
    ppermute x10, waiting for transfers between devices, over_x(): return lax.ppermute(value, 'fsdp', [(0, 1), (1, 0)])  41.2 us
    ppermute x31, starting transfers between devices, over_ctx(): return lax.ppermute(value, 'ctx', [(i, i ^ bit) for i in range(ctx_size)])  18 us
    pallas_call x1, Pallas kernels, body(): call(attn_bwd_kernel, (tp_size,), [by_step((rows, packed))] + [kv_block]...  17.6 us
    ppermute x10, starting transfers between devices, over_x(): return lax.ppermute(value, 'fsdp', [(0, 1), (1, 0)])  14.9 us
    pallas_call x1, Pallas kernels, body(): call(attn_fwd_kernel, (seqs,), [by_step((rows, head_cols))] + [by_step((r...  11.1 us
    pallas_call x1, Pallas kernels, body(): call(shared_kernel, (seqs // 2,), [by_pair(width)] * 2 + [whole((half, hi...  10.2 us
  transfers between devices with their start and end apart: 50, of which 17 were waited for; matrix products, arithmetic and copies ran while one was open for 16% of the time, Pallas kernels for 33%

profile of v5, /device:TPU:0, one launch (start us, length us, event | category | flops | bytes accessed | tf_op | source)
XLA Modules:
  0.0 398.2 jit_solution(17085065499247082016)
XLA Ops:
  8.6 4.8 %concatenate.28.own_ref = bf16[832,384]{1,0:T(8,128)(2,1)S(1)} concatenate(bf16[192,384]{1,0:T(8,128)(2,1)} %bitcast.195, bf16[8,384]{1,0:T(8,128)(2,1)} %bitcast.199, bf16[1,384]{1,0:T(2,128)(2,1)S(1)} %broadcast_in_dim.24, bf16[1,384]{1,0:T(2,128)(2,1)S(1)} %broadcast_in_dim.25, bf16[54,384]{1,0:T(8,128)(2,1)S(1)} %broadcast_in_dim.26, bf16[192,384]{1,0:T(8,128)(2,1)} %bitcast.196, ...), dimensions={0} | concatenate | bytes 1277952 | tf_op jit(solution)/shard_map/concatenate | solution.py:543
  35.0 7.5 %shard_map.280 = (bf16[4,256,768]{2,1,0:T(8,128)(2,1)}, bf16[4,256,192]{2,1,0:T(8,128)(2,1)}, bf16[4,256,384]{2,1,0:T(8,128)(2,1)}, bf16[4,256,640]{2,1,0:T(8,12...) custom-call(s32[5]{0:T(128)} %stack.29.scal, bf16[4,256,768]{2,1,0:T(8,128)(2,1)} %x_ref.5, ...), custom_call_target="tpu_custom_call" | custom-call | flops 1 | bytes 1 | tf_op jit(solution)/shard_map/pallas_call | solution.py:621
  45.7 15.1 %collective-permute-done.1.kv2 = bf16[4,256,384]{2,1,0:T(8,128)(2,1)S(1)} collective-permute-done((bf16[4,256,384]{2,1,0:T(8,128)(2,1)}, bf16[4,256,384]{2,1,0:T(8,128)(2,1)S(1)}, u32[]{:S(2)}, u32[]{:S(2)}) %collective-permute-start.1) | collective-permute-done | bytes 786464 | tf_op jit(solution)/shard_map/ppermute | solution.py:541
  65.5 11.1 %shard_map.281 = bf16[4,128,384]{2,1,0:T(8,128)(2,1)} custom-call(s32[5]{0:T(128)} %stack.29.scal, s32[4]{0:T(128)} %prefix.3, bf16[4,256,192]{2,1,0:T(8,128)(2,1)} %get-tuple-element.147.q_ref, bf16[4,256,384]{2,1,0:T(8,128)(2,1)} %get-tuple-element.139.kv0, bf16[4,256,384]{2,1,0:T(8,128)(2,1)} %copy-done.23, bf16[4,256,384]{2,1,0:T(8,128)(2,1)} %copy-done.22, ...), custom_call_target="tpu_custom_call" | custom-call | flops 1 | bytes 1 | tf_op jit(solution)/shard_map/pallas_call | solution.py:665
  78.3 20.9 %collective-permute-done.5.d0 = bf16[1152,384]{1,0:T(8,128)(2,1)} collective-permute-done((bf16[1152,384]{1,0:T(8,128)(2,1)}, bf16[1152,384]{1,0:T(8,128)(2,1)}, u32[]{:S(2)}, u32[]{:S(2)}) %collective-permute-start.5) | collective-permute-done | bytes 884768 | tf_op jit(solution)/shard_map/ppermute | solution.py:535
  101.9 10.2 %collective-permute-done.12.r2 = bf16[384,512]{1,0:T(8,128)(2,1)S(1)} collective-permute-done((bf16[384,512]{1,0:T(8,128)(2,1)}, bf16[384,512]{1,0:T(8,128)(2,1)S(1)}, u32[]{:S(2)}, u32[]{:S(2)}) %collective-permute-start.12) | collective-permute-done | bytes 393248 | tf_op jit(solution)/shard_map/ppermute | solution.py:541
  114.8 7.3 %shard_map.282 = (bf16[4,256,768]{2,1,0:T(8,128)(2,1)}, f32[256,768]{1,0:T(8,128)}, f32[4,8,256]{2,1,0:T(8,128)}, s32[4,8,256]{2,1,0:T(8,128)}) custom-call(s32[5]{0:T(128)} %stack.29.scal, bf16[4,4,128,384]{3,2,1,0:T(8,128)(2,1)} %bitcast.164, bf16[4,2,192,384]{3,2,1,0:T(8,128)(2,1)} %bitcast.166, bf16[4,256,768]{2,1,0:T(8,128)(2,1)} %x_ref.5, ...), custom_call_target="tpu_custom_call" | custom-call | flops 1 | bytes 1 | tf_op jit(solution)/shard_map/pallas_call | solution.py:685
  122.2 8.0 %collective-permute-done.13.d2 = bf16[1152,384]{1,0:T(8,128)(2,1)} collective-permute-done((bf16[1152,384]{1,0:T(8,128)(2,1)}, bf16[1152,384]{1,0:T(8,128)(2,1)}, u32[]{:S(2)}, u32[]{:S(2)}) %collective-permute-start.13) | collective-permute-done | bytes 884768 | tf_op jit(solution)/shard_map/ppermute | solution.py:541
  133.8 10.2 %shard_map.283 = (bf16[4,256,768]{2,1,0:T(8,128)(2,1)}, bf16[4,256,768]{2,1,0:T(8,128)(2,1)}, bf16[4,256,512]{2,1,0:T(8,128)(2,1)}, bf16[4,256,1024]{2,1,0:T(8,128)(2,1)}) custom-call(s32[5]{0:T(128)} %stack.29.scal, bf16[4,256,768]{2,1,0:T(8,128)(2,1)} %get-tuple-element.189.n2_ref, bf16[4,256,768]{2,1,0:T(8,128)(2,1)} %dy_ref.7, bf16[384,512]{1,0:T(8,128)(2,1)} %go_ref.1, ...), custom_call_target="tpu_custom_call" | custom-call | flops 1 | bytes 1 | tf_op jit(solution)/shard_map/pallas_call | solution.py:721
  144.0 5.0 %all-to-all-start = ((bf16[4,256,640]{2,1,0:T(8,128)(2,1)}), bf16[4,256,640]{2,1,0:T(8,128)(2,1)S(1)}, u32[]{:S(2)}, u32[]{:S(2)}) async-start(bf16[4,256,640]{2,1,0:T(8,128)(2,1)} %get-tuple-element.180), calls=%async_computation | async-start | bytes 2621440 | tf_op jit(solution)/shard_map/all_to_all | solution.py:735
  149.9 41.6 %shard_map.284 = (bf16[4,256,768]{2,1,0:T(8,128)(2,1)}, bf16[4,272,768]{2,1,0:T(8,128)(2,1)}, bf16[4,8,288,512]{3,2,1,0:T(8,128)(2,1)}, bf16[4,8,288,512]{3,2,1,0:T(8,128)(2,1)}) custom-call(s32[5]{0:T(128)} %stack.29.scal, bf16[4,256,768]{2,1,0:T(8,128)(2,1)} %get-tuple-element.189.n2_ref, bf16[4,256,768]{2,1,0:T(8,128)(2,1)} %dy_ref.7, ...), custom_call_target="tpu_custom_call" | custom-call | flops 1 | bytes 1 | tf_op jit(solution)/shard_map/pallas_call | solution.py:749
  193.7 7.6 %shard_map.285 = (bf16[4,1,288,512]{3,2,1,0:T(8,128)(2,1)}, bf16[4,1,288,512]{3,2,1,0:T(8,128)(2,1)}) custom-call(s32[5]{0:T(128)} %stack.29.scal, bf16[4,256,768]{2,1,0:T(8,128)(2,1)} %get-tuple-element.189.n2_ref, bf16[4,256,768]{2,1,0:T(8,128)(2,1)} %dy_ref.7, bf16[4,256,512]{2,1,0:T(8,128)(2,1)} %get-tuple-element.190.hid_ref, ...), custom_call_target="tpu_custom_call" | custom-call | flops 1 | bytes 1 | tf_op jit(solution)/shard_map/pallas_call | solution.py:772
  201.8 4.9 %collective-permute-done.20 = bf16[4,8,288,512]{3,2,1,0:T(8,128)(2,1)} collective-permute-done((bf16[4,8,288,512]{3,2,1,0:T(8,128)(2,1)}, bf16[4,8,288,512]{3,2,1,0:T(8,128)(2,1)}, u32[]{:S(2)}, u32[]{:S(2)}) %collective-permute-start.20) | collective-permute-done | bytes 9437216 | tf_op jit(solution)/shard_map/ppermute | solution.py:541
  221.4 8.1 %reduce-scatter.3.cloned.1.call-done.dn_ref = bf16[1,272,768]{2,1,0:T(8,128)(2,1)} async-done(((bf16[4,272,768]{2,1,0:T(8,128)(2,1)}), bf16[1,272,768]{2,1,0:T(8,128)(2,1)}) %reduce-scatter.3.cloned.1.call-update) | async-done | bytes 417808 | tf_op jit(solution)/shard_map/reduce_scatter | solution.py:768
  229.8 4.7 %shard_map.286 = (f32[256,768]{1,0:T(8,128)}, bf16[4,128,384]{2,1,0:T(8,128)(2,1)}, bf16[256,768]{1,0:T(8,128)(2,1)}, f32[16,768]{1,0:T(8,128)}) custom-call(s32[5]{0:T(128)} %stack.29.scal, bf16[1,272,768]{2,1,0:T(8,128)(2,1)} %reduce-scatter.3.cloned.1.call-done.dn_ref, f32[4,8,256]{2,1,0:T(8,128)} %get-tuple-element.166.gates_ref, ...), custom_call_target="tpu_custom_call" | custom-call | flops 1 | bytes 1 | tf_op jit(solution)/shard_map/pallas_call | solution.py:854
  234.5 17.6 %shard_map.287 = (bf16[4,256,192]{2,1,0:T(8,128)(2,1)}, bf16[4,256,384]{2,1,0:T(8,128)(2,1)}, bf16[4,256,384]{2,1,0:T(8,128)(2,1)}, bf16[4,256,384]{2,1,0:T(8,128)(2,1)}, bf16[4,256,384]{2,1,0:T(8,128)(2,1)}) custom-call(s32[5]{0:T(128)} %stack.29.scal, s32[4]{0:T(128)} %prefix.3, bf16[4,256,640]{2,1,0:T(8,128)(2,1)} %copy-done.3, ...), custom_call_target="tpu_custom_call" | custom-call | flops 1 | bytes 1 | tf_op jit(solution)/shard_map/pallas_call | solution.py:883
  256.5 5.6 %shard_map.288 = (bf16[4,4,96,384]{3,2,1,0:T(8,128)(2,1)}, bf16[4,4,96,384]{3,2,1,0:T(8,128)(2,1)}) custom-call(s32[5]{0:T(128)} %stack.29.scal, bf16[4,256,768]{2,1,0:T(8,128)(2,1)} %get-tuple-element.230.n1_ref, bf16[4,256,192]{2,1,0:T(8,128)(2,1)} %get-tuple-element.211.dq_ref, bf16[256,768]{1,0:T(8,128)(2,1)} %get-tuple-element.215.low_ref, ...), custom_call_target="tpu_custom_call" | custom-call | flops 1 | bytes 1 | tf_op jit(solution)/shard_map/pallas_call | solution.py:910
  268.7 14.5 %collective-permute-done.27.c_ref = bf16[4,256,384]{2,1,0:T(8,128)(2,1)} collective-permute-done((bf16[4,256,384]{2,1,0:T(8,128)(2,1)S(1)}, bf16[4,256,384]{2,1,0:T(8,128)(2,1)}, u32[]{:S(2)}, u32[]{:S(2)}) %collective-permute-start.27) | collective-permute-done | bytes 786464 | tf_op jit(solution)/shard_map/ppermute | solution.py:541
  283.1 5.0 %shard_map.289.dkv_ref = bf16[4,256,384]{2,1,0:T(8,128)(2,1)} custom-call(bf16[4,256,384]{2,1,0:T(8,128)(2,1)} %get-tuple-element.222.a_ref, bf16[4,256,384]{2,1,0:T(8,128)(2,1)} %collective-permute-done.26.b_ref, bf16[4,256,384]{2,1,0:T(8,128)(2,1)} %collective-permute-done.27.c_ref, f32[256,640]{1,0:T(8,128)} %get-tuple-element.136.cos_ref, ...), custom_call_target="tpu_custom_call" | custom-call | flops 1 | bytes 1 | tf_op jit(solution)/shard_map/pallas_call | solution.py:928
  288.1 7.1 %shard_map.290 = (bf16[256,768]{1,0:T(8,128)(2,1)}, f32[16,768]{1,0:T(8,128)}) custom-call(s32[5]{0:T(128)} %stack.29.scal, bf16[4,256,192]{2,1,0:T(8,128)(2,1)} %get-tuple-element.211.dq_ref, bf16[4,256,384]{2,1,0:T(8,128)(2,1)} %shard_map.289.dkv_ref, bf16[4,176,768]{2,1,0:T(8,128)(2,1)} %bitcast.189, bf16[4,176,768]{2,1,0:T(8,128)(2,1)} %collective-permute-done.17.w1, ...), custom_call_target="tpu_custom_call" | custom-call | flops 1 | bytes 1 | tf_op jit(solution)/shard_map/pallas_call | solution.py:940
  295.5 5.7 %shard_map.291 = (bf16[4,5,96,384]{3,2,1,0:T(8,128)(2,1)}, bf16[4,5,96,384]{3,2,1,0:T(8,128)(2,1)}) custom-call(s32[5]{0:T(128)} %stack.29.scal, bf16[4,256,768]{2,1,0:T(8,128)(2,1)} %get-tuple-element.230.n1_ref, bf16[4,256,384]{2,1,0:T(8,128)(2,1)} %shard_map.289.dkv_ref, f32[16,768]{1,0:T(8,128)} %get-tuple-element.233.sums_ref), custom_call_target="tpu_custom_call" | custom-call | flops 1 | bytes 1 | tf_op jit(solution)/shard_map/pallas_call | solution.py:955
  304.7 12.7 %collective-permute-done.34 = bf16[2,1,288,512]{3,2,1,0:T(8,128)(2,1)S(1)} collective-permute-done((bf16[2,1,288,512]{3,2,1,0:T(8,128)(2,1)S(1)}, bf16[2,1,288,512]{3,2,1,0:T(8,128)(2,1)S(1)}, u32[]{:S(2)}, u32[]{:S(2)}) %collective-permute-start.34) | collective-permute-done | bytes 589856 | tf_op jit(solution)/shard_map/ppermute | solution.py:541
  337.0 16.1 %collective-permute-done.35 = bf16[2,5,96,384]{3,2,1,0:T(8,128)(2,1)} collective-permute-done((bf16[2,5,96,384]{3,2,1,0:T(8,128)(2,1)}, bf16[2,5,96,384]{3,2,1,0:T(8,128)(2,1)}, u32[]{:S(2)}, u32[]{:S(2)}) %collective-permute-start.35) | collective-permute-done | bytes 737312 | tf_op jit(solution)/shard_map/ppermute | solution.py:535
  381.1 5.0 %all-to-all-done.1 = bf16[4,96,896]{2,1,0:T(8,128)(2,1)} async-done(((bf16[4,96,896]{2,1,0:T(8,128)(2,1)}), bf16[4,96,896]{2,1,0:T(8,128)(2,1)}, u32[]{:S(2)}, u32[]{:S(2)}) %all-to-all-start.1) | async-done | bytes 688160 | tf_op jit(solution)/shard_map/all_to_all | solution.py:994
  (238 shorter events, 127.2 us)
Async XLA Ops:
  7.2 58.3 %all-gather.11.cloned.1.call-start = ((), (), s32[]{:S(2)}) async-start(), calls=%async_computation.6 | async-start | bytes 1474560 | tf_op jit(solution)/shard_map/all_gather | solution.py:618
  30.9 31.6 %collective-permute-start.3 = (bf16[1344,512]{1,0:T(8,128)(2,1)}, bf16[1344,512]{1,0:T(8,128)(2,1)S(1)}, u32[]{:S(2)}, u32[]{:S(2)}) collective-permute-start(bf16[1344,512]{1,0:T(8,128)(2,1)} %pad_maximum_fusion.2), channel_id=1, source_target_pairs={{0,16},{16,0},{1,17},{17,1},{2,18},{18,2},{3,19},{19,3},{4,20},{20... | collective-permute-start | bytes 4128776 | tf_op jit(solution)/shard_map/ppermute | solution.py:535
  34.3 80.4 %all-gather.13.cloned.1.call-start = ((), (), s32[]{:S(2)}) async-start(), calls=%async_computation.7 | async-start | bytes 1966080 | tf_op jit(solution)/shard_map/all_gather | solution.py:674
  64.0 35.3 %collective-permute-start.6 = (bf16[1344,512]{1,0:T(8,128)(2,1)S(1)}, bf16[1344,512]{1,0:T(8,128)(2,1)S(1)}, u32[]{:S(2)}, u32[]{:S(2)}) collective-permute-start(bf16[1344,512]{1,0:T(8,128)(2,1)S(1)} %collective-permute-done.3.g0.u0.w0), channel_id=1, source_target_pairs={{0,8},{4,12},{8,0},{12,4},{1,9},{5,13},{9,1},{13,5},{2,10},{6,14},... | collective-permute-start | bytes 4128776 | tf_op jit(solution)/shard_map/ppermute | solution.py:541
  76.7 67.2 %all-gather.15.cloned.1.call-start = ((), (), s32[]{:S(2)}) async-start(), calls=%async_computation.8 | async-start | bytes 1351680 | tf_op jit(solution)/shard_map/all_gather | solution.py:684
  101.1 29.1 %collective-permute-start.13 = (bf16[1152,384]{1,0:T(8,128)(2,1)}, bf16[1152,384]{1,0:T(8,128)(2,1)}, u32[]{:S(2)}, u32[]{:S(2)}) collective-permute-start(bf16[1152,384]{1,0:T(8,128)(2,1)} %collective-permute-done.5.d0), channel_id=1, source_target_pairs={{0,8},{4,12},{8,0},{12,4},{1,9},{5,13},{9,1},{13,5},{2,10},{6,14},... | collective-permute-start | bytes 2654216 | tf_op jit(solution)/shard_map/ppermute | solution.py:541
  144.0 47.6 %all-to-all-start = ((bf16[4,256,640]{2,1,0:T(8,128)(2,1)}), bf16[4,256,640]{2,1,0:T(8,128)(2,1)S(1)}, u32[]{:S(2)}, u32[]{:S(2)}) async-start(bf16[4,256,640]{2,1,0:T(8,128)(2,1)} %get-tuple-element.180), calls=%async_computation | async-start | bytes 2621440 | tf_op jit(solution)/shard_map/all_to_all | solution.py:735
  149.0 80.5 %reduce-scatter.3.cloned.1.call-start = ((), (), s32[]{:S(2)}) async-start(), calls=%async_computation.4 | async-start | bytes 2088960 | tf_op jit(solution)/shard_map/reduce_scatter | solution.py:768
  149.0 42.5 %collective-permute-start.16 = (bf16[4,176,768]{2,1,0:T(8,128)(2,1)S(1)}, bf16[4,176,768]{2,1,0:T(8,128)(2,1)}, u32[]{:S(2)}, u32[]{:S(2)}) collective-permute-start(bf16[4,176,768]{2,1,0:T(8,128)(2,1)S(1)} %bitcast.190), channel_id=1, source_target_pairs={{0,8},{4,12},{8,0},{12,4},{1,9},{5,13},{9,1},{13,5},{2,10},{6,14},... | collective-permute-start | bytes 3244040 | tf_op jit(solution)/shard_map/ppermute | solution.py:541
  149.9 41.6 %collective-permute-start.17 = (bf16[4,176,768]{2,1,0:T(8,128)(2,1)S(1)}, bf16[4,176,768]{2,1,0:T(8,128)(2,1)}, u32[]{:S(2)}, u32[]{:S(2)}) collective-permute-start(bf16[4,176,768]{2,1,0:T(8,128)(2,1)S(1)} %bitcast.191), channel_id=1, source_target_pairs={{0,4},{4,0},{8,12},{12,8},{1,5},{5,1},{9,13},{13,9},{2,6},{6,2},{1... | collective-permute-start | bytes 3244040 | tf_op jit(solution)/shard_map/ppermute | solution.py:541
  192.1 91.1 %reduce-scatter.5.cloned.1.call-start = ((), (), s32[]{:S(2)}) async-start(), calls=%async_computation.5 | async-start | bytes 1966080 | tf_op jit(solution)/shard_map/reduce_scatter | solution.py:851
  216.3 35.8 %collective-permute-start.24 = (bf16[2,2,288,512]{3,2,1,0:T(8,128)(2,1)}, bf16[2,2,288,512]{3,2,1,0:T(8,128)(2,1)}, u32[]{:S(2)}, u32[]{:S(2)}) collective-permute-start(bf16[2,2,288,512]{3,2,1,0:T(8,128)(2,1)} %fusion.4), channel_id=1, source_target_pairs={{0,8},{4,12},{8,0},{12,4},{1,9},{5,13},{9,1},{13,5},{2,10},{6,14},... | collective-permute-start | bytes 3538952 | tf_op jit(solution)/shard_map/ppermute | solution.py:541
  217.5 34.6 %collective-permute-start.23 = (bf16[2,2,288,512]{3,2,1,0:T(8,128)(2,1)}, bf16[2,2,288,512]{3,2,1,0:T(8,128)(2,1)}, u32[]{:S(2)}, u32[]{:S(2)}) collective-permute-start(bf16[2,2,288,512]{3,2,1,0:T(8,128)(2,1)} %fusion.3), channel_id=1, source_target_pairs={{0,16},{16,0},{1,17},{17,1},{2,18},{18,2},{3,19},{19,3},{4,20},{20... | collective-permute-start | bytes 3538952 | tf_op jit(solution)/shard_map/ppermute | solution.py:535
  229.5 136.7 %all-gather.19.cloned.1.call-start = ((), (), s32[]{:S(2)}) async-start(), calls=%async_computation.10 | async-start | bytes 1966080 | tf_op jit(solution)/shard_map/all_gather | solution.py:953
  262.2 25.9 %collective-permute-start.31 = (bf16[4,176,768]{2,1,0:T(8,128)(2,1)}, bf16[4,176,768]{2,1,0:T(8,128)(2,1)}, u32[]{:S(2)}, u32[]{:S(2)}) collective-permute-start(bf16[4,176,768]{2,1,0:T(8,128)(2,1)} %collective-permute-done.16.w2), channel_id=1, source_target_pairs={{0,4},{4,0},{8,12},{12,8},{1,5},{5,1},{9,13},{13,9},{2,6},{6,2},{1... | collective-permute-start | bytes 3244040 | tf_op jit(solution)/shard_map/ppermute | solution.py:541
  264.1 60.8 %collective-permute-start.30 = (bf16[2,4,288,512]{3,2,1,0:T(8,128)(2,1)S(1)}, bf16[2,4,288,512]{3,2,1,0:T(8,128)(2,1)}, u32[]{:S(2)}, u32[]{:S(2)}) collective-permute-start(bf16[2,4,288,512]{3,2,1,0:T(8,128)(2,1)S(1)} %fusion), channel_id=1, source_target_pairs={{0,16},{16,0},{1,17},{17,1},{2,18},{18,2},{3,19},{19,3},{4,20},{20... | collective-permute-start | bytes 7077896 | tf_op jit(solution)/shard_map/ppermute | solution.py:535
  265.5 30.0 %collective-permute-start.32 = (bf16[2,288,512]{2,1,0:T(8,128)(2,1)}, bf16[2,288,512]{2,1,0:T(8,128)(2,1)}, u32[]{:S(2)}, u32[]{:S(2)}) collective-permute-start(bf16[2,288,512]{2,1,0:T(8,128)(2,1)} %get-tuple-element.316), channel_id=1, source_target_pairs={{0,8},{4,12},{8,0},{12,4},{1,9},{5,13},{9,1},{13,5},{2,10},{6,14},... | collective-permute-start | bytes 1769480 | tf_op jit(solution)/shard_map/ppermute | solution.py:541
  295.2 77.4 %all-gather.17.cloned.1.call-start = ((), (), s32[]{:S(2)}) async-start(), calls=%async_computation.9 | async-start | bytes 1966080 | tf_op jit(solution)/shard_map/all_gather | solution.py:927
  302.7 30.1 %collective-permute-start.36 = (bf16[2,288,512]{2,1,0:T(8,128)(2,1)}, bf16[2,288,512]{2,1,0:T(8,128)(2,1)}, u32[]{:S(2)}, u32[]{:S(2)}) collective-permute-start(bf16[2,288,512]{2,1,0:T(8,128)(2,1)} %get-tuple-element.315), channel_id=1, source_target_pairs={{0,16},{16,0},{1,17},{17,1},{2,18},{18,2},{3,19},{19,3},{4,20},{20... | collective-permute-start | bytes 1769480 | tf_op jit(solution)/shard_map/ppermute | solution.py:535
  304.2 26.0 %collective-permute-start.29 = (bf16[2,4,96,384]{3,2,1,0:T(8,128)(2,1)}, bf16[2,4,96,384]{3,2,1,0:T(8,128)(2,1)}, u32[]{:S(2)}, u32[]{:S(2)}) collective-permute-start(bf16[2,4,96,384]{3,2,1,0:T(8,128)(2,1)} %fusion.14), channel_id=1, source_target_pairs={{0,8},{4,12},{8,0},{12,4},{1,9},{5,13},{9,1},{13,5},{2,10},{6,14},... | collective-permute-start | bytes 1769480 | tf_op jit(solution)/shard_map/ppermute | solution.py:541
  319.5 35.4 %collective-permute-start.40 = (bf16[1,288,512]{2,1,0:T(8,128)(2,1)}, bf16[1,288,512]{2,1,0:T(8,128)(2,1)}, u32[]{:S(2)}, u32[]{:S(2)}) collective-permute-start(bf16[1,288,512]{2,1,0:T(8,128)(2,1)} %fusion.19), channel_id=1, source_target_pairs={{0,16},{16,0},{1,17},{17,1},{2,18},{18,2},{3,19},{19,3},{4,20},{20... | collective-permute-start | bytes 884744 | tf_op jit(solution)/shard_map/ppermute | solution.py:535
  324.2 28.8 %collective-permute-start.35 = (bf16[2,5,96,384]{3,2,1,0:T(8,128)(2,1)}, bf16[2,5,96,384]{3,2,1,0:T(8,128)(2,1)}, u32[]{:S(2)}, u32[]{:S(2)}) collective-permute-start(bf16[2,5,96,384]{3,2,1,0:T(8,128)(2,1)} %fusion.10), channel_id=1, source_target_pairs={{0,16},{16,0},{1,17},{17,1},{2,18},{18,2},{3,19},{19,3},{4,20},{20... | collective-permute-start | bytes 2211848 | tf_op jit(solution)/shard_map/ppermute | solution.py:535
  327.3 29.7 %collective-permute-start.39 = (bf16[4,288,512]{2,1,0:T(8,128)(2,1)S(1)}, bf16[4,288,512]{2,1,0:T(8,128)(2,1)}, u32[]{:S(2)}, u32[]{:S(2)}) collective-permute-start(bf16[4,288,512]{2,1,0:T(8,128)(2,1)S(1)} %fusion.2), channel_id=1, source_target_pairs={{0,8},{4,12},{8,0},{12,4},{1,9},{5,13},{9,1},{13,5},{2,10},{6,14},... | collective-permute-start | bytes 3538952 | tf_op jit(solution)/shard_map/ppermute | solution.py:541
  331.3 28.7 %collective-permute-start.38 = (bf16[4,96,384]{2,1,0:T(8,128)(2,1)S(1)}, bf16[4,96,384]{2,1,0:T(8,128)(2,1)S(1)}, u32[]{:S(2)}, u32[]{:S(2)}) collective-permute-start(bf16[4,96,384]{2,1,0:T(8,128)(2,1)S(1)} %fusion.16), channel_id=1, source_target_pairs={{0,16},{16,0},{1,17},{17,1},{2,18},{18,2},{3,19},{19,3},{4,20},{20... | collective-permute-start | bytes 884744 | tf_op jit(solution)/shard_map/ppermute | solution.py:535
  (61 other events, 653.4 us)
Sparse Core Ops, SparseCore 0:
  34.4 30.7 all-gather.10
  76.9 37.8 all-gather.12
  116.3 27.3 all-gather.14
  192.2 37.2 reduce-scatter.2
  231.7 34.2 reduce-scatter.4
  295.3 36.1 all-gather.18
  333.1 35.9 all-gather.16

commit v6 on v5

--- a/solution.py
+++ b/solution.py
@@ -96,7 +96,7 @@
     heads = width // HD
     kv = jnp.concatenate([kv0[0], kv1[0], kv2[0], kv3[0]], axis=0)
     k = kv[:, :width]
-    value_t = jnp.transpose(kv[:, width:].astype(F32)).astype(BF16)
+    value_t = jnp.transpose(kv[:, width:])
     seen = visible(scal, prefix[pl.program_id(0)], kv.shape[0], rows)
     outs = []
     for head in range(heads):
@@ -374,7 +374,7 @@
     kv = jnp.concatenate([kv0[0], kv1[0], kv2[0], kv3[0]], axis=0)
     k = kv[:, :width]
     v = kv[:, width:]
-    key_t = jnp.transpose(k.astype(F32)).astype(BF16)
+    key_t = jnp.transpose(k)
     do = jnp.concatenate([do_ref[0][:, :width], do_ref[0][:, width:]], axis=0)
     seen = visible(scal, prefix[scal[2]], kv.shape[0], rows)
     cosine, sine = cos_ref[...], sin_ref[...]
@@ -837,7 +837,7 @@
         cuts = ((0, 2, True), (2, 2, False), (4, 4, False))
         sums_of = [Sum(expert_group[0], got, y_first, first, count) for first, count, y_first in cuts]
         sums_of.append(Sum(shared_group[0], shared_got, True))
-        sent = [sums_of[1].first(), sums_of[0].first()]
+        sent = [sums_of[0].first(), sums_of[1].first()]
         sums_of[2].fence(*sent)
         sent.append(sums_of[2].first())
         (kv_seq_2,) = fence([kv_seq_2], *sent)

time: 400 us -> 400 us (level)
  no operation moved by 1% of the time
where the time goes in v6:
time: 400 us; the launch traced here: 398 us
  Pallas kernels  131 us (33%)
  waiting for transfers between devices  129 us (32%)
  other arithmetic  52.5 us (13%)
  starting transfers between devices  42.7 us (11%)
  local copies, waits for them, and re-layouts  28.7 us (7%)
  between operations  14.7 us (4%)
    ppermute x31, waiting for transfers between devices, over_ctx(): return lax.ppermute(value, 'ctx', [(i, i ^ bit) for i in range(ctx_size)])  71.3 us
    pallas_call x1, Pallas kernels, body(): call(moe_kernel, (experts + seqs,), [full, full, whole((seqs, 8, rows)),...  41.6 us
    ppermute x10, waiting for transfers between devices, over_x(): return lax.ppermute(value, 'fsdp', [(0, 1), (1, 0)])  41.2 us
    pallas_call x1, Pallas kernels, body(): call(attn_bwd_kernel, (tp_size,), [by_step((rows, packed))] + [kv_block]...  17.6 us
    ppermute x31, starting transfers between devices, over_ctx(): return lax.ppermute(value, 'ctx', [(i, i ^ bit) for i in range(ctx_size)])  17.3 us
    ppermute x10, starting transfers between devices, over_x(): return lax.ppermute(value, 'fsdp', [(0, 1), (1, 0)])  15.5 us
    pallas_call x1, Pallas kernels, body(): call(attn_fwd_kernel, (seqs,), [by_step((rows, head_cols))] + [by_step((r...  10.9 us
    pallas_call x1, Pallas kernels, body(): call(shared_kernel, (seqs // 2,), [by_pair(width)] * 2 + [whole((half, hi...  10.2 us
  transfers between devices with their start and end apart: 50, of which 17 were waited for; matrix products, arithmetic and copies ran while one was open for 16% of the time, Pallas kernels for 33%

profile of v6, /device:TPU:0, one launch (start us, length us, event | category | flops | bytes accessed | tf_op | source)
XLA Modules:
  0.0 397.9 jit_solution(7690600422923768091)
XLA Ops:
  8.6 4.8 %concatenate.28.own_ref = bf16[832,384]{1,0:T(8,128)(2,1)S(1)} concatenate(bf16[192,384]{1,0:T(8,128)(2,1)} %bitcast.195, bf16[8,384]{1,0:T(8,128)(2,1)} %bitcast.199, bf16[1,384]{1,0:T(2,128)(2,1)S(1)} %broadcast_in_dim.24, bf16[1,384]{1,0:T(2,128)(2,1)S(1)} %broadcast_in_dim.25, bf16[54,384]{1,0:T(8,128)(2,1)S(1)} %broadcast_in_dim.26, bf16[192,384]{1,0:T(8,128)(2,1)} %bitcast.196, ...), dimensions={0} | concatenate | bytes 1277952 | tf_op jit(solution)/shard_map/concatenate | solution.py:543
  35.0 7.5 %shard_map.280 = (bf16[4,256,768]{2,1,0:T(8,128)(2,1)}, bf16[4,256,192]{2,1,0:T(8,128)(2,1)}, bf16[4,256,384]{2,1,0:T(8,128)(2,1)}, bf16[4,256,640]{2,1,0:T(8,12...) custom-call(s32[5]{0:T(128)} %stack.29.scal, bf16[4,256,768]{2,1,0:T(8,128)(2,1)} %x_ref.5, ...), custom_call_target="tpu_custom_call" | custom-call | flops 1 | bytes 1 | tf_op jit(solution)/shard_map/pallas_call | solution.py:621
  45.7 15.1 %collective-permute-done.1.kv2 = bf16[4,256,384]{2,1,0:T(8,128)(2,1)S(1)} collective-permute-done((bf16[4,256,384]{2,1,0:T(8,128)(2,1)}, bf16[4,256,384]{2,1,0:T(8,128)(2,1)S(1)}, u32[]{:S(2)}, u32[]{:S(2)}) %collective-permute-start.1) | collective-permute-done | bytes 786464 | tf_op jit(solution)/shard_map/ppermute | solution.py:541
  65.5 10.9 %shard_map.281 = bf16[4,128,384]{2,1,0:T(8,128)(2,1)} custom-call(s32[5]{0:T(128)} %stack.29.scal, s32[4]{0:T(128)} %prefix.3, bf16[4,256,192]{2,1,0:T(8,128)(2,1)} %get-tuple-element.147.q_ref, bf16[4,256,384]{2,1,0:T(8,128)(2,1)} %get-tuple-element.139.kv0, bf16[4,256,384]{2,1,0:T(8,128)(2,1)} %copy-done.23, bf16[4,256,384]{2,1,0:T(8,128)(2,1)} %copy-done.22, ...), custom_call_target="tpu_custom_call" | custom-call | flops 1 | bytes 1 | tf_op jit(solution)/shard_map/pallas_call | solution.py:665
  78.0 20.9 %collective-permute-done.5.d0 = bf16[1152,384]{1,0:T(8,128)(2,1)} collective-permute-done((bf16[1152,384]{1,0:T(8,128)(2,1)}, bf16[1152,384]{1,0:T(8,128)(2,1)}, u32[]{:S(2)}, u32[]{:S(2)}) %collective-permute-start.5) | collective-permute-done | bytes 884768 | tf_op jit(solution)/shard_map/ppermute | solution.py:535
  101.6 10.2 %collective-permute-done.12.r2 = bf16[384,512]{1,0:T(8,128)(2,1)S(1)} collective-permute-done((bf16[384,512]{1,0:T(8,128)(2,1)}, bf16[384,512]{1,0:T(8,128)(2,1)S(1)}, u32[]{:S(2)}, u32[]{:S(2)}) %collective-permute-start.12) | collective-permute-done | bytes 393248 | tf_op jit(solution)/shard_map/ppermute | solution.py:541
  114.5 7.3 %shard_map.282 = (bf16[4,256,768]{2,1,0:T(8,128)(2,1)}, f32[256,768]{1,0:T(8,128)}, f32[4,8,256]{2,1,0:T(8,128)}, s32[4,8,256]{2,1,0:T(8,128)}) custom-call(s32[5]{0:T(128)} %stack.29.scal, bf16[4,4,128,384]{3,2,1,0:T(8,128)(2,1)} %bitcast.164, bf16[4,2,192,384]{3,2,1,0:T(8,128)(2,1)} %bitcast.166, bf16[4,256,768]{2,1,0:T(8,128)(2,1)} %x_ref.5, ...), custom_call_target="tpu_custom_call" | custom-call | flops 1 | bytes 1 | tf_op jit(solution)/shard_map/pallas_call | solution.py:685
  121.9 8.0 %collective-permute-done.13.d2 = bf16[1152,384]{1,0:T(8,128)(2,1)} collective-permute-done((bf16[1152,384]{1,0:T(8,128)(2,1)}, bf16[1152,384]{1,0:T(8,128)(2,1)}, u32[]{:S(2)}, u32[]{:S(2)}) %collective-permute-start.13) | collective-permute-done | bytes 884768 | tf_op jit(solution)/shard_map/ppermute | solution.py:541
  133.5 10.2 %shard_map.283 = (bf16[4,256,768]{2,1,0:T(8,128)(2,1)}, bf16[4,256,768]{2,1,0:T(8,128)(2,1)}, bf16[4,256,512]{2,1,0:T(8,128)(2,1)}, bf16[4,256,1024]{2,1,0:T(8,128)(2,1)}) custom-call(s32[5]{0:T(128)} %stack.29.scal, bf16[4,256,768]{2,1,0:T(8,128)(2,1)} %get-tuple-element.189.n2_ref, bf16[4,256,768]{2,1,0:T(8,128)(2,1)} %dy_ref.7, bf16[384,512]{1,0:T(8,128)(2,1)} %go_ref.1, ...), custom_call_target="tpu_custom_call" | custom-call | flops 1 | bytes 1 | tf_op jit(solution)/shard_map/pallas_call | solution.py:721
  143.7 5.0 %all-to-all-start = ((bf16[4,256,640]{2,1,0:T(8,128)(2,1)}), bf16[4,256,640]{2,1,0:T(8,128)(2,1)S(1)}, u32[]{:S(2)}, u32[]{:S(2)}) async-start(bf16[4,256,640]{2,1,0:T(8,128)(2,1)} %get-tuple-element.180), calls=%async_computation | async-start | bytes 2621440 | tf_op jit(solution)/shard_map/all_to_all | solution.py:735
  149.6 41.6 %shard_map.284 = (bf16[4,256,768]{2,1,0:T(8,128)(2,1)}, bf16[4,272,768]{2,1,0:T(8,128)(2,1)}, bf16[4,8,288,512]{3,2,1,0:T(8,128)(2,1)}, bf16[4,8,288,512]{3,2,1,0:T(8,128)(2,1)}) custom-call(s32[5]{0:T(128)} %stack.29.scal, bf16[4,256,768]{2,1,0:T(8,128)(2,1)} %get-tuple-element.189.n2_ref, bf16[4,256,768]{2,1,0:T(8,128)(2,1)} %dy_ref.7, ...), custom_call_target="tpu_custom_call" | custom-call | flops 1 | bytes 1 | tf_op jit(solution)/shard_map/pallas_call | solution.py:749
  193.5 7.6 %shard_map.285 = (bf16[4,1,288,512]{3,2,1,0:T(8,128)(2,1)}, bf16[4,1,288,512]{3,2,1,0:T(8,128)(2,1)}) custom-call(s32[5]{0:T(128)} %stack.29.scal, bf16[4,256,768]{2,1,0:T(8,128)(2,1)} %get-tuple-element.189.n2_ref, bf16[4,256,768]{2,1,0:T(8,128)(2,1)} %dy_ref.7, bf16[4,256,512]{2,1,0:T(8,128)(2,1)} %get-tuple-element.190.hid_ref, ...), custom_call_target="tpu_custom_call" | custom-call | flops 1 | bytes 1 | tf_op jit(solution)/shard_map/pallas_call | solution.py:772
  201.6 4.8 %collective-permute-done.20 = bf16[4,8,288,512]{3,2,1,0:T(8,128)(2,1)} collective-permute-done((bf16[4,8,288,512]{3,2,1,0:T(8,128)(2,1)}, bf16[4,8,288,512]{3,2,1,0:T(8,128)(2,1)}, u32[]{:S(2)}, u32[]{:S(2)}) %collective-permute-start.20) | collective-permute-done | bytes 9437216 | tf_op jit(solution)/shard_map/ppermute | solution.py:541
  221.1 8.1 %reduce-scatter.3.cloned.1.call-done.dn_ref = bf16[1,272,768]{2,1,0:T(8,128)(2,1)} async-done(((bf16[4,272,768]{2,1,0:T(8,128)(2,1)}), bf16[1,272,768]{2,1,0:T(8,128)(2,1)}) %reduce-scatter.3.cloned.1.call-update) | async-done | bytes 417808 | tf_op jit(solution)/shard_map/reduce_scatter | solution.py:768
  229.5 4.7 %shard_map.286 = (f32[256,768]{1,0:T(8,128)}, bf16[4,128,384]{2,1,0:T(8,128)(2,1)}, bf16[256,768]{1,0:T(8,128)(2,1)}, f32[16,768]{1,0:T(8,128)}) custom-call(s32[5]{0:T(128)} %stack.29.scal, bf16[1,272,768]{2,1,0:T(8,128)(2,1)} %reduce-scatter.3.cloned.1.call-done.dn_ref, f32[4,8,256]{2,1,0:T(8,128)} %get-tuple-element.166.gates_ref, ...), custom_call_target="tpu_custom_call" | custom-call | flops 1 | bytes 1 | tf_op jit(solution)/shard_map/pallas_call | solution.py:854
  234.2 17.6 %shard_map.287 = (bf16[4,256,192]{2,1,0:T(8,128)(2,1)}, bf16[4,256,384]{2,1,0:T(8,128)(2,1)}, bf16[4,256,384]{2,1,0:T(8,128)(2,1)}, bf16[4,256,384]{2,1,0:T(8,128)(2,1)}, bf16[4,256,384]{2,1,0:T(8,128)(2,1)}) custom-call(s32[5]{0:T(128)} %stack.29.scal, s32[4]{0:T(128)} %prefix.3, bf16[4,256,640]{2,1,0:T(8,128)(2,1)} %copy-done.3, ...), custom_call_target="tpu_custom_call" | custom-call | flops 1 | bytes 1 | tf_op jit(solution)/shard_map/pallas_call | solution.py:883
  256.2 5.6 %shard_map.288 = (bf16[4,4,96,384]{3,2,1,0:T(8,128)(2,1)}, bf16[4,4,96,384]{3,2,1,0:T(8,128)(2,1)}) custom-call(s32[5]{0:T(128)} %stack.29.scal, bf16[4,256,768]{2,1,0:T(8,128)(2,1)} %get-tuple-element.230.n1_ref, bf16[4,256,192]{2,1,0:T(8,128)(2,1)} %get-tuple-element.211.dq_ref, bf16[256,768]{1,0:T(8,128)(2,1)} %get-tuple-element.215.low_ref, ...), custom_call_target="tpu_custom_call" | custom-call | flops 1 | bytes 1 | tf_op jit(solution)/shard_map/pallas_call | solution.py:910
  268.3 14.5 %collective-permute-done.27.c_ref = bf16[4,256,384]{2,1,0:T(8,128)(2,1)} collective-permute-done((bf16[4,256,384]{2,1,0:T(8,128)(2,1)S(1)}, bf16[4,256,384]{2,1,0:T(8,128)(2,1)}, u32[]{:S(2)}, u32[]{:S(2)}) %collective-permute-start.27) | collective-permute-done | bytes 786464 | tf_op jit(solution)/shard_map/ppermute | solution.py:541
  282.8 5.0 %shard_map.289.dkv_ref = bf16[4,256,384]{2,1,0:T(8,128)(2,1)} custom-call(bf16[4,256,384]{2,1,0:T(8,128)(2,1)} %get-tuple-element.222.a_ref, bf16[4,256,384]{2,1,0:T(8,128)(2,1)} %collective-permute-done.26.b_ref, bf16[4,256,384]{2,1,0:T(8,128)(2,1)} %collective-permute-done.27.c_ref, f32[256,640]{1,0:T(8,128)} %get-tuple-element.136.cos_ref, ...), custom_call_target="tpu_custom_call" | custom-call | flops 1 | bytes 1 | tf_op jit(solution)/shard_map/pallas_call | solution.py:928
  287.8 7.1 %shard_map.290 = (bf16[256,768]{1,0:T(8,128)(2,1)}, f32[16,768]{1,0:T(8,128)}) custom-call(s32[5]{0:T(128)} %stack.29.scal, bf16[4,256,192]{2,1,0:T(8,128)(2,1)} %get-tuple-element.211.dq_ref, bf16[4,256,384]{2,1,0:T(8,128)(2,1)} %shard_map.289.dkv_ref, bf16[4,176,768]{2,1,0:T(8,128)(2,1)} %bitcast.189, bf16[4,176,768]{2,1,0:T(8,128)(2,1)} %collective-permute-done.17.w1, ...), custom_call_target="tpu_custom_call" | custom-call | flops 1 | bytes 1 | tf_op jit(solution)/shard_map/pallas_call | solution.py:940
  295.2 5.7 %shard_map.291 = (bf16[4,5,96,384]{3,2,1,0:T(8,128)(2,1)}, bf16[4,5,96,384]{3,2,1,0:T(8,128)(2,1)}) custom-call(s32[5]{0:T(128)} %stack.29.scal, bf16[4,256,768]{2,1,0:T(8,128)(2,1)} %get-tuple-element.230.n1_ref, bf16[4,256,384]{2,1,0:T(8,128)(2,1)} %shard_map.289.dkv_ref, f32[16,768]{1,0:T(8,128)} %get-tuple-element.233.sums_ref), custom_call_target="tpu_custom_call" | custom-call | flops 1 | bytes 1 | tf_op jit(solution)/shard_map/pallas_call | solution.py:955
  304.4 12.7 %collective-permute-done.34 = bf16[2,1,288,512]{3,2,1,0:T(8,128)(2,1)S(1)} collective-permute-done((bf16[2,1,288,512]{3,2,1,0:T(8,128)(2,1)S(1)}, bf16[2,1,288,512]{3,2,1,0:T(8,128)(2,1)S(1)}, u32[]{:S(2)}, u32[]{:S(2)}) %collective-permute-start.34) | collective-permute-done | bytes 589856 | tf_op jit(solution)/shard_map/ppermute | solution.py:541
  336.6 16.1 %collective-permute-done.35 = bf16[2,5,96,384]{3,2,1,0:T(8,128)(2,1)} collective-permute-done((bf16[2,5,96,384]{3,2,1,0:T(8,128)(2,1)}, bf16[2,5,96,384]{3,2,1,0:T(8,128)(2,1)}, u32[]{:S(2)}, u32[]{:S(2)}) %collective-permute-start.35) | collective-permute-done | bytes 737312 | tf_op jit(solution)/shard_map/ppermute | solution.py:535
  380.7 5.1 %all-to-all-done.1 = bf16[4,96,896]{2,1,0:T(8,128)(2,1)} async-done(((bf16[4,96,896]{2,1,0:T(8,128)(2,1)}), bf16[4,96,896]{2,1,0:T(8,128)(2,1)}, u32[]{:S(2)}, u32[]{:S(2)}) %all-to-all-start.1) | async-done | bytes 688160 | tf_op jit(solution)/shard_map/all_to_all | solution.py:994
  (238 shorter events, 127.2 us)
Async XLA Ops:
  7.2 58.3 %all-gather.11.cloned.1.call-start = ((), (), s32[]{:S(2)}) async-start(), calls=%async_computation.6 | async-start | bytes 1474560 | tf_op jit(solution)/shard_map/all_gather | solution.py:618
  30.9 31.6 %collective-permute-start.3 = (bf16[1344,512]{1,0:T(8,128)(2,1)}, bf16[1344,512]{1,0:T(8,128)(2,1)S(1)}, u32[]{:S(2)}, u32[]{:S(2)}) collective-permute-start(bf16[1344,512]{1,0:T(8,128)(2,1)} %pad_maximum_fusion.2), channel_id=1, source_target_pairs={{0,16},{16,0},{1,17},{17,1},{2,18},{18,2},{3,19},{19,3},{4,20},{20... | collective-permute-start | bytes 4128776 | tf_op jit(solution)/shard_map/ppermute | solution.py:535
  34.3 80.1 %all-gather.13.cloned.1.call-start = ((), (), s32[]{:S(2)}) async-start(), calls=%async_computation.7 | async-start | bytes 1966080 | tf_op jit(solution)/shard_map/all_gather | solution.py:674
  64.0 35.0 %collective-permute-start.6 = (bf16[1344,512]{1,0:T(8,128)(2,1)S(1)}, bf16[1344,512]{1,0:T(8,128)(2,1)S(1)}, u32[]{:S(2)}, u32[]{:S(2)}) collective-permute-start(bf16[1344,512]{1,0:T(8,128)(2,1)S(1)} %collective-permute-done.3.g0.u0.w0), channel_id=1, source_target_pairs={{0,8},{4,12},{8,0},{12,4},{1,9},{5,13},{9,1},{13,5},{2,10},{6,14},... | collective-permute-start | bytes 4128776 | tf_op jit(solution)/shard_map/ppermute | solution.py:541
  76.5 67.2 %all-gather.15.cloned.1.call-start = ((), (), s32[]{:S(2)}) async-start(), calls=%async_computation.8 | async-start | bytes 1351680 | tf_op jit(solution)/shard_map/all_gather | solution.py:684
  100.8 29.1 %collective-permute-start.13 = (bf16[1152,384]{1,0:T(8,128)(2,1)}, bf16[1152,384]{1,0:T(8,128)(2,1)}, u32[]{:S(2)}, u32[]{:S(2)}) collective-permute-start(bf16[1152,384]{1,0:T(8,128)(2,1)} %collective-permute-done.5.d0), channel_id=1, source_target_pairs={{0,8},{4,12},{8,0},{12,4},{1,9},{5,13},{9,1},{13,5},{2,10},{6,14},... | collective-permute-start | bytes 2654216 | tf_op jit(solution)/shard_map/ppermute | solution.py:541
  143.7 47.6 %all-to-all-start = ((bf16[4,256,640]{2,1,0:T(8,128)(2,1)}), bf16[4,256,640]{2,1,0:T(8,128)(2,1)S(1)}, u32[]{:S(2)}, u32[]{:S(2)}) async-start(bf16[4,256,640]{2,1,0:T(8,128)(2,1)} %get-tuple-element.180), calls=%async_computation | async-start | bytes 2621440 | tf_op jit(solution)/shard_map/all_to_all | solution.py:735
  148.7 80.5 %reduce-scatter.3.cloned.1.call-start = ((), (), s32[]{:S(2)}) async-start(), calls=%async_computation.4 | async-start | bytes 2088960 | tf_op jit(solution)/shard_map/reduce_scatter | solution.py:768
  148.7 42.5 %collective-permute-start.16 = (bf16[4,176,768]{2,1,0:T(8,128)(2,1)S(1)}, bf16[4,176,768]{2,1,0:T(8,128)(2,1)}, u32[]{:S(2)}, u32[]{:S(2)}) collective-permute-start(bf16[4,176,768]{2,1,0:T(8,128)(2,1)S(1)} %bitcast.190), channel_id=1, source_target_pairs={{0,8},{4,12},{8,0},{12,4},{1,9},{5,13},{9,1},{13,5},{2,10},{6,14},... | collective-permute-start | bytes 3244040 | tf_op jit(solution)/shard_map/ppermute | solution.py:541
  149.6 41.6 %collective-permute-start.17 = (bf16[4,176,768]{2,1,0:T(8,128)(2,1)S(1)}, bf16[4,176,768]{2,1,0:T(8,128)(2,1)}, u32[]{:S(2)}, u32[]{:S(2)}) collective-permute-start(bf16[4,176,768]{2,1,0:T(8,128)(2,1)S(1)} %bitcast.191), channel_id=1, source_target_pairs={{0,4},{4,0},{8,12},{12,8},{1,5},{5,1},{9,13},{13,9},{2,6},{6,2},{1... | collective-permute-start | bytes 3244040 | tf_op jit(solution)/shard_map/ppermute | solution.py:541
  191.8 91.0 %reduce-scatter.5.cloned.1.call-start = ((), (), s32[]{:S(2)}) async-start(), calls=%async_computation.5 | async-start | bytes 1966080 | tf_op jit(solution)/shard_map/reduce_scatter | solution.py:851
  216.0 35.8 %collective-permute-start.23 = (bf16[2,2,288,512]{3,2,1,0:T(8,128)(2,1)}, bf16[2,2,288,512]{3,2,1,0:T(8,128)(2,1)}, u32[]{:S(2)}, u32[]{:S(2)}) collective-permute-start(bf16[2,2,288,512]{3,2,1,0:T(8,128)(2,1)} %fusion.4), channel_id=1, source_target_pairs={{0,16},{16,0},{1,17},{17,1},{2,18},{18,2},{3,19},{19,3},{4,20},{20... | collective-permute-start | bytes 3538952 | tf_op jit(solution)/shard_map/ppermute | solution.py:535
  217.5 34.3 %collective-permute-start.24 = (bf16[2,2,288,512]{3,2,1,0:T(8,128)(2,1)}, bf16[2,2,288,512]{3,2,1,0:T(8,128)(2,1)}, u32[]{:S(2)}, u32[]{:S(2)}) collective-permute-start(bf16[2,2,288,512]{3,2,1,0:T(8,128)(2,1)} %fusion.3), channel_id=1, source_target_pairs={{0,8},{4,12},{8,0},{12,4},{1,9},{5,13},{9,1},{13,5},{2,10},{6,14},... | collective-permute-start | bytes 3538952 | tf_op jit(solution)/shard_map/ppermute | solution.py:541
  229.3 136.7 %all-gather.19.cloned.1.call-start = ((), (), s32[]{:S(2)}) async-start(), calls=%async_computation.10 | async-start | bytes 1966080 | tf_op jit(solution)/shard_map/all_gather | solution.py:953
  261.8 25.9 %collective-permute-start.31 = (bf16[4,176,768]{2,1,0:T(8,128)(2,1)}, bf16[4,176,768]{2,1,0:T(8,128)(2,1)}, u32[]{:S(2)}, u32[]{:S(2)}) collective-permute-start(bf16[4,176,768]{2,1,0:T(8,128)(2,1)} %collective-permute-done.16.w2), channel_id=1, source_target_pairs={{0,4},{4,0},{8,12},{12,8},{1,5},{5,1},{9,13},{13,9},{2,6},{6,2},{1... | collective-permute-start | bytes 3244040 | tf_op jit(solution)/shard_map/ppermute | solution.py:541
  263.7 60.8 %collective-permute-start.30 = (bf16[2,4,288,512]{3,2,1,0:T(8,128)(2,1)S(1)}, bf16[2,4,288,512]{3,2,1,0:T(8,128)(2,1)}, u32[]{:S(2)}, u32[]{:S(2)}) collective-permute-start(bf16[2,4,288,512]{3,2,1,0:T(8,128)(2,1)S(1)} %fusion), channel_id=1, source_target_pairs={{0,16},{16,0},{1,17},{17,1},{2,18},{18,2},{3,19},{19,3},{4,20},{20... | collective-permute-start | bytes 7077896 | tf_op jit(solution)/shard_map/ppermute | solution.py:535
  265.2 30.0 %collective-permute-start.32 = (bf16[2,288,512]{2,1,0:T(8,128)(2,1)}, bf16[2,288,512]{2,1,0:T(8,128)(2,1)}, u32[]{:S(2)}, u32[]{:S(2)}) collective-permute-start(bf16[2,288,512]{2,1,0:T(8,128)(2,1)} %get-tuple-element.316), channel_id=1, source_target_pairs={{0,8},{4,12},{8,0},{12,4},{1,9},{5,13},{9,1},{13,5},{2,10},{6,14},... | collective-permute-start | bytes 1769480 | tf_op jit(solution)/shard_map/ppermute | solution.py:541
  294.9 77.4 %all-gather.17.cloned.1.call-start = ((), (), s32[]{:S(2)}) async-start(), calls=%async_computation.9 | async-start | bytes 1966080 | tf_op jit(solution)/shard_map/all_gather | solution.py:927
  302.4 30.1 %collective-permute-start.36 = (bf16[2,288,512]{2,1,0:T(8,128)(2,1)}, bf16[2,288,512]{2,1,0:T(8,128)(2,1)}, u32[]{:S(2)}, u32[]{:S(2)}) collective-permute-start(bf16[2,288,512]{2,1,0:T(8,128)(2,1)} %get-tuple-element.315), channel_id=1, source_target_pairs={{0,16},{16,0},{1,17},{17,1},{2,18},{18,2},{3,19},{19,3},{4,20},{20... | collective-permute-start | bytes 1769480 | tf_op jit(solution)/shard_map/ppermute | solution.py:535
  303.8 26.0 %collective-permute-start.29 = (bf16[2,4,96,384]{3,2,1,0:T(8,128)(2,1)}, bf16[2,4,96,384]{3,2,1,0:T(8,128)(2,1)}, u32[]{:S(2)}, u32[]{:S(2)}) collective-permute-start(bf16[2,4,96,384]{3,2,1,0:T(8,128)(2,1)} %fusion.14), channel_id=1, source_target_pairs={{0,8},{4,12},{8,0},{12,4},{1,9},{5,13},{9,1},{13,5},{2,10},{6,14},... | collective-permute-start | bytes 1769480 | tf_op jit(solution)/shard_map/ppermute | solution.py:541
  319.2 35.4 %collective-permute-start.40 = (bf16[1,288,512]{2,1,0:T(8,128)(2,1)}, bf16[1,288,512]{2,1,0:T(8,128)(2,1)}, u32[]{:S(2)}, u32[]{:S(2)}) collective-permute-start(bf16[1,288,512]{2,1,0:T(8,128)(2,1)} %fusion.19), channel_id=1, source_target_pairs={{0,16},{16,0},{1,17},{17,1},{2,18},{18,2},{3,19},{19,3},{4,20},{20... | collective-permute-start | bytes 884744 | tf_op jit(solution)/shard_map/ppermute | solution.py:535
  323.9 28.8 %collective-permute-start.35 = (bf16[2,5,96,384]{3,2,1,0:T(8,128)(2,1)}, bf16[2,5,96,384]{3,2,1,0:T(8,128)(2,1)}, u32[]{:S(2)}, u32[]{:S(2)}) collective-permute-start(bf16[2,5,96,384]{3,2,1,0:T(8,128)(2,1)} %fusion.10), channel_id=1, source_target_pairs={{0,16},{16,0},{1,17},{17,1},{2,18},{18,2},{3,19},{19,3},{4,20},{20... | collective-permute-start | bytes 2211848 | tf_op jit(solution)/shard_map/ppermute | solution.py:535
  327.0 29.7 %collective-permute-start.39 = (bf16[4,288,512]{2,1,0:T(8,128)(2,1)S(1)}, bf16[4,288,512]{2,1,0:T(8,128)(2,1)}, u32[]{:S(2)}, u32[]{:S(2)}) collective-permute-start(bf16[4,288,512]{2,1,0:T(8,128)(2,1)S(1)} %fusion.2), channel_id=1, source_target_pairs={{0,8},{4,12},{8,0},{12,4},{1,9},{5,13},{9,1},{13,5},{2,10},{6,14},... | collective-permute-start | bytes 3538952 | tf_op jit(solution)/shard_map/ppermute | solution.py:541
  331.0 28.7 %collective-permute-start.38 = (bf16[4,96,384]{2,1,0:T(8,128)(2,1)S(1)}, bf16[4,96,384]{2,1,0:T(8,128)(2,1)S(1)}, u32[]{:S(2)}, u32[]{:S(2)}) collective-permute-start(bf16[4,96,384]{2,1,0:T(8,128)(2,1)S(1)} %fusion.16), channel_id=1, source_target_pairs={{0,16},{16,0},{1,17},{17,1},{2,18},{18,2},{3,19},{19,3},{4,20},{20... | collective-permute-start | bytes 884744 | tf_op jit(solution)/shard_map/ppermute | solution.py:535
  (61 other events, 652.9 us)
Sparse Core Ops, SparseCore 0:
  34.4 30.7 all-gather.10
  76.6 37.8 all-gather.12
  116.0 27.3 all-gather.14
  191.9 37.2 reduce-scatter.2
  231.4 34.3 reduce-scatter.4
  295.0 36.0 all-gather.18
  332.7 35.9 all-gather.16

commit v7 on v6

--- a/solution.py
+++ b/solution.py
@@ -226,7 +226,7 @@
 def moe_kernel(
     scal, n2_ref, dy_ref, slots_ref, gates_ref, ys_ref, dn_in_ref, gate_own, up_own, down_own,
     w0, w1, w2, w3, r0, r1, r2, r3, d0, d1, d2, d3,
-    y_ref, dn_ref, keep_ref, send_ref, wgu_s, wd_s, sems, pick_s, ye_s, dx_s, xe_s, dy_s, de_s, gs_s, dprob_s,
+    y_ref, dn_ref, keep_ref, send_ref, wgu_s, wd_s, sems, pick_s, yd_s, xe_s, dy_s, de_s, gs_s, dprob_s,
 ):
     step = pl.program_id(0)
     seqs, rows, width = n2_ref.shape
@@ -314,7 +314,7 @@
         ye = (ye * gs_s[odd][:, 0:1]).astype(BF16)
         for s in range(seqs):
             at = slice(s * SLOTS, (s + 1) * SLOTS)
-            ye_s[s, slot_at, :] = ye[at]
+            yd_s[s, slot_at, :width] = ye[at]
             hit = slots_ref[s, pl.ds(expert, 1), :] == slot
             dprob_s[s, pl.ds(expert, 1), :] = jnp.sum(jnp.where(hit, dots[at], 0.0), 0, keepdims=True)
         back = mm_nt(de_s[odd], wd[...])
@@ -323,15 +323,16 @@
         dab = jnp.concatenate([da, db], axis=1)
         dx = mm_nt(dab, wgu[...]).astype(BF16)
         for s in range(seqs):
-            dx_s[s, slot_at, :] = dx[s * SLOTS:(s + 1) * SLOTS]
+            yd_s[s, slot_at, width:] = dx[s * SLOTS:(s + 1) * SLOTS]
         put_all_grads(scal[4], keep_ref, send_ref, xe, de_s[odd], hid, dab)
 
     @pl.when(step >= experts)
     def _():
         s = step - experts
         pick = pick_s[s]
-        y_ref[0] = (ys_ref[0].astype(F32) + mm_tn(pick, ye_s[s])).astype(BF16)
-        dn_ref[0, 0:rows, :] = (dn_in_ref[0].astype(F32) + mm_tn(pick, dx_s[s])).astype(BF16)
+        both = mm_tn(pick, yd_s[s])
+        y_ref[0] = (ys_ref[0].astype(F32) + both[:, :width]).astype(BF16)
+        dn_ref[0, 0:rows, :] = (dn_in_ref[0].astype(F32) + both[:, width:]).astype(BF16)
         tail = jnp.concatenate([dprob_s[s], jnp.zeros((dn_ref.shape[1] - rows - experts, rows), F32)], axis=0)
         tail = jnp.concatenate([tail, jnp.zeros((tail.shape[0], width - rows), F32)], axis=1)
         dn_ref[0, rows:, :] = tail.astype(BF16)
@@ -758,7 +759,7 @@
         [pltpu.VMEM((2, width, 2 * hidden), BF16), pltpu.VMEM((2, hidden, width), BF16)]
         + [pltpu.SemaphoreType.DMA((2, 6))]
         + [pltpu.VMEM((seqs, experts * SLOTS, rows), BF16)]
-        + [pltpu.VMEM((seqs, experts * SLOTS, width), BF16)] * 2
+        + [pltpu.VMEM((seqs, experts * SLOTS, 2 * width), BF16)]
         + [pltpu.VMEM((2, slot_rows, width), BF16)] * 3
         + [pltpu.VMEM((2, slot_rows, 128), F32), pltpu.VMEM((seqs, 8, rows), F32)],
     )(scal, n2, cotangent, slots, gates, ys, dn_shared, *own[:3], *wide_p, *rest_p, *down_p)

time: 400 us -> 400 us (level)
  no operation moved by 1% of the time
where the time goes in v7:
time: 400 us; the launch traced here: 398 us
  Pallas kernels  131 us (33%)
  waiting for transfers between devices  129 us (32%)
  other arithmetic  52.5 us (13%)
  starting transfers between devices  42.7 us (11%)
  local copies, waits for them, and re-layouts  28.7 us (7%)
  between operations  14.7 us (4%)
    ppermute x31, waiting for transfers between devices, over_ctx(): return lax.ppermute(value, 'ctx', [(i, i ^ bit) for i in range(ctx_size)])  71.3 us
    pallas_call x1, Pallas kernels, body(): call(moe_kernel, (experts + seqs,), [full, full, whole((seqs, 8, rows)),...  41.6 us
    ppermute x10, waiting for transfers between devices, over_x(): return lax.ppermute(value, 'fsdp', [(0, 1), (1, 0)])  41.2 us
    pallas_call x1, Pallas kernels, body(): call(attn_bwd_kernel, (tp_size,), [by_step((rows, packed))] + [kv_block]...  17.6 us
    ppermute x31, starting transfers between devices, over_ctx(): return lax.ppermute(value, 'ctx', [(i, i ^ bit) for i in range(ctx_size)])  17.3 us
    ppermute x10, starting transfers between devices, over_x(): return lax.ppermute(value, 'fsdp', [(0, 1), (1, 0)])  15.5 us
    pallas_call x1, Pallas kernels, body(): call(attn_fwd_kernel, (seqs,), [by_step((rows, head_cols))] + [by_step((r...  10.9 us
    pallas_call x1, Pallas kernels, body(): call(shared_kernel, (seqs // 2,), [by_pair(width)] * 2 + [whole((half, hi...  10.2 us
  transfers between devices with their start and end apart: 50, of which 17 were waited for; matrix products, arithmetic and copies ran while one was open for 16% of the time, Pallas kernels for 33%

profile of v7, /device:TPU:0, one launch (start us, length us, event | category | flops | bytes accessed | tf_op | source)
XLA Modules:
  0.0 397.9 jit_solution(11584511153648394817)
XLA Ops:
  8.6 4.8 %concatenate.28.own_ref = bf16[832,384]{1,0:T(8,128)(2,1)S(1)} concatenate(bf16[192,384]{1,0:T(8,128)(2,1)} %bitcast.195, bf16[8,384]{1,0:T(8,128)(2,1)} %bitcast.199, bf16[1,384]{1,0:T(2,128)(2,1)S(1)} %broadcast_in_dim.24, bf16[1,384]{1,0:T(2,128)(2,1)S(1)} %broadcast_in_dim.25, bf16[54,384]{1,0:T(8,128)(2,1)S(1)} %broadcast_in_dim.26, bf16[192,384]{1,0:T(8,128)(2,1)} %bitcast.196, ...), dimensions={0} | concatenate | bytes 1277952 | tf_op jit(solution)/shard_map/concatenate | solution.py:544
  35.0 7.5 %shard_map.280 = (bf16[4,256,768]{2,1,0:T(8,128)(2,1)}, bf16[4,256,192]{2,1,0:T(8,128)(2,1)}, bf16[4,256,384]{2,1,0:T(8,128)(2,1)}, bf16[4,256,640]{2,1,0:T(8,12...) custom-call(s32[5]{0:T(128)} %stack.29.scal, bf16[4,256,768]{2,1,0:T(8,128)(2,1)} %x_ref.5, ...), custom_call_target="tpu_custom_call" | custom-call | flops 1 | bytes 1 | tf_op jit(solution)/shard_map/pallas_call | solution.py:622
  45.7 15.1 %collective-permute-done.1.kv2 = bf16[4,256,384]{2,1,0:T(8,128)(2,1)S(1)} collective-permute-done((bf16[4,256,384]{2,1,0:T(8,128)(2,1)}, bf16[4,256,384]{2,1,0:T(8,128)(2,1)S(1)}, u32[]{:S(2)}, u32[]{:S(2)}) %collective-permute-start.1) | collective-permute-done | bytes 786464 | tf_op jit(solution)/shard_map/ppermute | solution.py:542
  65.5 10.9 %shard_map.281 = bf16[4,128,384]{2,1,0:T(8,128)(2,1)} custom-call(s32[5]{0:T(128)} %stack.29.scal, s32[4]{0:T(128)} %prefix.3, bf16[4,256,192]{2,1,0:T(8,128)(2,1)} %get-tuple-element.147.q_ref, bf16[4,256,384]{2,1,0:T(8,128)(2,1)} %get-tuple-element.139.kv0, bf16[4,256,384]{2,1,0:T(8,128)(2,1)} %copy-done.23, bf16[4,256,384]{2,1,0:T(8,128)(2,1)} %copy-done.22, ...), custom_call_target="tpu_custom_call" | custom-call | flops 1 | bytes 1 | tf_op jit(solution)/shard_map/pallas_call | solution.py:666
  78.0 20.9 %collective-permute-done.5.d0 = bf16[1152,384]{1,0:T(8,128)(2,1)} collective-permute-done((bf16[1152,384]{1,0:T(8,128)(2,1)}, bf16[1152,384]{1,0:T(8,128)(2,1)}, u32[]{:S(2)}, u32[]{:S(2)}) %collective-permute-start.5) | collective-permute-done | bytes 884768 | tf_op jit(solution)/shard_map/ppermute | solution.py:536
  101.6 10.2 %collective-permute-done.12.r2 = bf16[384,512]{1,0:T(8,128)(2,1)S(1)} collective-permute-done((bf16[384,512]{1,0:T(8,128)(2,1)}, bf16[384,512]{1,0:T(8,128)(2,1)S(1)}, u32[]{:S(2)}, u32[]{:S(2)}) %collective-permute-start.12) | collective-permute-done | bytes 393248 | tf_op jit(solution)/shard_map/ppermute | solution.py:542
  114.5 7.3 %shard_map.282 = (bf16[4,256,768]{2,1,0:T(8,128)(2,1)}, f32[256,768]{1,0:T(8,128)}, f32[4,8,256]{2,1,0:T(8,128)}, s32[4,8,256]{2,1,0:T(8,128)}) custom-call(s32[5]{0:T(128)} %stack.29.scal, bf16[4,4,128,384]{3,2,1,0:T(8,128)(2,1)} %bitcast.164, bf16[4,2,192,384]{3,2,1,0:T(8,128)(2,1)} %bitcast.166, bf16[4,256,768]{2,1,0:T(8,128)(2,1)} %x_ref.5, ...), custom_call_target="tpu_custom_call" | custom-call | flops 1 | bytes 1 | tf_op jit(solution)/shard_map/pallas_call | solution.py:686
  121.9 8.0 %collective-permute-done.13.d2 = bf16[1152,384]{1,0:T(8,128)(2,1)} collective-permute-done((bf16[1152,384]{1,0:T(8,128)(2,1)}, bf16[1152,384]{1,0:T(8,128)(2,1)}, u32[]{:S(2)}, u32[]{:S(2)}) %collective-permute-start.13) | collective-permute-done | bytes 884768 | tf_op jit(solution)/shard_map/ppermute | solution.py:542
  133.5 10.2 %shard_map.283 = (bf16[4,256,768]{2,1,0:T(8,128)(2,1)}, bf16[4,256,768]{2,1,0:T(8,128)(2,1)}, bf16[4,256,512]{2,1,0:T(8,128)(2,1)}, bf16[4,256,1024]{2,1,0:T(8,128)(2,1)}) custom-call(s32[5]{0:T(128)} %stack.29.scal, bf16[4,256,768]{2,1,0:T(8,128)(2,1)} %get-tuple-element.189.n2_ref, bf16[4,256,768]{2,1,0:T(8,128)(2,1)} %dy_ref.7, bf16[384,512]{1,0:T(8,128)(2,1)} %go_ref.1, ...), custom_call_target="tpu_custom_call" | custom-call | flops 1 | bytes 1 | tf_op jit(solution)/shard_map/pallas_call | solution.py:722
  143.7 5.0 %all-to-all-start = ((bf16[4,256,640]{2,1,0:T(8,128)(2,1)}), bf16[4,256,640]{2,1,0:T(8,128)(2,1)S(1)}, u32[]{:S(2)}, u32[]{:S(2)}) async-start(bf16[4,256,640]{2,1,0:T(8,128)(2,1)} %get-tuple-element.180), calls=%async_computation | async-start | bytes 2621440 | tf_op jit(solution)/shard_map/all_to_all | solution.py:736
  149.6 41.6 %shard_map.284 = (bf16[4,256,768]{2,1,0:T(8,128)(2,1)}, bf16[4,272,768]{2,1,0:T(8,128)(2,1)}, bf16[4,8,288,512]{3,2,1,0:T(8,128)(2,1)}, bf16[4,8,288,512]{3,2,1,0:T(8,128)(2,1)}) custom-call(s32[5]{0:T(128)} %stack.29.scal, bf16[4,256,768]{2,1,0:T(8,128)(2,1)} %get-tuple-element.189.n2_ref, bf16[4,256,768]{2,1,0:T(8,128)(2,1)} %dy_ref.7, ...), custom_call_target="tpu_custom_call" | custom-call | flops 1 | bytes 1 | tf_op jit(solution)/shard_map/pallas_call | solution.py:750
  193.5 7.6 %shard_map.285 = (bf16[4,1,288,512]{3,2,1,0:T(8,128)(2,1)}, bf16[4,1,288,512]{3,2,1,0:T(8,128)(2,1)}) custom-call(s32[5]{0:T(128)} %stack.29.scal, bf16[4,256,768]{2,1,0:T(8,128)(2,1)} %get-tuple-element.189.n2_ref, bf16[4,256,768]{2,1,0:T(8,128)(2,1)} %dy_ref.7, bf16[4,256,512]{2,1,0:T(8,128)(2,1)} %get-tuple-element.190.hid_ref, ...), custom_call_target="tpu_custom_call" | custom-call | flops 1 | bytes 1 | tf_op jit(solution)/shard_map/pallas_call | solution.py:773
  201.6 4.8 %collective-permute-done.20 = bf16[4,8,288,512]{3,2,1,0:T(8,128)(2,1)} collective-permute-done((bf16[4,8,288,512]{3,2,1,0:T(8,128)(2,1)}, bf16[4,8,288,512]{3,2,1,0:T(8,128)(2,1)}, u32[]{:S(2)}, u32[]{:S(2)}) %collective-permute-start.20) | collective-permute-done | bytes 9437216 | tf_op jit(solution)/shard_map/ppermute | solution.py:542
  221.1 8.1 %reduce-scatter.3.cloned.1.call-done.dn_ref = bf16[1,272,768]{2,1,0:T(8,128)(2,1)} async-done(((bf16[4,272,768]{2,1,0:T(8,128)(2,1)}), bf16[1,272,768]{2,1,0:T(8,128)(2,1)}) %reduce-scatter.3.cloned.1.call-update) | async-done | bytes 417808 | tf_op jit(solution)/shard_map/reduce_scatter | solution.py:769
  229.5 4.7 %shard_map.286 = (f32[256,768]{1,0:T(8,128)}, bf16[4,128,384]{2,1,0:T(8,128)(2,1)}, bf16[256,768]{1,0:T(8,128)(2,1)}, f32[16,768]{1,0:T(8,128)}) custom-call(s32[5]{0:T(128)} %stack.29.scal, bf16[1,272,768]{2,1,0:T(8,128)(2,1)} %reduce-scatter.3.cloned.1.call-done.dn_ref, f32[4,8,256]{2,1,0:T(8,128)} %get-tuple-element.166.gates_ref, ...), custom_call_target="tpu_custom_call" | custom-call | flops 1 | bytes 1 | tf_op jit(solution)/shard_map/pallas_call | solution.py:855
  234.2 17.6 %shard_map.287 = (bf16[4,256,192]{2,1,0:T(8,128)(2,1)}, bf16[4,256,384]{2,1,0:T(8,128)(2,1)}, bf16[4,256,384]{2,1,0:T(8,128)(2,1)}, bf16[4,256,384]{2,1,0:T(8,128)(2,1)}, bf16[4,256,384]{2,1,0:T(8,128)(2,1)}) custom-call(s32[5]{0:T(128)} %stack.29.scal, s32[4]{0:T(128)} %prefix.3, bf16[4,256,640]{2,1,0:T(8,128)(2,1)} %copy-done.3, ...), custom_call_target="tpu_custom_call" | custom-call | flops 1 | bytes 1 | tf_op jit(solution)/shard_map/pallas_call | solution.py:884
  256.2 5.6 %shard_map.288 = (bf16[4,4,96,384]{3,2,1,0:T(8,128)(2,1)}, bf16[4,4,96,384]{3,2,1,0:T(8,128)(2,1)}) custom-call(s32[5]{0:T(128)} %stack.29.scal, bf16[4,256,768]{2,1,0:T(8,128)(2,1)} %get-tuple-element.230.n1_ref, bf16[4,256,192]{2,1,0:T(8,128)(2,1)} %get-tuple-element.211.dq_ref, bf16[256,768]{1,0:T(8,128)(2,1)} %get-tuple-element.215.low_ref, ...), custom_call_target="tpu_custom_call" | custom-call | flops 1 | bytes 1 | tf_op jit(solution)/shard_map/pallas_call | solution.py:911
  268.3 14.5 %collective-permute-done.27.c_ref = bf16[4,256,384]{2,1,0:T(8,128)(2,1)} collective-permute-done((bf16[4,256,384]{2,1,0:T(8,128)(2,1)S(1)}, bf16[4,256,384]{2,1,0:T(8,128)(2,1)}, u32[]{:S(2)}, u32[]{:S(2)}) %collective-permute-start.27) | collective-permute-done | bytes 786464 | tf_op jit(solution)/shard_map/ppermute | solution.py:542
  282.8 5.0 %shard_map.289.dkv_ref = bf16[4,256,384]{2,1,0:T(8,128)(2,1)} custom-call(bf16[4,256,384]{2,1,0:T(8,128)(2,1)} %get-tuple-element.222.a_ref, bf16[4,256,384]{2,1,0:T(8,128)(2,1)} %collective-permute-done.26.b_ref, bf16[4,256,384]{2,1,0:T(8,128)(2,1)} %collective-permute-done.27.c_ref, f32[256,640]{1,0:T(8,128)} %get-tuple-element.136.cos_ref, ...), custom_call_target="tpu_custom_call" | custom-call | flops 1 | bytes 1 | tf_op jit(solution)/shard_map/pallas_call | solution.py:929
  287.8 7.1 %shard_map.290 = (bf16[256,768]{1,0:T(8,128)(2,1)}, f32[16,768]{1,0:T(8,128)}) custom-call(s32[5]{0:T(128)} %stack.29.scal, bf16[4,256,192]{2,1,0:T(8,128)(2,1)} %get-tuple-element.211.dq_ref, bf16[4,256,384]{2,1,0:T(8,128)(2,1)} %shard_map.289.dkv_ref, bf16[4,176,768]{2,1,0:T(8,128)(2,1)} %bitcast.189, bf16[4,176,768]{2,1,0:T(8,128)(2,1)} %collective-permute-done.17.w1, ...), custom_call_target="tpu_custom_call" | custom-call | flops 1 | bytes 1 | tf_op jit(solution)/shard_map/pallas_call | solution.py:941
  295.2 5.7 %shard_map.291 = (bf16[4,5,96,384]{3,2,1,0:T(8,128)(2,1)}, bf16[4,5,96,384]{3,2,1,0:T(8,128)(2,1)}) custom-call(s32[5]{0:T(128)} %stack.29.scal, bf16[4,256,768]{2,1,0:T(8,128)(2,1)} %get-tuple-element.230.n1_ref, bf16[4,256,384]{2,1,0:T(8,128)(2,1)} %shard_map.289.dkv_ref, f32[16,768]{1,0:T(8,128)} %get-tuple-element.233.sums_ref), custom_call_target="tpu_custom_call" | custom-call | flops 1 | bytes 1 | tf_op jit(solution)/shard_map/pallas_call | solution.py:956
  304.4 12.7 %collective-permute-done.34 = bf16[2,1,288,512]{3,2,1,0:T(8,128)(2,1)S(1)} collective-permute-done((bf16[2,1,288,512]{3,2,1,0:T(8,128)(2,1)S(1)}, bf16[2,1,288,512]{3,2,1,0:T(8,128)(2,1)S(1)}, u32[]{:S(2)}, u32[]{:S(2)}) %collective-permute-start.34) | collective-permute-done | bytes 589856 | tf_op jit(solution)/shard_map/ppermute | solution.py:542
  336.6 16.1 %collective-permute-done.35 = bf16[2,5,96,384]{3,2,1,0:T(8,128)(2,1)} collective-permute-done((bf16[2,5,96,384]{3,2,1,0:T(8,128)(2,1)}, bf16[2,5,96,384]{3,2,1,0:T(8,128)(2,1)}, u32[]{:S(2)}, u32[]{:S(2)}) %collective-permute-start.35) | collective-permute-done | bytes 737312 | tf_op jit(solution)/shard_map/ppermute | solution.py:536
  380.7 5.1 %all-to-all-done.1 = bf16[4,96,896]{2,1,0:T(8,128)(2,1)} async-done(((bf16[4,96,896]{2,1,0:T(8,128)(2,1)}), bf16[4,96,896]{2,1,0:T(8,128)(2,1)}, u32[]{:S(2)}, u32[]{:S(2)}) %all-to-all-start.1) | async-done | bytes 688160 | tf_op jit(solution)/shard_map/all_to_all | solution.py:995
  (238 shorter events, 127.2 us)
Async XLA Ops:
  7.2 58.3 %all-gather.11.cloned.1.call-start = ((), (), s32[]{:S(2)}) async-start(), calls=%async_computation.6 | async-start | bytes 1474560 | tf_op jit(solution)/shard_map/all_gather | solution.py:619
  30.9 31.6 %collective-permute-start.3 = (bf16[1344,512]{1,0:T(8,128)(2,1)}, bf16[1344,512]{1,0:T(8,128)(2,1)S(1)}, u32[]{:S(2)}, u32[]{:S(2)}) collective-permute-start(bf16[1344,512]{1,0:T(8,128)(2,1)} %pad_maximum_fusion.2), channel_id=1, source_target_pairs={{0,16},{16,0},{1,17},{17,1},{2,18},{18,2},{3,19},{19,3},{4,20},{20... | collective-permute-start | bytes 4128776 | tf_op jit(solution)/shard_map/ppermute | solution.py:536
  34.3 80.1 %all-gather.13.cloned.1.call-start = ((), (), s32[]{:S(2)}) async-start(), calls=%async_computation.7 | async-start | bytes 1966080 | tf_op jit(solution)/shard_map/all_gather | solution.py:675
  64.0 35.0 %collective-permute-start.6 = (bf16[1344,512]{1,0:T(8,128)(2,1)S(1)}, bf16[1344,512]{1,0:T(8,128)(2,1)S(1)}, u32[]{:S(2)}, u32[]{:S(2)}) collective-permute-start(bf16[1344,512]{1,0:T(8,128)(2,1)S(1)} %collective-permute-done.3.g0.u0.w0), channel_id=1, source_target_pairs={{0,8},{4,12},{8,0},{12,4},{1,9},{5,13},{9,1},{13,5},{2,10},{6,14},... | collective-permute-start | bytes 4128776 | tf_op jit(solution)/shard_map/ppermute | solution.py:542
  76.5 67.2 %all-gather.15.cloned.1.call-start = ((), (), s32[]{:S(2)}) async-start(), calls=%async_computation.8 | async-start | bytes 1351680 | tf_op jit(solution)/shard_map/all_gather | solution.py:685
  100.8 29.1 %collective-permute-start.13 = (bf16[1152,384]{1,0:T(8,128)(2,1)}, bf16[1152,384]{1,0:T(8,128)(2,1)}, u32[]{:S(2)}, u32[]{:S(2)}) collective-permute-start(bf16[1152,384]{1,0:T(8,128)(2,1)} %collective-permute-done.5.d0), channel_id=1, source_target_pairs={{0,8},{4,12},{8,0},{12,4},{1,9},{5,13},{9,1},{13,5},{2,10},{6,14},... | collective-permute-start | bytes 2654216 | tf_op jit(solution)/shard_map/ppermute | solution.py:542
  143.7 47.6 %all-to-all-start = ((bf16[4,256,640]{2,1,0:T(8,128)(2,1)}), bf16[4,256,640]{2,1,0:T(8,128)(2,1)S(1)}, u32[]{:S(2)}, u32[]{:S(2)}) async-start(bf16[4,256,640]{2,1,0:T(8,128)(2,1)} %get-tuple-element.180), calls=%async_computation | async-start | bytes 2621440 | tf_op jit(solution)/shard_map/all_to_all | solution.py:736
  148.7 80.5 %reduce-scatter.3.cloned.1.call-start = ((), (), s32[]{:S(2)}) async-start(), calls=%async_computation.4 | async-start | bytes 2088960 | tf_op jit(solution)/shard_map/reduce_scatter | solution.py:769
  148.7 42.5 %collective-permute-start.16 = (bf16[4,176,768]{2,1,0:T(8,128)(2,1)S(1)}, bf16[4,176,768]{2,1,0:T(8,128)(2,1)}, u32[]{:S(2)}, u32[]{:S(2)}) collective-permute-start(bf16[4,176,768]{2,1,0:T(8,128)(2,1)S(1)} %bitcast.190), channel_id=1, source_target_pairs={{0,8},{4,12},{8,0},{12,4},{1,9},{5,13},{9,1},{13,5},{2,10},{6,14},... | collective-permute-start | bytes 3244040 | tf_op jit(solution)/shard_map/ppermute | solution.py:542
  149.6 41.6 %collective-permute-start.17 = (bf16[4,176,768]{2,1,0:T(8,128)(2,1)S(1)}, bf16[4,176,768]{2,1,0:T(8,128)(2,1)}, u32[]{:S(2)}, u32[]{:S(2)}) collective-permute-start(bf16[4,176,768]{2,1,0:T(8,128)(2,1)S(1)} %bitcast.191), channel_id=1, source_target_pairs={{0,4},{4,0},{8,12},{12,8},{1,5},{5,1},{9,13},{13,9},{2,6},{6,2},{1... | collective-permute-start | bytes 3244040 | tf_op jit(solution)/shard_map/ppermute | solution.py:542
  191.8 91.0 %reduce-scatter.5.cloned.1.call-start = ((), (), s32[]{:S(2)}) async-start(), calls=%async_computation.5 | async-start | bytes 1966080 | tf_op jit(solution)/shard_map/reduce_scatter | solution.py:852
  216.0 35.8 %collective-permute-start.23 = (bf16[2,2,288,512]{3,2,1,0:T(8,128)(2,1)}, bf16[2,2,288,512]{3,2,1,0:T(8,128)(2,1)}, u32[]{:S(2)}, u32[]{:S(2)}) collective-permute-start(bf16[2,2,288,512]{3,2,1,0:T(8,128)(2,1)} %fusion.4), channel_id=1, source_target_pairs={{0,16},{16,0},{1,17},{17,1},{2,18},{18,2},{3,19},{19,3},{4,20},{20... | collective-permute-start | bytes 3538952 | tf_op jit(solution)/shard_map/ppermute | solution.py:536
  217.5 34.3 %collective-permute-start.24 = (bf16[2,2,288,512]{3,2,1,0:T(8,128)(2,1)}, bf16[2,2,288,512]{3,2,1,0:T(8,128)(2,1)}, u32[]{:S(2)}, u32[]{:S(2)}) collective-permute-start(bf16[2,2,288,512]{3,2,1,0:T(8,128)(2,1)} %fusion.3), channel_id=1, source_target_pairs={{0,8},{4,12},{8,0},{12,4},{1,9},{5,13},{9,1},{13,5},{2,10},{6,14},... | collective-permute-start | bytes 3538952 | tf_op jit(solution)/shard_map/ppermute | solution.py:542
  229.3 136.7 %all-gather.19.cloned.1.call-start = ((), (), s32[]{:S(2)}) async-start(), calls=%async_computation.10 | async-start | bytes 1966080 | tf_op jit(solution)/shard_map/all_gather | solution.py:954
  261.8 25.9 %collective-permute-start.31 = (bf16[4,176,768]{2,1,0:T(8,128)(2,1)}, bf16[4,176,768]{2,1,0:T(8,128)(2,1)}, u32[]{:S(2)}, u32[]{:S(2)}) collective-permute-start(bf16[4,176,768]{2,1,0:T(8,128)(2,1)} %collective-permute-done.16.w2), channel_id=1, source_target_pairs={{0,4},{4,0},{8,12},{12,8},{1,5},{5,1},{9,13},{13,9},{2,6},{6,2},{1... | collective-permute-start | bytes 3244040 | tf_op jit(solution)/shard_map/ppermute | solution.py:542
  263.7 60.8 %collective-permute-start.30 = (bf16[2,4,288,512]{3,2,1,0:T(8,128)(2,1)S(1)}, bf16[2,4,288,512]{3,2,1,0:T(8,128)(2,1)}, u32[]{:S(2)}, u32[]{:S(2)}) collective-permute-start(bf16[2,4,288,512]{3,2,1,0:T(8,128)(2,1)S(1)} %fusion), channel_id=1, source_target_pairs={{0,16},{16,0},{1,17},{17,1},{2,18},{18,2},{3,19},{19,3},{4,20},{20... | collective-permute-start | bytes 7077896 | tf_op jit(solution)/shard_map/ppermute | solution.py:536
  265.2 30.0 %collective-permute-start.32 = (bf16[2,288,512]{2,1,0:T(8,128)(2,1)}, bf16[2,288,512]{2,1,0:T(8,128)(2,1)}, u32[]{:S(2)}, u32[]{:S(2)}) collective-permute-start(bf16[2,288,512]{2,1,0:T(8,128)(2,1)} %get-tuple-element.316), channel_id=1, source_target_pairs={{0,8},{4,12},{8,0},{12,4},{1,9},{5,13},{9,1},{13,5},{2,10},{6,14},... | collective-permute-start | bytes 1769480 | tf_op jit(solution)/shard_map/ppermute | solution.py:542
  294.9 77.4 %all-gather.17.cloned.1.call-start = ((), (), s32[]{:S(2)}) async-start(), calls=%async_computation.9 | async-start | bytes 1966080 | tf_op jit(solution)/shard_map/all_gather | solution.py:928
  302.4 30.1 %collective-permute-start.36 = (bf16[2,288,512]{2,1,0:T(8,128)(2,1)}, bf16[2,288,512]{2,1,0:T(8,128)(2,1)}, u32[]{:S(2)}, u32[]{:S(2)}) collective-permute-start(bf16[2,288,512]{2,1,0:T(8,128)(2,1)} %get-tuple-element.315), channel_id=1, source_target_pairs={{0,16},{16,0},{1,17},{17,1},{2,18},{18,2},{3,19},{19,3},{4,20},{20... | collective-permute-start | bytes 1769480 | tf_op jit(solution)/shard_map/ppermute | solution.py:536
  303.8 26.0 %collective-permute-start.29 = (bf16[2,4,96,384]{3,2,1,0:T(8,128)(2,1)}, bf16[2,4,96,384]{3,2,1,0:T(8,128)(2,1)}, u32[]{:S(2)}, u32[]{:S(2)}) collective-permute-start(bf16[2,4,96,384]{3,2,1,0:T(8,128)(2,1)} %fusion.14), channel_id=1, source_target_pairs={{0,8},{4,12},{8,0},{12,4},{1,9},{5,13},{9,1},{13,5},{2,10},{6,14},... | collective-permute-start | bytes 1769480 | tf_op jit(solution)/shard_map/ppermute | solution.py:542
  319.2 35.4 %collective-permute-start.40 = (bf16[1,288,512]{2,1,0:T(8,128)(2,1)}, bf16[1,288,512]{2,1,0:T(8,128)(2,1)}, u32[]{:S(2)}, u32[]{:S(2)}) collective-permute-start(bf16[1,288,512]{2,1,0:T(8,128)(2,1)} %fusion.19), channel_id=1, source_target_pairs={{0,16},{16,0},{1,17},{17,1},{2,18},{18,2},{3,19},{19,3},{4,20},{20... | collective-permute-start | bytes 884744 | tf_op jit(solution)/shard_map/ppermute | solution.py:536
  323.9 28.8 %collective-permute-start.35 = (bf16[2,5,96,384]{3,2,1,0:T(8,128)(2,1)}, bf16[2,5,96,384]{3,2,1,0:T(8,128)(2,1)}, u32[]{:S(2)}, u32[]{:S(2)}) collective-permute-start(bf16[2,5,96,384]{3,2,1,0:T(8,128)(2,1)} %fusion.10), channel_id=1, source_target_pairs={{0,16},{16,0},{1,17},{17,1},{2,18},{18,2},{3,19},{19,3},{4,20},{20... | collective-permute-start | bytes 2211848 | tf_op jit(solution)/shard_map/ppermute | solution.py:536
  327.0 29.7 %collective-permute-start.39 = (bf16[4,288,512]{2,1,0:T(8,128)(2,1)S(1)}, bf16[4,288,512]{2,1,0:T(8,128)(2,1)}, u32[]{:S(2)}, u32[]{:S(2)}) collective-permute-start(bf16[4,288,512]{2,1,0:T(8,128)(2,1)S(1)} %fusion.2), channel_id=1, source_target_pairs={{0,8},{4,12},{8,0},{12,4},{1,9},{5,13},{9,1},{13,5},{2,10},{6,14},... | collective-permute-start | bytes 3538952 | tf_op jit(solution)/shard_map/ppermute | solution.py:542
  331.0 28.7 %collective-permute-start.38 = (bf16[4,96,384]{2,1,0:T(8,128)(2,1)S(1)}, bf16[4,96,384]{2,1,0:T(8,128)(2,1)S(1)}, u32[]{:S(2)}, u32[]{:S(2)}) collective-permute-start(bf16[4,96,384]{2,1,0:T(8,128)(2,1)S(1)} %fusion.16), channel_id=1, source_target_pairs={{0,16},{16,0},{1,17},{17,1},{2,18},{18,2},{3,19},{19,3},{4,20},{20... | collective-permute-start | bytes 884744 | tf_op jit(solution)/shard_map/ppermute | solution.py:536
  (61 other events, 652.9 us)
Sparse Core Ops, SparseCore 0:
  34.4 30.7 all-gather.10
  76.6 37.8 all-gather.12
  116.0 27.3 all-gather.14
  191.9 37.2 reduce-scatter.2
  231.4 34.3 reduce-scatter.4
  295.0 36.0 all-gather.18
  332.7 35.9 all-gather.16
